TPU v7x, 32 devices: a whole 2x2x4 slice. The times are simulated.
32 devices in a mesh: lon: 8 (over z, x), probe: 4 (over y, core).
Axes of the slice: x: 2, y: 2, z: 4, core: 2. Of those that a mesh axis runs over, the one named last changes fastest.
Arguments:
- increments: float32 [64, 192, 8, 256], P('probe', 'lon'), may hold values from -6 to 6
- winds: float32 [2, 192, 8, 256], P(None, 'lon'), may hold values from -0.2 to 0.2
- obs_weight: float32 [192, 8, 256], P('lon'), may hold values from 0.1 to 10
Outputs:
- basis: float32 [64, 48, 512], P('probe', 'lon')
- upper: float32 [64, 64], replicated
All inputs are finite; a program needn't handle non-finite values.
Results may differ from a plain program's by a relative error of at most 0.00011.
Values sent between devices are 32-bit elements; how exact they have to be, the bound alone decides.
No kernel may reach another device: no remote copies, remote signals or barrier semaphores. Data moves between devices by JAX's collectives and lax.ppermute only.
A program may use at most 128 MiB of HBM per device.

v0:
```python
import jax
import jax.numpy as jnp
from jax import lax
from jax.sharding import PartitionSpec as P


def padded(block, sides, width):
    for axis, dim in sides:
        count = lax.axis_size(axis)
        forward = [(i, i + 1) for i in range(count - 1)]
        forward.append((count - 1, 0))
        backward = [(target, source) for source, target in forward]
        low = lax.ppermute(
            lax.slice_in_dim(block, block.shape[dim] - width, None, axis=dim), axis, forward
        )
        high = lax.ppermute(lax.slice_in_dim(block, 0, width, axis=dim), axis, backward)
        block = jnp.concatenate([low, block, high], axis=dim)
    return block


def lat_mask(field):
    rows = lax.broadcasted_iota(jnp.int32, field.shape, field.ndim - 1)
    return jnp.where(rows > 0, field, jnp.zeros_like(field))


def below(field):
    return jnp.concatenate([jnp.zeros_like(field[..., :1]), field[..., :-1]], axis=-1)


def above(field):
    return jnp.concatenate([field[..., 1:], jnp.zeros_like(field[..., :1])], axis=-1)


def forward_core(widened, east, north):
    a_pos = jnp.maximum(east, 0.0)
    b_neg = jnp.minimum(east, 0.0)
    c_pos = jnp.maximum(north[1:-1], 0.0)
    d_neg = jnp.minimum(north[1:-1], 0.0)
    flux_w = a_pos[1:] * widened[:, :-1] + b_neg[1:] * widened[:, 1:]
    inner = widened[:, 1:-1]
    flux_s = c_pos * below(inner) + d_neg * inner
    flux_n = above(flux_s)
    return inner - (flux_w[:, 1:] - flux_w[:, :-1]) - (flux_n - flux_s)


def adjoint_core(widened, east, north):
    a_pos = jnp.maximum(east, 0.0)
    b_neg = jnp.minimum(east, 0.0)[1:-1]
    c_pos = jnp.maximum(north[1:-1], 0.0)
    d_neg = jnp.minimum(north[1:-1], 0.0)
    a_east = a_pos[2:]
    c_north = above(c_pos)
    inner = widened[:, 1:-1]
    west_val = widened[:, :-2]
    east_val = widened[:, 2:]
    return (
        inner * (1.0 - a_east + b_neg - c_north + d_neg)
        - b_neg * west_val
        + a_east * east_val
        - d_neg * below(inner)
        + c_north * above(inner)
    )


def body(increments, winds, obs_weight):
    extended = padded(winds, (("lon", 1),), 2)
    wide_east = extended[0]
    wide_north = lat_mask(extended[1])
    near_east = wide_east[1:-1]
    near_north = wide_north[1:-1]

    def widen_two(field):
        return padded(field, (("lon", 1),), 2)

    state = forward_core(
        forward_core(widen_two(increments), wide_east, wide_north), near_east, near_north
    )
    state = obs_weight * state
    state = adjoint_core(
        adjoint_core(widen_two(state), wide_east, wide_north), near_east, near_north
    )
    sketch = increments + state
    probe_count, lon_count, level_count, lat_count = sketch.shape
    coarse = jnp.mean(
        sketch.reshape(probe_count, lon_count // 4, 4, level_count, lat_count // 4, 4), axis=(2, 5)
    )
    coarse = coarse.reshape(probe_count, -1)
    all_probes = probe_count * lax.axis_size("probe")
    ident = jnp.eye(all_probes, dtype=jnp.float32)
    full_panel = lax.all_gather(coarse, "probe", axis=0, tiled=True)
    local_gram = jnp.dot(
        full_panel,
        full_panel.T,
        precision=lax.Precision.HIGHEST,
        preferred_element_type=jnp.float32,
    )
    gram = lax.psum(local_gram, "lon")
    lower = jnp.linalg.cholesky(gram)
    inverse = lax.linalg.triangular_solve(lower, ident, left_side=True, lower=True)
    own_rows = lax.dynamic_slice_in_dim(
        inverse, lax.axis_index("probe") * probe_count, probe_count, 0
    )
    basis = jnp.dot(
        own_rows, full_panel, precision=lax.Precision.HIGHEST, preferred_element_type=jnp.float32
    )
    return (basis.reshape(probe_count, lon_count // 4, -1), lower.T)


def solution(mesh):
    in_specs = (P("probe", "lon", None, None), P(None, "lon", None, None), P("lon", None, None))
    out_specs = (P("probe", "lon", None), P())
    return jax.shard_map(body, mesh=mesh, in_specs=in_specs, out_specs=out_specs, check_vma=False)
```

profile of v0, /device:TPU:0, one launch (start us, length us, event | category | flops | bytes accessed | tf_op | source)
XLA Modules:
  0.0 140.8 jit_solution(5732611059656219188)
XLA Ops:
  0.6 0.8 fusion.28
  1.4 2.9 %collective-permute-start.2 = (f32[2,2,8,256]{3,2,1,0:T(8,128)S(1)}, f32[2,2,8,256]{3,2,1,0:T(8,128)S(1)}, u32[]{:S(2)}, u32[]{:S(2)}) collective-permute-start(f32[2,2,8,256]{3,2,1,0:T(8,128)S(1)} %get-tuple-element.25), channel_id=1, source_target_pairs={{0,4},{4,8},{8,12},{12,16},{16,20},{20,24},{24,28},{28,0},{1,5},{5... | collective-permute-start | bytes 98312 | tf_op jit(solution)/shard_map/ppermute | solution.py:13
  4.4 3.1 %collective-permute-start.3 = (f32[2,2,8,256]{3,2,1,0:T(8,128)S(1)}, f32[2,2,8,256]{3,2,1,0:T(8,128)S(1)}, u32[]{:S(2)}, u32[]{:S(2)}) collective-permute-start(f32[2,2,8,256]{3,2,1,0:T(8,128)S(1)} %get-tuple-element.24), channel_id=1, source_target_pairs={{4,0},{8,4},{12,8},{16,12},{20,16},{24,20},{28,24},{0,28},{5,1},{9... | collective-permute-start | bytes 98312 | tf_op jit(solution)/shard_map/ppermute | solution.py:16
  7.5 1.1 fusion.27
  8.6 4.7 %collective-permute-start.1 = (f32[16,2,8,256]{3,2,1,0:T(8,128)S(1)}, f32[16,2,8,256]{3,2,1,0:T(8,128)S(1)}, u32[]{:S(2)}, u32[]{:S(2)}) collective-permute-start(f32[16,2,8,256]{3,2,1,0:T(8,128)S(1)} %get-tuple-element.18), channel_id=1, source_target_pairs={{4,0},{8,4},{12,8},{16,12},{20,16},{24,20},{28,24},{0,28},{5,1},{9... | collective-permute-start | bytes 786440 | tf_op jit(solution)/shard_map/ppermute | solution.py:16
  13.3 1.0 constant_dynamic-update-slice_fusion.4
  14.6 0.8 slice_bitcast_fusion.5
  15.4 0.8 subtract_add_fusion.1
  16.4 0.7 subtract_add_fusion
  17.1 2.6 %collective-permute-done = f32[16,2,8,256]{3,2,1,0:T(8,128)S(1)} collective-permute-done((f32[16,2,8,256]{3,2,1,0:T(8,128)S(1)}, f32[16,2,8,256]{3,2,1,0:T(8,128)S(1)}, u32[]{:S(2)}, u32[]{:S(2)}) %collective-permute-start) | collective-permute-done | bytes 262176 | tf_op jit(solution)/shard_map/ppermute | solution.py:13
  19.8 0.2 constant_dynamic-update-slice_fusion.1
  20.0 2.0 %collective-permute-done.1 = f32[16,2,8,256]{3,2,1,0:T(8,128)S(1)} collective-permute-done((f32[16,2,8,256]{3,2,1,0:T(8,128)S(1)}, f32[16,2,8,256]{3,2,1,0:T(8,128)S(1)}, u32[]{:S(2)}, u32[]{:S(2)}) %collective-permute-start.1) | collective-permute-done | bytes 262176 | tf_op jit(solution)/shard_map/ppermute | solution.py:16
  22.0 0.3 slice.244
  22.4 1.0 multiply_add_fusion
  23.4 2.7 %slice.245 = f32[16,26,8,255]{3,2,1,0:T(8,128)} slice(f32[16,26,8,256]{3,2,1,0:T(8,128)S(1)} %multiply_add_fusion), slice={[0:16], [0:26], [0:8], [1:256]} | slice | bytes 6789120 | tf_op jit(solution)/shard_map/slice | solution.py:31
  26.0 0.4 fusion
  26.5 2.9 %fusion.6 = f32[16,26,8,256]{3,2,1,0:T(8,128)S(1)} fusion(f32[16,27,8,256]{3,2,1,0:T(8,128)S(1)} %fusion, f32[16,26,8,256]{3,2,1,0:T(8,128)S(1)} %multiply_add_fusion, f32[16,26,8,255]{3,2,1,0:T(8,128)} %slice.245, f32[16,28,8,256]{3,2,1,0:T(8,128)S(1)} %constant_dynamic-update-slice_fusion), kind=kLoop, calls=%fused_computation.11 | loop fusion | flops 3407872 | bytes 20433920 | tf_op jit(solution)/shard_map/sub | solution.py:43
  29.3 0.2 slice.255
  29.6 0.9 multiply_add_fusion.1
  30.5 2.5 %slice.256 = f32[16,24,8,255]{3,2,1,0:T(8,128)} slice(f32[16,24,8,256]{3,2,1,0:T(8,128)S(1)} %multiply_add_fusion.1), slice={[0:16], [0:24], [0:8], [1:256]} | slice | bytes 6266880 | tf_op jit(solution)/shard_map/slice | solution.py:31
  33.0 0.4 fusion.7
  33.4 0.6 copy-done.7
  34.0 2.7 %fusion.15 = f32[16,24,8,256]{3,2,1,0:T(8,128)S(1)} fusion(f32[16,25,8,256]{3,2,1,0:T(8,128)S(1)} %fusion.7, f32[16,24,8,256]{3,2,1,0:T(8,128)S(1)} %multiply_add_fusion.1, f32[16,24,8,255]{3,2,1,0:T(8,128)} %slice.256, f32[16,26,8,256]{3,2,1,0:T(8,128)S(1)} %fusion.6, f32[24,8,256]{2,1,0:T(8,128)S(1)} %copy-done.7), kind=kLoop, calls=%fused_computation.29 | loop fusion | flops 3932160 | bytes 19058688 | tf_op jit(solution)/shard_map/mul | solution.py:78
  36.7 0.5 collective-permute-start.4
  37.3 4.2 %collective-permute-start.5 = (f32[16,2,8,256]{3,2,1,0:T(8,128)S(1)}, f32[16,2,8,256]{3,2,1,0:T(8,128)S(1)}, u32[]{:S(2)}, u32[]{:S(2)}) collective-permute-start(f32[16,2,8,256]{3,2,1,0:T(8,128)S(1)} %get-tuple-element.17), channel_id=1, source_target_pairs={{4,0},{8,4},{12,8},{16,12},{20,16},{24,20},{28,24},{0,28},{5,1},{9... | collective-permute-start | bytes 786440 | tf_op jit(solution)/shard_map/ppermute | solution.py:16
  41.6 6.0 %collective-permute-done.4 = f32[16,2,8,256]{3,2,1,0:T(8,128)S(1)} collective-permute-done((f32[16,2,8,256]{3,2,1,0:T(8,128)S(1)}, f32[16,2,8,256]{3,2,1,0:T(8,128)S(1)}, u32[]{:S(2)}, u32[]{:S(2)}) %collective-permute-start.4) | collective-permute-done | bytes 262176 | tf_op jit(solution)/shard_map/ppermute | solution.py:13
  47.6 2.9 %collective-permute-done.5 = f32[16,2,8,256]{3,2,1,0:T(8,128)S(1)} collective-permute-done((f32[16,2,8,256]{3,2,1,0:T(8,128)S(1)}, f32[16,2,8,256]{3,2,1,0:T(8,128)S(1)}, u32[]{:S(2)}, u32[]{:S(2)}) %collective-permute-start.5) | collective-permute-done | bytes 262176 | tf_op jit(solution)/shard_map/ppermute | solution.py:16
  50.5 0.2 pad_maximum_fusion
  50.8 1.2 fusion.24
  52.0 2.7 %fusion.4 = f32[16,26,8,256]{3,2,1,0:T(8,128)S(1)} fusion(f32[16,28,8,256]{3,2,1,0:T(8,128)S(1)} %pad_maximum_fusion, f32[16,24,8,256]{3,2,1,0:T(8,128)S(1)} %fusion.15, f32[16,2,8,256]{3,2,1,0:T(8,128)S(1)} %collective-permute-done.4, f32[16,2,8,256]{3,2,1,0:T(8,128)S(1)} %collective-permute-done.5, f32[16,26,8,255]{3,2,1,0:T(8,128)S(1)} %get-tuple-element.13, ...), kind=kLoop, calls=%fused_computation.8 | loop fusion | flops 9371648 | bytes 18339840 | tf_op jit(solution)/shard_map/add | solution.py:57
  54.7 1.1 fusion.25
  55.8 0.7 copy-done.1
  56.6 2.3 %fusion.11 = f32[16,24,8,256]{3,2,1,0:T(8,128)S(1)} fusion(f32[16,24,8,256]{3,2,1,0:T(8,128)S(1)} %copy-done.1, f32[16,26,8,256]{3,2,1,0:T(8,128)S(1)} %fusion.4, f32[16,24,8,255]{3,2,1,0:T(8,128)S(1)} %get-tuple-element.15, f32[16,24,8,255]{3,2,1,0:T(8,128)S(1)} %get-tuple-element.14, f32[24,8,256]{2,1,0:T(8,128)S(1)} %copy-done.6, ...), kind=kLoop, calls=%fused_computation.22 | loop fusion | flops 7864320 | bytes 22978560 | tf_op jit(solution)/shard_map/add | solution.py:82
  58.9 12.1 %copy.25 = f32[16,24,8,256]{0,2,3,1:T(8,128)} copy(f32[16,24,8,256]{3,2,1,0:T(8,128)S(1)} %fusion.11) | data formatting | bytes 6291456 | tf_op jit(solution)/shard_map/add | solution.py:82
  71.0 10.1 %reduce_sum.9 = f32[16,6,8,64]{0,2,3,1:T(8,128)S(1)} reduce(f32[16,6,4,8,64,4]{0,3,5,4,2,1:T(8,128)} %bitcast.49, f32[]{:T(128)} %constant.56.clone.1), dimensions={2,5}, to_apply=%region_0.1 | reduce | flops 737280 | bytes 3342340 | tf_op jit(solution)/shard_map/reduce_sum | solution.py:84
  81.2 0.5 copy.26
  81.8 0.2 div.18
  81.9 8.6 %all_gather.3 = f32[64,3072]{1,0:T(8,128)S(1)} all-gather(f32[16,3072]{1,0:T(8,128)S(1)} %div.18), channel_id=1, replica_groups=mesh['lon'=8,'probe'=4] {'probe'}, dimensions={0}, use_global_device_ids=true | all-gather | bytes 983040 | tf_op jit(solution)/shard_map/all_gather | solution.py:90
  90.5 0.8 fusion.29
  91.3 35.2 %psum.7 = f32[64,64]{0,1:T(8,128)S(1)} all-reduce(f32[64,64]{0,1:T(8,128)S(1)} %fusion.29), channel_id=1, replica_groups=mesh['lon'=8,'probe'=4] {'lon'}, use_global_device_ids=true, to_apply=%region_1.2 | all-reduce | flops 4096 | bytes 32768 | tf_op jit(solution)/shard_map/psum | solution.py:97
  126.6 5.8 %cholesky.17 = f32[64,64]{1,0:T(8,128)S(1)} custom-call(f32[64,64]{1,0:T(8,128)S(1)} %fusion.19), custom_call_target="Cholesky" | custom-call | tf_op jit(solution)/shard_map/jit(cholesky)/cholesky | solution.py:98
  132.5 0.6 compare_reduce_fusion
  133.1 0.7 fusion.20
  133.8 4.9 %custom-call.6 = f32[1,64,64]{1,2,0:T(8,128)S(1)} custom-call(f32[1,64,64]{2,1,0:T(8,128)S(1)} %get-tuple-element.33), custom_call_target="InvertDiagBlocksLowerTriangular" | custom-call | tf_op jit(solution)/shard_map/triangular_solve | solution.py:99
  138.7 0.2 fusion.17
  138.9 0.5 fusion.21
  139.4 0.7 copy.34
  140.1 0.7 copy.30
  (37 shorter events, 0.8 us)
Async XLA Ops:
  1.4 11.9 %collective-permute-start.2 = (f32[2,2,8,256]{3,2,1,0:T(8,128)S(1)}, f32[2,2,8,256]{3,2,1,0:T(8,128)S(1)}, u32[]{:S(2)}, u32[]{:S(2)}) collective-permute-start(f32[2,2,8,256]{3,2,1,0:T(8,128)S(1)} %get-tuple-element.25), channel_id=1, source_target_pairs={{0,4},{4,8},{8,12},{12,16},{16,20},{20,24},{24,28},{28,0},{1,5},{5... | collective-permute-start | bytes 98312 | tf_op jit(solution)/shard_map/ppermute | solution.py:13
  4.4 10.0 %collective-permute-start.3 = (f32[2,2,8,256]{3,2,1,0:T(8,128)S(1)}, f32[2,2,8,256]{3,2,1,0:T(8,128)S(1)}, u32[]{:S(2)}, u32[]{:S(2)}) collective-permute-start(f32[2,2,8,256]{3,2,1,0:T(8,128)S(1)} %get-tuple-element.24), channel_id=1, source_target_pairs={{4,0},{8,4},{12,8},{16,12},{20,16},{24,20},{28,24},{0,28},{5,1},{9... | collective-permute-start | bytes 98312 | tf_op jit(solution)/shard_map/ppermute | solution.py:16
  8.5 11.2 %collective-permute-start = (f32[16,2,8,256]{3,2,1,0:T(8,128)S(1)}, f32[16,2,8,256]{3,2,1,0:T(8,128)S(1)}, u32[]{:S(2)}, u32[]{:S(2)}) collective-permute-start(f32[16,2,8,256]{3,2,1,0:T(8,128)S(1)} %get-tuple-element.19), channel_id=1, source_target_pairs={{0,4},{4,8},{8,12},{12,16},{16,20},{20,24},{24,28},{28,0},{1,5},{5... | collective-permute-start | bytes 786440 | tf_op jit(solution)/shard_map/ppermute | solution.py:13
  8.6 13.4 %collective-permute-start.1 = (f32[16,2,8,256]{3,2,1,0:T(8,128)S(1)}, f32[16,2,8,256]{3,2,1,0:T(8,128)S(1)}, u32[]{:S(2)}, u32[]{:S(2)}) collective-permute-start(f32[16,2,8,256]{3,2,1,0:T(8,128)S(1)} %get-tuple-element.18), channel_id=1, source_target_pairs={{4,0},{8,4},{12,8},{16,12},{20,16},{24,20},{28,24},{0,28},{5,1},{9... | collective-permute-start | bytes 786440 | tf_op jit(solution)/shard_map/ppermute | solution.py:16
  14.5 5.3 %copy-start = (f32[16,24,8,256]{3,2,1,0:T(8,128)S(1)}, f32[16,24,8,256]{3,2,1,0:T(8,128)}, u32[]{:S(2)}) copy-start(f32[16,24,8,256]{3,2,1,0:T(8,128)} %param.3) | copy-start | bytes 9437188
  30.5 2.6 %copy-start.3 = (f32[25,8,256]{2,1,0:T(8,128)S(1)}, f32[25,8,256]{2,1,0:T(8,128)}, u32[]{:S(2)}) copy-start(f32[25,8,256]{2,1,0:T(8,128)} %get-tuple-element.38) | copy-start | bytes 614404
  30.5 2.5 %copy-start.4 = (f32[25,8,256]{2,1,0:T(8,128)S(1)}, f32[25,8,256]{2,1,0:T(8,128)}, u32[]{:S(2)}) copy-start(f32[25,8,256]{2,1,0:T(8,128)} %get-tuple-element.39) | copy-start | bytes 614404
  33.0 0.9 copy-start.7
  36.7 10.9 %collective-permute-start.4 = (f32[16,2,8,256]{3,2,1,0:T(8,128)S(1)}, f32[16,2,8,256]{3,2,1,0:T(8,128)S(1)}, u32[]{:S(2)}, u32[]{:S(2)}) collective-permute-start(f32[16,2,8,256]{3,2,1,0:T(8,128)S(1)} %get-tuple-element.16), channel_id=1, source_target_pairs={{0,4},{4,8},{8,12},{12,16},{16,20},{20,24},{24,28},{28,0},{1,5},{5... | collective-permute-start | bytes 786440 | tf_op jit(solution)/shard_map/ppermute | solution.py:13
  37.3 13.3 %collective-permute-start.5 = (f32[16,2,8,256]{3,2,1,0:T(8,128)S(1)}, f32[16,2,8,256]{3,2,1,0:T(8,128)S(1)}, u32[]{:S(2)}, u32[]{:S(2)}) collective-permute-start(f32[16,2,8,256]{3,2,1,0:T(8,128)S(1)} %get-tuple-element.17), channel_id=1, source_target_pairs={{4,0},{8,4},{12,8},{16,12},{20,16},{24,20},{28,24},{0,28},{5,1},{9... | collective-permute-start | bytes 786440 | tf_op jit(solution)/shard_map/ppermute | solution.py:16
  50.8 1.2 copy-start.2
  54.7 1.9 %copy-start.1 = (f32[16,24,8,256]{3,2,1,0:T(8,128)S(1)}, f32[16,24,8,256]{3,2,1,0:T(8,128)}, u32[]{:S(2)}) copy-start(f32[16,24,8,256]{3,2,1,0:T(8,128)} %param.3) | copy-start | bytes 9437188
  54.7 1.9 %copy-start.5 = (f32[24,8,256]{2,1,0:T(8,128)S(1)}, f32[24,8,256]{2,1,0:T(8,128)}, u32[]{:S(2)}) copy-start(f32[24,8,256]{2,1,0:T(8,128)} %get-tuple-element.26) | copy-start | bytes 589828
  54.7 1.9 %copy-start.6 = (f32[24,8,256]{2,1,0:T(8,128)S(1)}, f32[24,8,256]{2,1,0:T(8,128)}, u32[]{:S(2)}) copy-start(f32[24,8,256]{2,1,0:T(8,128)} %get-tuple-element.31) | copy-start | bytes 589828
where the time goes:
time: 141 us
  blocking collectives  43.8 us (31%)
  other arithmetic  37.4 us (27%)
  local copies, waits for them, and re-layouts  27.9 us (20%)
  starting transfers between devices  15.6 us (11%)
  waiting for transfers between devices  13.6 us (10%)
  matrix products  1.48 us (1%)
    psum x1, blocking collectives, body(): gram = lax.psum(local_gram, 'lon')  35.2 us
    add x1, local copies, waits for them, and re-layouts, body(): sketch = increments + state  12.1 us
    ppermute x3, starting transfers between devices, padded(): lax.ppermute(lax.slice_in_dim(block, 0, width, axis=dim), axis, backward)  12 us
    reduce_sum x1, other arithmetic, body(): jnp.mean(sketch.reshape(probe_count, lon_count // 4, 4, level_count, lat_...  10.1 us
    ppermute x3, waiting for transfers between devices, padded(): lax.ppermute(lax.slice_in_dim(block, block.shape[dim] - width, None, axis...  8.66 us
    all_gather x1, blocking collectives, body(): full_panel = lax.all_gather(coarse, 'probe', axis=0, tiled=True)  8.63 us
    another operation x3, other arithmetic, body(): lower = jnp.linalg.cholesky(gram)  6.52 us
    slice x4, local copies, waits for them, and re-layouts, above(): field[..., 1:]  5.41 us
  transfers between devices with their start and end apart: 6, of which 4 were waited for; matrix products, arithmetic and copies ran while one was open for 4% of the time, Pallas kernels for 0%

commit v1 on v0

v1 whole, which is shorter than its diff:
```python
import functools

import jax
import jax.numpy as jnp
from jax import lax
from jax.experimental import pallas as pl
from jax.experimental.pallas import tpu as pltpu
from jax.sharding import PartitionSpec as P

F32 = jnp.float32
BF16 = jnp.bfloat16
HALF = 128
DIAG, EAST, WEST, SOUTH_UP, SOUTH_DOWN, NORTH_UP, NORTH_DOWN = range(7)
PLANES = 7


def halves(ref, *index):
    return [ref[index + (slice(None), slice(h * HALF, (h + 1) * HALF))] for h in (0, 1)]


def store(ref, value, *index):
    for h in (0, 1):
        ref[index + (slice(None), slice(h * HALF, (h + 1) * HALF))] = value[h]


class Lanes:
    def __init__(self):
        lane = lax.broadcasted_iota(jnp.int32, (8, HALF), 1)
        self.first = lane == 0
        self.last = lane == HALF - 1
        self.phase = lane & 3
        self.even = ((lane >> 2) & 1) == 0
        self.third = [lax.rem((lane + h * HALF) >> 2, 3) for h in (0, 1)]
        low = self.phase < 2
        self.near = [lax.rem(t + jnp.where(low, 2, 1), 3) for t in self.third]
        self.far = [lax.rem(t + jnp.where(low, 1, 2), 3) for t in self.third]

    def below(self, f):
        r0, r1 = pltpu.roll(f[0], 1, 1), pltpu.roll(f[1], 1, 1)
        return [r0, jnp.where(self.first, r0, r1)]

    def above(self, f):
        r0, r1 = pltpu.roll(f[0], HALF - 1, 1), pltpu.roll(f[1], HALF - 1, 1)
        return [jnp.where(self.last, r1, r0), r1]


def write_coefficients(coef, slot, u, u_next, v, lanes):
    v = [jnp.where(lanes.first, 0.0, v[0]), v[1]]
    south_up = [jnp.maximum(x, 0.0) for x in v]
    south_down = [jnp.maximum(-x, 0.0) for x in v]
    north = []
    for field in (south_up, south_down):
        r0, r1 = pltpu.roll(field[0], HALF - 1, 1), pltpu.roll(field[1], HALF - 1, 1)
        north.append([jnp.where(lanes.last, r1, r0), jnp.where(lanes.last, r0, r1)])
    east = [jnp.maximum(x, 0.0) for x in u]
    west = [jnp.maximum(-x, 0.0) for x in u]
    diag = [
        1.0 - jnp.maximum(u_next[h], 0.0) - west[h] - north[0][h] - south_down[h] for h in (0, 1)
    ]
    for plane, value in (
        (DIAG, diag),
        (EAST, east),
        (WEST, west),
        (SOUTH_UP, south_up),
        (SOUTH_DOWN, south_down),
        (NORTH_UP, north[0]),
        (NORTH_DOWN, north[1]),
    ):
        store(coef, value, plane, slot)


def stencil(lanes, field, r, get, forward):
    total = [None, None]

    def add(coefficient, value):
        for h in (0, 1):
            term = coefficient[h] * value[h]
            total[h] = term if total[h] is None else total[h] + term

    if r in field:
        here = field[r]
        add(get(DIAG, r), here)
        add(get(SOUTH_UP if forward else SOUTH_DOWN, r), lanes.below(here))
        add(get(NORTH_DOWN if forward else NORTH_UP, r), lanes.above(here))
    if r - 1 in field:
        add(get(EAST if forward else WEST, r), field[r - 1])
    if r + 1 in field:
        add(get(WEST if forward else EAST, r + 1), field[r + 1])
    return total


def block_weights(lanes, get, get_obs, first, last):
    state = [{}, {}]
    for r in range(max(first - 3, -1), min(last + 3, 4) + 1):
        if r == -1:
            own = get(WEST, 0)
            other = None
        elif r == 4:
            own = get(EAST, 4)
            other = None
        else:
            own = get(DIAG, r)
            if r > 0:
                own = [x + y for x, y in zip(own, get(EAST, r))]
            if r < 3:
                own = [x + y for x, y in zip(own, get(WEST, r + 1))]
            south, north = get(SOUTH_UP, r), get(NORTH_DOWN, r)
            inner_south = [jnp.where(lanes.phase == 0, 0.0, x) for x in south]
            inner_north = [jnp.where(lanes.phase == 3, 0.0, x) for x in north]
            own = [x + y + z for x, y, z in zip(own, inner_south, inner_north)]
            other = [
                jnp.where(lanes.phase == 0, x, jnp.where(lanes.phase == 3, y, 0.0))
                for x, y in zip(south, north)
            ]
        for colour in (0, 1):
            mine = lanes.even if colour == 0 else jnp.logical_not(lanes.even)
            state[colour][r] = [
                jnp.where(mine, own[h], 0.0 if other is None else other[h]) for h in (0, 1)
            ]
    wide = [{}, {}, {}]
    for r in range(max(first - 2, -2), min(last + 2, 5) + 1):
        obs = get_obs(r)
        pair = [stencil(lanes, state[colour], r, get, True) for colour in (0, 1)]
        pair = [[obs[h] * value[h] for h in (0, 1)] for value in pair]
        own = [jnp.where(lanes.even, pair[0][h], pair[1][h]) for h in (0, 1)]
        other = [jnp.where(lanes.even, pair[1][h], pair[0][h]) for h in (0, 1)]
        for colour in range(3):
            wide[colour][r] = [
                jnp.where(
                    lanes.third[h] == colour,
                    own[h],
                    jnp.where(lanes.near[h] == colour, other[h], 0.0),
                )
                for h in (0, 1)
            ]
    once = [
        {
            r: stencil(lanes, wide[colour], r, get, False)
            for r in range(max(first - 1, -3), min(last + 1, 6) + 1)
        }
        for colour in range(3)
    ]
    weights = {}
    for r in range(first, last + 1):
        twice = [stencil(lanes, once[colour], r, get, False) for colour in range(3)]

        def pick(index):
            return [
                jnp.where(
                    index[h] == 0, twice[0][h], jnp.where(index[h] == 1, twice[1][h], twice[2][h])
                )
                for h in (0, 1)
            ]

        own = pick(lanes.third)
        if 0 <= r <= 3:
            own = [x + 1.0 for x in own]
        weights[r, 0] = own
        if -3 <= r <= 6:
            weights[r, 1] = pick(lanes.near)
        if -1 <= r <= 4:
            weights[r, 2] = pick(lanes.far)
    return weights


def apply_weights(keys, read_weight, read_field, write, probes):
    count = len(probes)
    sums = {}
    for r in sorted({r for r, _ in keys}):
        fields = [read_field(probe, r) for probe in probes]
        for part in range(3):
            if (r, part) not in keys:
                continue
            weight = read_weight(r, part)
            for n in range(count):
                for h in (0, 1):
                    term = weight[h] * fields[n][h]
                    key = (n, part, h)
                    sums[key] = sums[key] + term if key in sums else term
    for n, probe in enumerate(probes):
        for part in range(3):
            for h in (0, 1):
                if (n, part, h) in sums:
                    write(probe, part, h, sums[n, part, h])
                else:
                    write(probe, part, h, jnp.zeros((8, HALF), F32))


def pooling(parity):
    row = lax.broadcasted_iota(jnp.int32, (3 * 256, HALF), 0)
    column = lax.broadcasted_iota(jnp.int32, (3 * 256, HALF), 1) - 64 * parity
    part, lat = row >> 8, row & 255
    low = (lat & 3) < 2
    shift = jnp.where(
        part == 0, 0, jnp.where(part == 1, jnp.where(low, -1, 1), jnp.where(low, 1, -1))
    )
    hit = (column >= 0) & (column < 64) & ((lat >> 2) + shift == column)
    return jnp.where(hit, 1.0 / 16.0, 0.0).astype(BF16)


def split3(x):
    high = x.astype(BF16)
    rest = x - high.astype(F32)
    middle = rest.astype(BF16)
    low = (rest - middle.astype(F32)).astype(BF16)
    return high, middle, low


def pool_into(sums, rows, count, write):
    total = None
    for parity in (0, 1):
        matrix = pooling(parity)
        pieces = [
            jnp.concatenate(
                [
                    sums[piece, pl.ds(n * count * 8 + 2 * pair + parity, count, stride=8), :]
                    for piece in range(6)
                ],
                axis=1,
            )
            for n in range(rows)
            for pair in range(4)
        ]
        for part in split3(jnp.concatenate(pieces, axis=0)):
            term = jnp.dot(part, matrix, preferred_element_type=F32)
            total = term if total is None else total + term
    for n in range(rows):
        for pair in range(4):
            start = (n * 4 + pair) * count
            write(n, pair, total[start : start + count])


GROUP = 4


def interior_kernel(winds, obs, field_hbm, out, coef, weights, sums, field, sem):
    count, lons = field.shape[0], field.shape[1]
    blocks = lons // 4 - 2
    fetch = pltpu.make_async_copy(field_hbm, field, sem)
    fetch.start()
    lanes = Lanes()

    def coefficients(lon, carry):
        write_coefficients(
            coef,
            lon,
            halves(winds, 0, lon),
            halves(winds, 0, jnp.minimum(lon + 1, lons - 1)),
            halves(winds, 1, lon),
            lanes,
        )
        return carry

    lax.fori_loop(0, lons, coefficients, 0)

    def weigh(block, carry):
        base = (block + 1) * 4

        def get(plane, r):
            return halves(coef, plane, base + r)

        result = block_weights(lanes, get, lambda r: halves(obs, base + r), -4, 7)
        for (r, part), value in result.items():
            store(weights, value, block, part, r + 4)
        return carry

    lax.fori_loop(0, blocks, weigh, 0)
    fetch.wait()
    keys = [(r, 0) for r in range(-4, 8)]
    keys += [(r, 1) for r in range(-3, 7)]
    keys += [(r, 2) for r in range(-1, 5)]
    groups = count // GROUP

    def sweep(step, carry):
        block = step // groups
        start = (step % groups) * GROUP

        def write(probe, part, h, value):
            row = pl.multiple_of((block * count + probe) * 8, 8)
            sums[2 * part + h, pl.ds(row, 8), :] = value

        apply_weights(
            keys,
            lambda r, part: halves(weights, block, part, r + 4),
            lambda probe, r: halves(field, probe, block * 4 + 4 + r),
            write,
            [start + n for n in range(GROUP)],
        )
        return carry

    lax.fori_loop(0, blocks * groups, sweep, 0)

    def put(n, pair, value):
        column = (n * 4 + pair) * HALF
        out[:, column : column + HALF] = value

    pool_into(sums, blocks, count, put)


def edge_kernel(
    winds, obs, from_low, from_high, field_hbm, out, coef, weights, sums, field, sems
):
    count, lons = field_hbm.shape[0], field_hbm.shape[1]
    fetches = [
        pltpu.make_async_copy(
            field_hbm.at[:, pl.ds(start, 8)], field.at[:, pl.ds(8 * side, 8)], sems.at[side]
        )
        for side, start in ((0, 0), (1, lons - 8))
    ]
    for fetch in fetches:
        fetch.start()
    lanes = Lanes()

    def wind(which, lon):
        if lon < 0:
            return halves(from_low, 3 * which + lon + 3)
        if lon >= lons:
            return halves(from_high, 4 * which + lon - lons)
        return halves(winds, which, lon)

    def weight_at(lon):
        if lon < 0:
            return halves(from_low, 6 + lon + 2)
        if lon >= lons:
            return halves(from_high, 8 + lon - lons)
        return halves(obs, lon)

    slots = {}
    for lon in list(range(-3, 8)) + list(range(lons - 8, lons + 4)):
        slots[lon] = len(slots)
        last = lon == lons + 3
        write_coefficients(
            coef, slots[lon], wind(0, lon), wind(0, lon if last else lon + 1), wind(1, lon), lanes
        )
    jobs = (
        (-4, 4, 7),
        (0, 0, 7),
        (lons - 4, -4, 3),
        (lons, -4, -1),
    )
    kept = []
    for n, (base, first, last) in enumerate(jobs):
        result = block_weights(
            lanes,
            lambda plane, r: halves(coef, plane, slots[base + r]),
            lambda r: weight_at(base + r),
            first,
            last,
        )
        for (r, part), value in result.items():
            store(weights, value, n, part, r + 4)
        kept.append(set(result))
    for fetch in fetches:
        fetch.wait()

    def sweep(step, carry):
        start = step * GROUP
        for n, (base, first, last) in enumerate(jobs):

            def write(probe, part, h, value):
                row = pl.multiple_of((n * count + probe) * 8, 8)
                sums[2 * part + h, pl.ds(row, 8), :] = value

            def read(probe, r):
                lon = base + r
                return halves(field, probe, lon if lon < 8 else lon - (lons - 16))

            apply_weights(
                kept[n],
                lambda r, part: halves(weights, n, part, r + 4),
                read,
                write,
                [start + k for k in range(GROUP)],
            )
        return carry

    lax.fori_loop(0, count // GROUP, sweep, 0)

    def put(n, pair, value):
        column = (n * 4 + pair) * HALF
        out[:, column : column + HALF] = value

    pool_into(sums, 4, count, put)


def factor_kernel(where, grams, panel, basis, upper, inverse):
    size = grams.shape[1]
    gram = grams[0]
    for n in range(1, grams.shape[0]):
        gram = gram + grams[n]
    row = lax.broadcasted_iota(jnp.int32, (size, size), 0)
    column = lax.broadcasted_iota(jnp.int32, (size, size), 1)
    state = jnp.concatenate([gram, jnp.where(row == column, 1.0, 0.0).astype(F32)], axis=1)
    tiles = [state[8 * t : 8 * t + 8] for t in range(size // 8)]
    sub = lax.broadcasted_iota(jnp.int32, (8, 2 * size), 0)
    scales = []
    for k in range(size):
        own, at = k // 8, k % 8
        pivot_row = jnp.broadcast_to(tiles[own][at : at + 1], (8, 2 * size))
        pivot = jnp.broadcast_to(pivot_row[:, k : k + 1], (8, 2 * size))
        scaled = pivot_row / pivot
        for t in range(own, size // 8):
            factor = jnp.broadcast_to(tiles[t][:, k : k + 1], (8, 2 * size))
            update = factor * scaled
            if t == own:
                update = jnp.where(sub > at, update, 0.0)
            tiles[t] = tiles[t] - update
        scales.append(lax.rsqrt(pivot))
    for t in range(size // 8):
        scale = scales[8 * t]
        for at in range(1, 8):
            scale = jnp.where(sub == at, scales[8 * t + at], scale)
        rows = tiles[t] * scale
        column = lax.broadcasted_iota(jnp.int32, (8, size), 1)
        here = lax.broadcasted_iota(jnp.int32, (8, size), 0) + 8 * t
        upper[8 * t : 8 * t + 8] = jnp.where(column >= here, rows[:, :size], 0.0)
        inverse[8 * t : 8 * t + 8] = rows[:, size:]
    count = basis.shape[0]
    own_rows = inverse[pl.ds(pl.multiple_of(where[0] * count, 8), count)]
    width = basis.shape[2]
    for n in range(basis.shape[1]):
        basis[:, n, :] = jnp.dot(
            own_rows,
            panel[:, n * width : (n + 1) * width],
            precision=lax.Precision.HIGHEST,
            preferred_element_type=F32,
        )


VMEM = pl.BlockSpec(memory_space=pltpu.VMEM)
SMEM = pl.BlockSpec(memory_space=pltpu.SMEM)
ANY = pl.BlockSpec(memory_space=pl.ANY)
LIMIT = 48 * 1024 * 1024


def body(increments, winds, obs_weight):
    count, lons, levels, lats = increments.shape
    blocks = lons // 4
    ring = lax.axis_size("lon")
    up = [(i, (i + 1) % ring) for i in range(ring)]
    down = [(i, (i - 1) % ring) for i in range(ring)]
    pack_up = jnp.concatenate([winds[0, -3:], winds[1, -3:], obs_weight[-2:]], axis=0)
    pack_down = jnp.concatenate([winds[0, :4], winds[1, :4], obs_weight[:2]], axis=0)
    from_low = lax.ppermute(pack_up, "lon", up)
    from_high = lax.ppermute(pack_down, "lon", down)
    inner = pl.pallas_call(
        interior_kernel,
        out_shape=jax.ShapeDtypeStruct((count, (blocks - 2) * 512), F32),
        in_specs=[VMEM, VMEM, ANY],
        out_specs=VMEM,
        scratch_shapes=[
            pltpu.VMEM((PLANES, lons, levels, lats), F32),
            pltpu.VMEM((blocks - 2, 3, 12, levels, lats), F32),
            pltpu.VMEM((6, (blocks - 2) * count * 8, HALF), F32),
            pltpu.VMEM((count, lons, levels, lats), F32),
            pltpu.SemaphoreType.DMA,
        ],
        compiler_params=pltpu.CompilerParams(vmem_limit_bytes=LIMIT),
        name="interior",
    )(winds, obs_weight, increments)
    edges = pl.pallas_call(
        edge_kernel,
        out_shape=jax.ShapeDtypeStruct((count, 4 * 512), F32),
        in_specs=[VMEM, VMEM, VMEM, VMEM, ANY],
        out_specs=VMEM,
        scratch_shapes=[
            pltpu.VMEM((PLANES, 23, levels, lats), F32),
            pltpu.VMEM((4, 3, 12, levels, lats), F32),
            pltpu.VMEM((6, 4 * count * 8, HALF), F32),
            pltpu.VMEM((count, 16, levels, lats), F32),
            pltpu.SemaphoreType.DMA((2,)),
        ],
        compiler_params=pltpu.CompilerParams(vmem_limit_bytes=LIMIT),
        name="edges",
    )(winds, obs_weight, from_low, from_high, increments)
    to_low, own_low, own_high, to_high = jnp.split(edges, 4, axis=1)
    own_low = own_low + lax.ppermute(to_high, "lon", up)
    own_high = own_high + lax.ppermute(to_low, "lon", down)
    coarse = jnp.concatenate([own_low, inner, own_high], axis=1)
    panel = lax.all_gather(coarse, "probe", axis=0, tiled=True)
    gram = jnp.dot(
        panel, panel.T, precision=lax.Precision.HIGHEST, preferred_element_type=F32
    )
    grams = lax.all_to_all(
        jnp.broadcast_to(gram[None], (ring,) + gram.shape), "lon", 0, 0, tiled=True
    )
    probes = panel.shape[0]
    basis, upper = pl.pallas_call(
        factor_kernel,
        out_shape=(
            jax.ShapeDtypeStruct((count, blocks, 512), F32),
            jax.ShapeDtypeStruct((probes, probes), F32),
        ),
        in_specs=[SMEM, VMEM, VMEM],
        out_specs=(VMEM, VMEM),
        scratch_shapes=[pltpu.VMEM((probes, probes), F32)],
        compiler_params=pltpu.CompilerParams(vmem_limit_bytes=LIMIT),
        name="factor",
    )(lax.axis_index("probe").reshape(1).astype(jnp.int32), grams, panel)
    return basis, upper


def solution(mesh):
    in_specs = (P("probe", "lon", None, None), P(None, "lon", None, None), P("lon", None, None))
    out_specs = (P("probe", "lon", None), P())
    return jax.shard_map(body, mesh=mesh, in_specs=in_specs, out_specs=out_specs, check_vma=False)
```

time: 141 us -> 68.9 us (0.49)
  other arithmetic: 37.4 us -> 1 us
  blocking collectives: 43.8 us -> 8.63 us
  local copies, waits for them, and re-layouts: 27.9 us -> 8.36 us
  Pallas kernels: 0 us -> 18 us
  waiting for transfers between devices: 13.6 us -> 21.3 us
  starting transfers between devices: 15.6 us -> 9.58 us
    psum x1 -> x0, blocking collectives: 35.2 us -> none  [body(): gram = lax.psum(local_gram, 'lon')]
    pallas_call x0 -> x3, Pallas kernels: none -> 18 us  [the longest x1 9.17 us: body(): pl.pallas_call(factor_kernel, out_shape=(jax.ShapeDtypeStruct((count, blo...]
    add x1 -> x0, local copies, waits for them, and re-layouts: 12.1 us -> none  [body(): sketch = increments + state]
    another operation x4 -> x0, other arithmetic: 11.4 us -> none  [the longest x3 6.52 us: body(): lower = jnp.linalg.cholesky(gram)]
    slice x15 -> x1, local copies, waits for them, and re-layouts: 11 us -> 0.74 us  [body(): obs_weight[:2]]
    reduce_sum x1 -> x0, other arithmetic: 10.1 us -> none  [body(): jnp.mean(sketch.reshape(probe_count, lon_count // 4, 4, level_count, lat_...]
    ppermute x6 -> x4, starting transfers between devices: 15.6 us -> 6.2 us  [the longest x1 6.03 us: body(): from_high = lax.ppermute(pack_down, 'lon', down)]
    add x8 -> x2, other arithmetic: 9.22 us -> 0.02 us  [the longest x1 0.01 us: body(): own_low = own_low + lax.ppermute(to_high, 'lon', up)]
  transfers between devices with their start and end apart: 6 -> 5, of which waited for: 4 -> 3; matrix products, arithmetic and copies ran while one was open for 4% -> 1% of each run, Pallas kernels for 0% -> 9%
where the time goes in v1:
time: 68.9 us; the launch traced here: 68.4 us
  waiting for transfers between devices  21.3 us (31%)
  Pallas kernels  18 us (26%)
  starting transfers between devices  9.58 us (14%)
  blocking collectives  8.63 us (13%)
  local copies, waits for them, and re-layouts  8.36 us (12%)
  other arithmetic  1 us (1%)
  matrix products  0.76 us (1%)
  between operations  0.76 us (1%)
    pallas_call x1, Pallas kernels, body(): pl.pallas_call(factor_kernel, out_shape=(jax.ShapeDtypeStruct((count, blo...  9.17 us
    all_gather x1, blocking collectives, body(): panel = lax.all_gather(coarse, 'probe', axis=0, tiled=True)  8.63 us
    all_to_all x1, waiting for transfers between devices, body(): lax.all_to_all(jnp.broadcast_to(gram[None], (ring,) + gram.shape), 'lon',...  7.71 us
    ppermute x1, waiting for transfers between devices, body(): from_low = lax.ppermute(pack_up, 'lon', up)  6.95 us
    ppermute x1, waiting for transfers between devices, body(): own_low = own_low + lax.ppermute(to_high, 'lon', up)  6.6 us
    ppermute x1, starting transfers between devices, body(): from_high = lax.ppermute(pack_down, 'lon', down)  6.03 us
    pallas_call x1, Pallas kernels, body(): pl.pallas_call(interior_kernel, out_shape=jax.ShapeDtypeStruct((count, (b...  6.02 us
    unnamed x10, local copies, waits for them, and re-layouts  4.75 us
  transfers between devices with their start and end apart: 5, of which 3 were waited for; matrix products, arithmetic and copies ran while one was open for 1% of the time, Pallas kernels for 9%

profile of v1, /device:TPU:0, one launch (start us, length us, event | category | flops | bytes accessed | tf_op | source)
XLA Modules:
  0.0 68.4 jit_solution(6801816369350457181)
XLA Ops:
  0.6 0.7 %fusion = (f32[2,8,256]{2,1,0:T(8,128)S(1)}, f32[2,8,256]{2,1,0:T(8,128)S(1)}) fusion(f32[24,8,256]{2,1,0:T(8,128)} %obs.3), kind=kLoop, calls=%fused_computation.9 | loop fusion | bytes 65536 | tf_op jit(solution)/shard_map/slice | solution.py:443
  1.4 0.8 %slice_bitcast_fusion.1 = (f32[4,8,256]{2,1,0:T(8,128)S(1)}, f32[4,8,256]{2,1,0:T(8,128)S(1)}) fusion(f32[2,24,8,256]{3,2,1,0:T(8,128)} %winds.3), kind=kLoop, calls=%fused_computation.6 | loop fusion | bytes 131072 | tf_op jit(solution)/shard_map/squeeze | solution.py:443
  2.2 6.0 %collective-permute-start.1 = (f32[10,8,256]{2,1,0:T(8,128)S(1)}, f32[10,8,256]{2,1,0:T(8,128)S(1)}, u32[]{:S(2)}, u32[]{:S(2)}) collective-permute-start(f32[10,8,256]{2,1,0:T(8,128)S(1)} %pad_maximum_fusion.1), channel_id=1, source_target_pairs={{0,28},{4,0},{8,4},{12,8},{16,12},{20,16},{24,20},{28,24},{1,29},{... | collective-permute-start | bytes 245768 | tf_op jit(solution)/shard_map/ppermute | solution.py:445
  8.2 0.8 %slice_bitcast_fusion.3 = (f32[3,8,256]{2,1,0:T(8,128)S(1)}, f32[3,8,256]{2,1,0:T(8,128)S(1)}) fusion(f32[2,24,8,256]{3,2,1,0:T(8,128)} %winds.3), kind=kLoop, calls=%fused_computation.8 | loop fusion | bytes 98304 | tf_op jit(solution)/shard_map/squeeze | solution.py:442
  9.0 0.1 collective-permute-start
  9.0 6.9 %collective-permute-done.from_low = f32[8,8,256]{2,1,0:T(8,128)S(1)} collective-permute-done((f32[8,8,256]{2,1,0:T(8,128)S(1)}, f32[8,8,256]{2,1,0:T(8,128)S(1)}, u32[]{:S(2)}, u32[]{:S(2)}) %collective-permute-start) | collective-permute-done | bytes 65568 | tf_op jit(solution)/shard_map/ppermute | solution.py:444
  16.0 0.0 collective-permute-done.1.from_high
  16.0 0.0 copy-start
  16.0 1.9 %copy-done = f32[16,24,8,256]{3,2,1,0:T(8,128)S(1)} copy-done((f32[16,24,8,256]{3,2,1,0:T(8,128)S(1)}, f32[16,24,8,256]{3,2,1,0:T(8,128)}, u32[]{:S(2)}) %copy-start) | copy-done | bytes 3145752
  17.9 0.0 copy-start.2
  17.9 1.0 %copy-done.2 = f32[2,24,8,256]{3,2,1,0:T(8,128)S(1)} copy-done((f32[2,24,8,256]{3,2,1,0:T(8,128)S(1)}, f32[2,24,8,256]{3,2,1,0:T(8,128)}, u32[]{:S(2)}) %copy-start.2) | copy-done | bytes 393240
  18.9 0.0 copy-start.3
  18.9 0.9 %copy-done.3 = f32[24,8,256]{2,1,0:T(8,128)S(1)} copy-done((f32[24,8,256]{2,1,0:T(8,128)S(1)}, f32[24,8,256]{2,1,0:T(8,128)}, u32[]{:S(2)}) %copy-start.3) | copy-done | bytes 196632
  19.8 0.0 copy-start.1
  19.8 2.8 %edges.1 = f32[16,2048]{1,0:T(8,128)S(1)} custom-call(f32[2,24,8,256]{3,2,1,0:T(8,128)S(1)} %copy-done.2, f32[24,8,256]{2,1,0:T(8,128)S(1)} %copy-done.3, f32[8,8,256]{2,1,0:T(8,128)S(1)} %collective-permute-done.from_low, f32[10,8,256]{2,1,0:T(8,128)S(1)} %collective-permute-done.1.from_high, f32[16,24,8,256]{3,2,1,0:T(8,128)S(1)} %copy-done), custom_call_target="tpu_custom_call" | custom-call | tf_op jit(solution)/shard_map/edges/pallas_call | solution.py:461
  22.6 0.1 collective-permute-start.2
  22.7 6.6 %collective-permute-done.2 = f32[16,512]{1,0:T(8,128)S(1)} collective-permute-done((f32[16,512]{1,0:T(8,128)S(1)}, f32[16,512]{1,0:T(8,128)S(1)}, u32[]{:S(2)}, u32[]{:S(2)}) %collective-permute-start.2) | collective-permute-done | bytes 32800 | tf_op jit(solution)/shard_map/ppermute | solution.py:477
  29.3 0.1 collective-permute-start.3
  29.4 0.0 copy-done.1
  29.4 6.0 %interior.1 = f32[16,2048]{1,0:T(8,128)S(1)} custom-call(f32[2,24,8,256]{3,2,1,0:T(8,128)S(1)} %copy-done.2, f32[24,8,256]{2,1,0:T(8,128)S(1)} %copy-done.3, f32[16,24,8,256]{3,2,1,0:T(8,128)S(1)} %copy-done.1), custom_call_target="tpu_custom_call" | custom-call | tf_op jit(solution)/shard_map/interior/pallas_call | solution.py:446
  35.4 0.0 collective-permute-done.3
  35.5 8.6 %all_gather.3.panel = f32[64,3072]{1,0:T(8,128)S(1)} all-gather(f32[16,3072]{1,0:T(8,128)S(1)} %pad_maximum_fusion), channel_id=1, replica_groups=mesh['lon'=8,'probe'=4] {'probe'}, dimensions={0}, use_global_device_ids=true | all-gather | bytes 983040 | tf_op jit(solution)/shard_map/all_gather | solution.py:480
  44.1 0.8 %fusion.1 = f32[64,64]{1,0:T(8,128)S(1)} fusion(f32[64,3072]{1,0:T(8,128)S(1)} %all_gather.3.panel), kind=kOutput, calls=%fused_computation.10 | convolution fusion | flops 150994944 | bytes 802816 | tf_op jit(solution)/shard_map/dot_general | solution.py:481
  44.9 0.8 %reshape.9 = f32[8,1,4096]{2,1,0:T(1,128)} reshape(f32[8,64,64]{2,1,0:T(8,128)S(1)} %broadcast_in_dim.2) | data formatting | bytes 262144
  45.7 3.4 %all-to-all-start = ((f32[8,1,4096]{2,1,0:T(1,128)}), f32[8,1,4096]{2,1,0:T(1,128)S(1)}, u32[]{:S(2)}, u32[]{:S(2)}) async-start(f32[8,1,4096]{2,1,0:T(1,128)} %reshape.9), calls=%async_computation | async-start | bytes 262144 | tf_op jit(solution)/shard_map/all_to_all | solution.py:484
  49.1 7.7 %all-to-all-done = f32[8,1,4096]{2,1,0:T(1,128)S(1)} async-done(((f32[8,1,4096]{2,1,0:T(1,128)}), f32[8,1,4096]{2,1,0:T(1,128)S(1)}, u32[]{:S(2)}, u32[]{:S(2)}) %all-to-all-start) | async-done | bytes 131104 | tf_op jit(solution)/shard_map/all_to_all | solution.py:484
  56.8 0.5 broadcast.1
  57.3 1.0 %reduce = f32[8,4096]{1,0:T(8,128)S(1)} reduce(f32[8,1,4096]{2,1,0:T(1,128)S(1)} %all-to-all-done, f32[]{:T(128)} %broadcast.1), dimensions={1}, to_apply=%all_to_all.3.reduce_sub_computation | reduce | bytes 262148 | tf_op jit(solution)/shard_map/all_to_all | solution.py:484
  58.3 0.1 reshape.10.grams
  58.4 9.2 %factor.1 = (f32[16,6,512]{2,1,0:T(8,128)S(1)}, f32[64,64]{1,0:T(8,128)}) custom-call(s32[1]{0:T(128)} %bitcast.where, f32[8,64,64]{2,1,0:T(8,128)S(1)} %reshape.10.grams, f32[64,3072]{1,0:T(8,128)S(1)} %all_gather.3.panel), custom_call_target="tpu_custom_call" | custom-call | tf_op jit(solution)/shard_map/factor/pallas_call | solution.py:488
  67.6 0.8 %copy.5 = f32[16,6,512]{2,0,1:T(8,128)} copy(f32[16,6,512]{2,1,0:T(8,128)S(1)} %get-tuple-element.2) | data formatting | bytes 393216 | tf_op jit(solution)/shard_map/factor/pallas_call | solution.py:488
  (7 shorter events, 0.1 us)
Async XLA Ops:
  2.2 13.8 %collective-permute-start.1 = (f32[10,8,256]{2,1,0:T(8,128)S(1)}, f32[10,8,256]{2,1,0:T(8,128)S(1)}, u32[]{:S(2)}, u32[]{:S(2)}) collective-permute-start(f32[10,8,256]{2,1,0:T(8,128)S(1)} %pad_maximum_fusion.1), channel_id=1, source_target_pairs={{0,28},{4,0},{8,4},{12,8},{16,12},{20,16},{24,20},{28,24},{1,29},{... | collective-permute-start | bytes 245768 | tf_op jit(solution)/shard_map/ppermute | solution.py:445
  9.0 7.0 %collective-permute-start = (f32[8,8,256]{2,1,0:T(8,128)S(1)}, f32[8,8,256]{2,1,0:T(8,128)S(1)}, u32[]{:S(2)}, u32[]{:S(2)}) collective-permute-start(f32[8,8,256]{2,1,0:T(8,128)S(1)} %pad_maximum_fusion.2), channel_id=1, source_target_pairs={{0,4},{4,8},{8,12},{12,16},{16,20},{20,24},{24,28},{28,0},{1,5},{5... | collective-permute-start | bytes 196616 | tf_op jit(solution)/shard_map/ppermute | solution.py:444
  16.0 1.9 %copy-start = (f32[16,24,8,256]{3,2,1,0:T(8,128)S(1)}, f32[16,24,8,256]{3,2,1,0:T(8,128)}, u32[]{:S(2)}) copy-start(f32[16,24,8,256]{3,2,1,0:T(8,128)} %field_hbm.3) | copy-start | bytes 9437188
  17.9 1.0 %copy-start.2 = (f32[2,24,8,256]{3,2,1,0:T(8,128)S(1)}, f32[2,24,8,256]{3,2,1,0:T(8,128)}, u32[]{:S(2)}) copy-start(f32[2,24,8,256]{3,2,1,0:T(8,128)} %winds.3) | copy-start | bytes 1179652
  18.9 0.9 %copy-start.3 = (f32[24,8,256]{2,1,0:T(8,128)S(1)}, f32[24,8,256]{2,1,0:T(8,128)}, u32[]{:S(2)}) copy-start(f32[24,8,256]{2,1,0:T(8,128)} %obs.3) | copy-start | bytes 589828
  19.8 9.6 %copy-start.1 = (f32[16,24,8,256]{3,2,1,0:T(8,128)S(1)}, f32[16,24,8,256]{3,2,1,0:T(8,128)}, u32[]{:S(2)}) copy-start(f32[16,24,8,256]{3,2,1,0:T(8,128)} %field_hbm.3) | copy-start | bytes 9437188
  22.6 6.7 %collective-permute-start.2 = (f32[16,512]{1,0:T(8,128)S(1)}, f32[16,512]{1,0:T(8,128)S(1)}, u32[]{:S(2)}, u32[]{:S(2)}) collective-permute-start(f32[16,512]{1,0:T(8,128)S(1)} %split.17), channel_id=1, source_target_pairs={{0,4},{4,8},{8,12},{12,16},{16,20},{20,24},{24,28},{28,0},{1,5},{5... | collective-permute-start | bytes 98312 | tf_op jit(solution)/shard_map/ppermute | solution.py:477
  29.3 6.1 %collective-permute-start.3 = (f32[16,512]{1,0:T(8,128)S(1)}, f32[16,512]{1,0:T(8,128)S(1)}, u32[]{:S(2)}, u32[]{:S(2)}) collective-permute-start(f32[16,512]{1,0:T(8,128)S(1)} %get-tuple-element.11), channel_id=1, source_target_pairs={{0,28},{4,0},{8,4},{12,8},{16,12},{20,16},{24,20},{28,24},{1,29},{... | collective-permute-start | bytes 98312 | tf_op jit(solution)/shard_map/ppermute | solution.py:478
  45.7 11.1 %all-to-all-start = ((f32[8,1,4096]{2,1,0:T(1,128)}), f32[8,1,4096]{2,1,0:T(1,128)S(1)}, u32[]{:S(2)}, u32[]{:S(2)}) async-start(f32[8,1,4096]{2,1,0:T(1,128)} %reshape.9), calls=%async_computation | async-start | bytes 262144 | tf_op jit(solution)/shard_map/all_to_all | solution.py:484

commit v2 on v1

--- a/solution.py
+++ b/solution.py
@@ -233,12 +233,42 @@
 GROUP = 4
 
 
-def interior_kernel(winds, obs, field_hbm, out, coef, weights, sums, field, sem):
+def fetch_all(copies):
+    for copy in copies:
+        copy.start()
+    return copies
+
+
+def pack_kernel(winds, obs, low, high, sems):
+    lons = obs.shape[0]
+    copies = fetch_all(
+        [
+            pltpu.make_async_copy(winds.at[0, pl.ds(lons - 3, 3)], low.at[pl.ds(0, 3)], sems.at[0]),
+            pltpu.make_async_copy(winds.at[1, pl.ds(lons - 3, 3)], low.at[pl.ds(3, 3)], sems.at[1]),
+            pltpu.make_async_copy(obs.at[pl.ds(lons - 2, 2)], low.at[pl.ds(6, 2)], sems.at[2]),
+            pltpu.make_async_copy(winds.at[0, pl.ds(0, 4)], high.at[pl.ds(0, 4)], sems.at[3]),
+            pltpu.make_async_copy(winds.at[1, pl.ds(0, 4)], high.at[pl.ds(4, 4)], sems.at[4]),
+            pltpu.make_async_copy(obs.at[pl.ds(0, 2)], high.at[pl.ds(8, 2)], sems.at[5]),
+        ]
+    )
+    for copy in copies:
+        copy.wait()
+
+
+def interior_kernel(
+    winds_hbm, obs_hbm, field_hbm, out, winds, obs, coef, weights, sums, field, sems
+):
     count, lons = field.shape[0], field.shape[1]
     blocks = lons // 4 - 2
-    fetch = pltpu.make_async_copy(field_hbm, field, sem)
-    fetch.start()
+    wind_copy, obs_copy, field_copy = fetch_all(
+        [
+            pltpu.make_async_copy(winds_hbm, winds, sems.at[0]),
+            pltpu.make_async_copy(obs_hbm, obs, sems.at[1]),
+            pltpu.make_async_copy(field_hbm, field, sems.at[2]),
+        ]
+    )
     lanes = Lanes()
+    wind_copy.wait()
 
     def coefficients(lon, carry):
         write_coefficients(
@@ -252,6 +282,7 @@
         return carry
 
     lax.fori_loop(0, lons, coefficients, 0)
+    obs_copy.wait()
 
     def weigh(block, carry):
         base = (block + 1) * 4
@@ -265,7 +296,7 @@
         return carry
 
     lax.fori_loop(0, blocks, weigh, 0)
-    fetch.wait()
+    field_copy.wait()
     keys = [(r, 0) for r in range(-4, 8)]
     keys += [(r, 1) for r in range(-3, 7)]
     keys += [(r, 2) for r in range(-1, 5)]
@@ -298,37 +329,57 @@
 
 
 def edge_kernel(
-    winds, obs, from_low, from_high, field_hbm, out, coef, weights, sums, field, sems
+    winds_hbm, obs_hbm, from_low, from_high, field_hbm,
+    to_low, own_low, own_high, to_high,
+    winds, obs, coef, weights, sums, field, sems,
 ):
     count, lons = field_hbm.shape[0], field_hbm.shape[1]
-    fetches = [
-        pltpu.make_async_copy(
-            field_hbm.at[:, pl.ds(start, 8)], field.at[:, pl.ds(8 * side, 8)], sems.at[side]
-        )
-        for side, start in ((0, 0), (1, lons - 8))
-    ]
-    for fetch in fetches:
-        fetch.start()
+    sides = ((0, 0), (1, lons - 8))
+    copies = fetch_all(
+        [
+            pltpu.make_async_copy(
+                winds_hbm.at[:, pl.ds(start, 8)], winds.at[:, pl.ds(8 * side, 8)], sems.at[side]
+            )
+            for side, start in sides
+        ]
+        + [
+            pltpu.make_async_copy(
+                obs_hbm.at[pl.ds(start, 8)], obs.at[pl.ds(8 * side, 8)], sems.at[2 + side]
+            )
+            for side, start in sides
+        ]
+        + [
+            pltpu.make_async_copy(
+                field_hbm.at[:, pl.ds(start, 8)], field.at[:, pl.ds(8 * side, 8)], sems.at[4 + side]
+            )
+            for side, start in sides
+        ]
+    )
     lanes = Lanes()
+    for copy in copies[:4]:
+        copy.wait()
+
+    def near(lon):
+        return lon if lon < 8 else lon - (lons - 16)
 
     def wind(which, lon):
         if lon < 0:
             return halves(from_low, 3 * which + lon + 3)
         if lon >= lons:
             return halves(from_high, 4 * which + lon - lons)
-        return halves(winds, which, lon)
+        return halves(winds, which, near(lon))
 
     def weight_at(lon):
         if lon < 0:
             return halves(from_low, 6 + lon + 2)
         if lon >= lons:
             return halves(from_high, 8 + lon - lons)
-        return halves(obs, lon)
+        return halves(obs, near(lon))
 
     slots = {}
     for lon in list(range(-3, 8)) + list(range(lons - 8, lons + 4)):
         slots[lon] = len(slots)
-        last = lon == lons + 3
+        last = lon in (7, lons + 3)
         write_coefficients(
             coef, slots[lon], wind(0, lon), wind(0, lon if last else lon + 1), wind(1, lon), lanes
         )
@@ -350,8 +401,8 @@
         for (r, part), value in result.items():
             store(weights, value, n, part, r + 4)
         kept.append(set(result))
-    for fetch in fetches:
-        fetch.wait()
+    for copy in copies[4:]:
+        copy.wait()
 
     def sweep(step, carry):
         start = step * GROUP
@@ -361,143 +412,211 @@
                 row = pl.multiple_of((n * count + probe) * 8, 8)
                 sums[2 * part + h, pl.ds(row, 8), :] = value
 
-            def read(probe, r):
-                lon = base + r
-                return halves(field, probe, lon if lon < 8 else lon - (lons - 16))
-
             apply_weights(
                 kept[n],
                 lambda r, part: halves(weights, n, part, r + 4),
-                read,
+                lambda probe, r: halves(field, probe, near(base + r)),
                 write,
                 [start + k for k in range(GROUP)],
             )
         return carry
 
     lax.fori_loop(0, count // GROUP, sweep, 0)
+    outs = (to_low, own_low, own_high, to_high)
 
     def put(n, pair, value):
-        column = (n * 4 + pair) * HALF
-        out[:, column : column + HALF] = value
+        outs[n][:, pair * HALF : (pair + 1) * HALF] = value
 
     pool_into(sums, 4, count, put)
 
 
-def factor_kernel(where, grams, panel, basis, upper, inverse):
-    size = grams.shape[1]
-    gram = grams[0]
+def self_product(panel):
+    return lax.dot_general(
+        panel,
+        panel,
+        (((1,), (1,)), ((), ())),
+        precision=lax.Precision.HIGHEST,
+        preferred_element_type=F32,
+    )
+
+
+def inner_gram_kernel(panel, out):
+    out[...] = self_product(panel[...])
+
+
+def gram_kernel(panel, inner, out):
+    gram = self_product(panel[...]) + inner[...]
+    half = gram.shape[0] // 2
+    packed = jnp.concatenate([gram[:half], gram[half:]], axis=1)
+    for n in range(out.shape[0]):
+        out[n] = packed
+
+
+def factor_kernel(where, grams, inner, edge, basis, upper, inverse):
+    packed = grams[0]
     for n in range(1, grams.shape[0]):
-        gram = gram + grams[n]
+        packed = packed + grams[n]
+    size = 2 * packed.shape[0]
+    gram = jnp.concatenate([packed[:, :size], packed[:, size:]], axis=0)
     row = lax.broadcasted_iota(jnp.int32, (size, size), 0)
     column = lax.broadcasted_iota(jnp.int32, (size, size), 1)
     state = jnp.concatenate([gram, jnp.where(row == column, 1.0, 0.0).astype(F32)], axis=1)
     tiles = [state[8 * t : 8 * t + 8] for t in range(size // 8)]
-    sub = lax.broadcasted_iota(jnp.int32, (8, 2 * size), 0)
+    full = (8, 2 * size)
+    sub = lax.broadcasted_iota(jnp.int32, full, 0)
     scales = []
-    for k in range(size):
-        own, at = k // 8, k % 8
-        pivot_row = jnp.broadcast_to(tiles[own][at : at + 1], (8, 2 * size))
-        pivot = jnp.broadcast_to(pivot_row[:, k : k + 1], (8, 2 * size))
-        scaled = pivot_row / pivot
-        for t in range(own, size // 8):
-            factor = jnp.broadcast_to(tiles[t][:, k : k + 1], (8, 2 * size))
-            update = factor * scaled
-            if t == own:
-                update = jnp.where(sub > at, update, 0.0)
+    for own in range(size // 8):
+        spread = {
+            (t, j): jnp.broadcast_to(tiles[t][:, 8 * own + j : 8 * own + j + 1], full)
+            for t in range(own, size // 8)
+            for j in range(8)
+        }
+        pivots = {
+            (i, j): jnp.broadcast_to(spread[own, j][i : i + 1], full)
+            for i in range(8)
+            for j in range(i + 1)
+        }
+        rows = [jnp.broadcast_to(tiles[own][j : j + 1], full) for j in range(8)]
+        inverses = []
+        for j in range(8):
+            inverses.append(1.0 / pivots[j, j])
+            scales.append(lax.rsqrt(pivots[j, j]))
+            for i in range(j + 1, 8):
+                ratio = pivots[i, j] * inverses[j]
+                for m in range(i, 8):
+                    pivots[m, i] = pivots[m, i] - ratio * pivots[m, j]
+                rows[i] = rows[i] - ratio * rows[j]
+                for t in range(own + 1, size // 8):
+                    spread[t, i] = spread[t, i] - ratio * spread[t, j]
+        for t in range(own + 1, size // 8):
+            update = (spread[t, 0] * inverses[0]) * rows[0]
+            for j in range(1, 8):
+                update = update + (spread[t, j] * inverses[j]) * rows[j]
             tiles[t] = tiles[t] - update
-        scales.append(lax.rsqrt(pivot))
+        for j in range(8):
+            tiles[own] = jnp.where(sub == j, rows[j], tiles[own])
     for t in range(size // 8):
         scale = scales[8 * t]
         for at in range(1, 8):
             scale = jnp.where(sub == at, scales[8 * t + at], scale)
-        rows = tiles[t] * scale
+        scaled = tiles[t] * scale
         column = lax.broadcasted_iota(jnp.int32, (8, size), 1)
         here = lax.broadcasted_iota(jnp.int32, (8, size), 0) + 8 * t
-        upper[8 * t : 8 * t + 8] = jnp.where(column >= here, rows[:, :size], 0.0)
-        inverse[8 * t : 8 * t + 8] = rows[:, size:]
-    count = basis.shape[0]
+        upper[8 * t : 8 * t + 8] = jnp.where(column >= here, scaled[:, :size], 0.0)
+        inverse[8 * t : 8 * t + 8] = scaled[:, size:]
+    blocks, count, width = basis.shape
     own_rows = inverse[pl.ds(pl.multiple_of(where[0] * count, 8), count)]
-    width = basis.shape[2]
-    for n in range(basis.shape[1]):
-        basis[:, n, :] = jnp.dot(
-            own_rows,
-            panel[:, n * width : (n + 1) * width],
-            precision=lax.Precision.HIGHEST,
-            preferred_element_type=F32,
+
+    def project(columns):
+        return jnp.dot(
+            own_rows, columns, precision=lax.Precision.HIGHEST, preferred_element_type=F32
         )
+
+    basis[0] = project(edge[:, :width])
+    for n in range(blocks - 2):
+        basis[n + 1] = project(inner[:, n * width : (n + 1) * width])
+    basis[blocks - 1] = project(edge[:, width:])
 
 
 VMEM = pl.BlockSpec(memory_space=pltpu.VMEM)
 SMEM = pl.BlockSpec(memory_space=pltpu.SMEM)
-ANY = pl.BlockSpec(memory_space=pl.ANY)
-LIMIT = 48 * 1024 * 1024
+HBM = pl.BlockSpec(memory_space=pltpu.HBM)
+MIB = 1024 * 1024
+
+
+def shape(*dims):
+    return jax.ShapeDtypeStruct(dims, F32)
+
+
+def call(kernel, name, out_shape, in_specs, scratch=(), flops=0):
+    return pl.pallas_call(
+        kernel,
+        out_shape=out_shape,
+        in_specs=in_specs,
+        out_specs=jax.tree.map(lambda _: VMEM, out_shape),
+        scratch_shapes=scratch,
+        compiler_params=pltpu.CompilerParams(vmem_limit_bytes=32 * MIB),
+        cost_estimate=pl.CostEstimate(flops=flops, bytes_accessed=4_000_000, transcendentals=0),
+        name=name,
+    )
 
 
 def body(increments, winds, obs_weight):
     count, lons, levels, lats = increments.shape
     blocks = lons // 4
+    probes = count * lax.axis_size("probe")
     ring = lax.axis_size("lon")
     up = [(i, (i + 1) % ring) for i in range(ring)]
     down = [(i, (i - 1) % ring) for i in range(ring)]
-    pack_up = jnp.concatenate([winds[0, -3:], winds[1, -3:], obs_weight[-2:]], axis=0)
-    pack_down = jnp.concatenate([winds[0, :4], winds[1, :4], obs_weight[:2]], axis=0)
+    dma = pltpu.SemaphoreType.DMA
+    increments, winds, obs_weight = (
+        pltpu.with_memory_space_constraint(x, pltpu.HBM) for x in (increments, winds, obs_weight)
+    )
+    pack_up, pack_down = call(
+        pack_kernel,
+        "pack",
+        (shape(8, levels, lats), shape(10, levels, lats)),
+        [HBM, HBM],
+        [dma((6,))],
+    )(winds, obs_weight)
     from_low = lax.ppermute(pack_up, "lon", up)
     from_high = lax.ppermute(pack_down, "lon", down)
-    inner = pl.pallas_call(
+    inner = call(
         interior_kernel,
-        out_shape=jax.ShapeDtypeStruct((count, (blocks - 2) * 512), F32),
-        in_specs=[VMEM, VMEM, ANY],
-        out_specs=VMEM,
-        scratch_shapes=[
+        "interior",
+        shape(count, (blocks - 2) * 512),
+        [HBM, HBM, HBM],
+        [
+            pltpu.VMEM((2, lons, levels, lats), F32),
+            pltpu.VMEM((lons, levels, lats), F32),
             pltpu.VMEM((PLANES, lons, levels, lats), F32),
             pltpu.VMEM((blocks - 2, 3, 12, levels, lats), F32),
             pltpu.VMEM((6, (blocks - 2) * count * 8, HALF), F32),
             pltpu.VMEM((count, lons, levels, lats), F32),
-            pltpu.SemaphoreType.DMA,
+            dma((3,)),
         ],
-        compiler_params=pltpu.CompilerParams(vmem_limit_bytes=LIMIT),
-        name="interior",
+        200_000_000,
     )(winds, obs_weight, increments)
-    edges = pl.pallas_call(
+    edges = call(
         edge_kernel,
-        out_shape=jax.ShapeDtypeStruct((count, 4 * 512), F32),
-        in_specs=[VMEM, VMEM, VMEM, VMEM, ANY],
-        out_specs=VMEM,
-        scratch_shapes=[
+        "edges",
+        (shape(count, 512),) * 4,
+        [HBM, HBM, VMEM, VMEM, HBM],
+        [
+            pltpu.VMEM((2, 16, levels, lats), F32),
+            pltpu.VMEM((16, levels, lats), F32),
             pltpu.VMEM((PLANES, 23, levels, lats), F32),
             pltpu.VMEM((4, 3, 12, levels, lats), F32),
             pltpu.VMEM((6, 4 * count * 8, HALF), F32),
             pltpu.VMEM((count, 16, levels, lats), F32),
-            pltpu.SemaphoreType.DMA((2,)),
+            dma((6,)),
         ],
-        compiler_params=pltpu.CompilerParams(vmem_limit_bytes=LIMIT),
-        name="edges",
+        100_000_000,
     )(winds, obs_weight, from_low, from_high, increments)
-    to_low, own_low, own_high, to_high = jnp.split(edges, 4, axis=1)
+    to_low, own_low, own_high, to_high = edges
+    inner, own_low = lax.optimization_barrier((inner, own_low))
     own_low = own_low + lax.ppermute(to_high, "lon", up)
     own_high = own_high + lax.ppermute(to_low, "lon", down)
-    coarse = jnp.concatenate([own_low, inner, own_high], axis=1)
-    panel = lax.all_gather(coarse, "probe", axis=0, tiled=True)
-    gram = jnp.dot(
-        panel, panel.T, precision=lax.Precision.HIGHEST, preferred_element_type=F32
-    )
-    grams = lax.all_to_all(
-        jnp.broadcast_to(gram[None], (ring,) + gram.shape), "lon", 0, 0, tiled=True
-    )
-    probes = panel.shape[0]
-    basis, upper = pl.pallas_call(
+    inner_panel = lax.all_gather(inner, "probe", axis=0, tiled=True)
+    inner_gram = call(
+        inner_gram_kernel, "inner_gram", shape(probes, probes), [VMEM], (), 25_000_000
+    )(inner_panel)
+    edge_panel = lax.all_gather(
+        jnp.concatenate([own_low, own_high], axis=1), "probe", axis=0, tiled=True
+    )
+    grams = call(
+        gram_kernel, "gram", shape(ring, probes // 2, 2 * probes), [VMEM, VMEM], (), 10_000_000
+    )(edge_panel, inner_gram)
+    grams = lax.all_to_all(grams, "lon", 0, 0, tiled=True)
+    basis, upper = call(
         factor_kernel,
-        out_shape=(
-            jax.ShapeDtypeStruct((count, blocks, 512), F32),
-            jax.ShapeDtypeStruct((probes, probes), F32),
-        ),
-        in_specs=[SMEM, VMEM, VMEM],
-        out_specs=(VMEM, VMEM),
-        scratch_shapes=[pltpu.VMEM((probes, probes), F32)],
-        compiler_params=pltpu.CompilerParams(vmem_limit_bytes=LIMIT),
-        name="factor",
-    )(lax.axis_index("probe").reshape(1).astype(jnp.int32), grams, panel)
-    return basis, upper
+        "factor",
+        (shape(blocks, count, 512), shape(probes, probes)),
+        [SMEM, VMEM, VMEM, VMEM],
+        [pltpu.VMEM((probes, probes), F32)],
+        10_000_000,
+    )(lax.axis_index("probe").reshape(1).astype(jnp.int32), grams, inner_panel, edge_panel)
+    return basis.transpose(1, 0, 2), upper
 
 
 def solution(mesh):

time: 68.9 us -> 52.4 us (0.76)
  waiting for transfers between devices: 21.3 us -> 7.87 us
  local copies, waits for them, and re-layouts: 8.36 us -> 0 us
  starting transfers between devices: 9.58 us -> 14.2 us
  blocking collectives: 8.63 us -> 13 us
  Pallas kernels: 18 us -> 16.2 us
  other arithmetic: 1 us -> 0.02 us
  matrix products: 0.76 us -> 0 us
    ppermute x1, waiting for transfers between devices: 6.95 us -> 0.15 us  [body(): from_low = lax.ppermute(pack_up, 'lon', up)]
    ppermute x1, waiting for transfers between devices: 6.6 us -> 0.01 us  [body(): own_low = own_low + lax.ppermute(to_high, 'lon', up)]
    unnamed x10 -> x0, local copies, waits for them, and re-layouts: 4.75 us -> none
    ppermute x1, starting transfers between devices: 0.06 us -> 4.71 us  [body(): own_high = own_high + lax.ppermute(to_low, 'lon', down)]
    all_gather x1 -> x2, blocking collectives: 8.63 us -> 13 us  [the longest x1 7.18 us: body(): inner_panel = lax.all_gather(inner, 'probe', axis=0, tiled=True)]
    pallas_call x3 -> x6, Pallas kernels: 18 us -> 16.2 us  [the longest x1 6.8 us: body(): call(interior_kernel, 'interior', shape(count, (blocks - 2) * 512), [HBM,...]
    squeeze x2 -> x0, local copies, waits for them, and re-layouts: 1.54 us -> none  [the longest x1 0.78 us: body(): winds[0, :4]]
    all_to_all x1 -> x0, other arithmetic: 0.95 us -> none  [body(): lax.all_to_all(jnp.broadcast_to(gram[None], (ring,) + gram.shape), 'lon',...]
  transfers between devices with their start and end apart: 5 -> 5, of which waited for: 3 -> 2; matrix products, arithmetic and copies ran while one was open for 1% -> 0% of each run, Pallas kernels for 9% -> 14%
where the time goes in v2:
time: 52.4 us; the launch traced here: 52 us
  Pallas kernels  16.2 us (31%)
  starting transfers between devices  14.2 us (27%)
  blocking collectives  13 us (25%)
  waiting for transfers between devices  7.87 us (15%)
  between operations  0.72 us (1%)
    all_to_all x1, waiting for transfers between devices, body(): grams = lax.all_to_all(grams, 'lon', 0, 0, tiled=True)  7.71 us
    all_gather x1, blocking collectives, body(): inner_panel = lax.all_gather(inner, 'probe', axis=0, tiled=True)  7.18 us
    pallas_call x1, Pallas kernels, body(): call(interior_kernel, 'interior', shape(count, (blocks - 2) * 512), [HBM,...  6.8 us
    ppermute x1, starting transfers between devices, body(): from_high = lax.ppermute(pack_down, 'lon', down)  6.03 us
    all_gather x1, blocking collectives, body(): lax.all_gather(jnp.concatenate([own_low, own_high], axis=1), 'probe', axi...  5.86 us
    ppermute x1, starting transfers between devices, body(): own_high = own_high + lax.ppermute(to_low, 'lon', down)  4.71 us
    pallas_call x1, Pallas kernels, body(): call(edge_kernel, 'edges', (shape(count, 512),) * 4, [HBM, HBM, VMEM, VME...  3.72 us
    all_to_all x1, starting transfers between devices, body(): grams = lax.all_to_all(grams, 'lon', 0, 0, tiled=True)  3.37 us
  transfers between devices with their start and end apart: 5, of which 2 were waited for; matrix products, arithmetic and copies ran while one was open for 0% of the time, Pallas kernels for 14%

profile of v2, /device:TPU:0, one launch (start us, length us, event | category | flops | bytes accessed | tf_op | source)
XLA Modules:
  0.0 52.0 jit_solution(15601252598640124103)
XLA Ops:
  0.6 0.9 %pack.1 = (f32[8,8,256]{2,1,0:T(8,128)S(1)}, f32[10,8,256]{2,1,0:T(8,128)S(1)}) custom-call(f32[2,24,8,256]{3,2,1,0:T(8,128)} %winds_hbm.3, f32[24,8,256]{2,1,0:T(8,128)} %obs_hbm.3), custom_call_target="tpu_custom_call" | custom-call | bytes 4000000 | tf_op jit(solution)/shard_map/pack/pallas_call | solution.py:555
  1.5 6.0 %collective-permute-start.1 = (f32[10,8,256]{2,1,0:T(8,128)S(1)}, f32[10,8,256]{2,1,0:T(8,128)S(1)}, u32[]{:S(2)}, u32[]{:S(2)}) collective-permute-start(f32[10,8,256]{2,1,0:T(8,128)S(1)} %get-tuple-element.13), channel_id=1, source_target_pairs={{0,28},{4,0},{8,4},{12,8},{16,12},{20,16},{24,20},{28,24},{1,29},{... | collective-permute-start | bytes 245768 | tf_op jit(solution)/shard_map/ppermute | solution.py:563
  7.5 0.0 collective-permute-start
  7.6 6.8 %interior.1 = f32[16,2048]{1,0:T(8,128)S(1)} custom-call(f32[2,24,8,256]{3,2,1,0:T(8,128)} %winds_hbm.3, f32[24,8,256]{2,1,0:T(8,128)} %obs_hbm.3, f32[16,24,8,256]{3,2,1,0:T(8,128)} %field_hbm.3), custom_call_target="tpu_custom_call" | custom-call | flops 200000000 | bytes 4000000 | tf_op jit(solution)/shard_map/interior/pallas_call | solution.py:564
  14.4 0.2 collective-permute-done.from_low
  14.5 0.0 collective-permute-done.1.from_high
  14.5 3.7 %edges.1 = (f32[16,512]{1,0:T(8,128)S(1)}, f32[16,512]{1,0:T(8,128)S(1)}, f32[16,512]{1,0:T(8,128)S(1)}, f32[16,512]{1,0:T(8,128)S(1)}) custom-call(f32[2,24,8,256]{3,2,1,0:T(8,128)} %winds_hbm.3, f32[24,8,256]{2,1,0:T(8,128)} %obs_hbm.3, f32[8,8,256]{2,1,0:T(8,128)S(1)} %collective-permute-done.from_low, ...), custom_call_target="tpu_custom_call" | custom-call | flops 100000000 | bytes 4000000 | tf_op jit(solution)/shard_map/edges/pallas_call | solution.py:580
  18.2 0.1 collective-permute-start.2
  18.3 4.7 %collective-permute-start.3 = (f32[16,512]{1,0:T(8,128)S(1)}, f32[16,512]{1,0:T(8,128)S(1)}, u32[]{:S(2)}, u32[]{:S(2)}) collective-permute-start(f32[16,512]{1,0:T(8,128)S(1)} %get-tuple-element.18), channel_id=1, source_target_pairs={{0,28},{4,0},{8,4},{12,8},{16,12},{20,16},{24,20},{28,24},{1,29},{... | collective-permute-start | bytes 98312 | tf_op jit(solution)/shard_map/ppermute | solution.py:599
  23.0 7.2 %all_gather.7.panel.inner = f32[64,2048]{1,0:T(8,128)S(1)} all-gather(f32[16,2048]{1,0:T(8,128)S(1)} %interior.1), channel_id=1, replica_groups=mesh['lon'=8,'probe'=4] {'probe'}, dimensions={0}, use_global_device_ids=true | all-gather | bytes 655360 | tf_op jit(solution)/shard_map/all_gather | solution.py:600
  30.2 0.6 %inner_gram.1.inner = f32[64,64]{1,0:T(8,128)S(1)} custom-call(f32[64,2048]{1,0:T(8,128)S(1)} %all_gather.7.panel.inner), custom_call_target="tpu_custom_call" | custom-call | flops 25000000 | bytes 4000000 | tf_op jit(solution)/shard_map/inner_gram/pallas_call | solution.py:601
  30.8 0.0 collective-permute-done.2
  30.8 0.0 collective-permute-done.3
  30.8 5.9 %all_gather.6.panel.edge = f32[64,1024]{1,0:T(8,128)S(1)} all-gather(f32[16,1024]{1,0:T(8,128)S(1)} %pad_maximum_fusion), channel_id=1, replica_groups=mesh['lon'=8,'probe'=4] {'probe'}, dimensions={0}, use_global_device_ids=true | all-gather | bytes 327680 | tf_op jit(solution)/shard_map/all_gather | solution.py:604
  36.7 1.1 %gram.1 = f32[8,32,128]{2,1,0:T(8,128)} custom-call(f32[64,1024]{1,0:T(8,128)S(1)} %all_gather.6.panel.edge, f32[64,64]{1,0:T(8,128)S(1)} %inner_gram.1.inner), custom_call_target="tpu_custom_call" | custom-call | flops 10000000 | bytes 4000000 | tf_op jit(solution)/shard_map/gram/pallas_call | solution.py:607
  37.8 3.4 %all-to-all-start = ((f32[8,32,128]{2,1,0:T(8,128)}), f32[8,32,128]{2,1,0:T(8,128)S(1)}, u32[]{:S(2)}, u32[]{:S(2)}) async-start(f32[8,32,128]{2,1,0:T(8,128)} %gram.1), calls=%async_computation | async-start | bytes 262144 | tf_op jit(solution)/shard_map/all_to_all | solution.py:610
  41.2 7.7 %all-to-all-done.grams = f32[8,32,128]{2,1,0:T(8,128)S(1)} async-done(((f32[8,32,128]{2,1,0:T(8,128)}), f32[8,32,128]{2,1,0:T(8,128)S(1)}, u32[]{:S(2)}, u32[]{:S(2)}) %all-to-all-start) | async-done | bytes 131104 | tf_op jit(solution)/shard_map/all_to_all | solution.py:610
  48.9 3.1 %factor.1 = (f32[6,16,512]{2,1,0:T(8,128)}, f32[64,64]{1,0:T(8,128)}) custom-call(s32[1]{0:T(128)} %bitcast.where, f32[8,32,128]{2,1,0:T(8,128)S(1)} %all-to-all-done.grams, f32[64,2048]{1,0:T(8,128)S(1)} %all_gather.7.panel.inner, f32[64,1024]{1,0:T(8,128)S(1)} %all_gather.6.panel.edge), custom_call_target="tpu_custom_call" | custom-call | flops 10000000 | bytes 4000000 | tf_op jit(solution)/shard_map/factor/pallas_call | solution.py:611
  (3 shorter events, 0.0 us)
Async XLA Ops:
  1.5 13.0 %collective-permute-start.1 = (f32[10,8,256]{2,1,0:T(8,128)S(1)}, f32[10,8,256]{2,1,0:T(8,128)S(1)}, u32[]{:S(2)}, u32[]{:S(2)}) collective-permute-start(f32[10,8,256]{2,1,0:T(8,128)S(1)} %get-tuple-element.13), channel_id=1, source_target_pairs={{0,28},{4,0},{8,4},{12,8},{16,12},{20,16},{24,20},{28,24},{1,29},{... | collective-permute-start | bytes 245768 | tf_op jit(solution)/shard_map/ppermute | solution.py:563
  7.5 7.0 %collective-permute-start = (f32[8,8,256]{2,1,0:T(8,128)S(1)}, f32[8,8,256]{2,1,0:T(8,128)S(1)}, u32[]{:S(2)}, u32[]{:S(2)}) collective-permute-start(f32[8,8,256]{2,1,0:T(8,128)S(1)} %get-tuple-element.12), channel_id=1, source_target_pairs={{0,4},{4,8},{8,12},{12,16},{16,20},{20,24},{24,28},{28,0},{1,5},{5... | collective-permute-start | bytes 196616 | tf_op jit(solution)/shard_map/ppermute | solution.py:562
  18.2 12.5 %collective-permute-start.2 = (f32[16,512]{1,0:T(8,128)S(1)}, f32[16,512]{1,0:T(8,128)S(1)}, u32[]{:S(2)}, u32[]{:S(2)}) collective-permute-start(f32[16,512]{1,0:T(8,128)S(1)} %get-tuple-element.16), channel_id=1, source_target_pairs={{0,4},{4,8},{8,12},{12,16},{16,20},{20,24},{24,28},{28,0},{1,5},{5... | collective-permute-start | bytes 98312 | tf_op jit(solution)/shard_map/ppermute | solution.py:598
  18.3 12.5 %collective-permute-start.3 = (f32[16,512]{1,0:T(8,128)S(1)}, f32[16,512]{1,0:T(8,128)S(1)}, u32[]{:S(2)}, u32[]{:S(2)}) collective-permute-start(f32[16,512]{1,0:T(8,128)S(1)} %get-tuple-element.18), channel_id=1, source_target_pairs={{0,28},{4,0},{8,4},{12,8},{16,12},{20,16},{24,20},{28,24},{1,29},{... | collective-permute-start | bytes 98312 | tf_op jit(solution)/shard_map/ppermute | solution.py:599
  37.8 11.1 %all-to-all-start = ((f32[8,32,128]{2,1,0:T(8,128)}), f32[8,32,128]{2,1,0:T(8,128)S(1)}, u32[]{:S(2)}, u32[]{:S(2)}) async-start(f32[8,32,128]{2,1,0:T(8,128)} %gram.1), calls=%async_computation | async-start | bytes 262144 | tf_op jit(solution)/shard_map/all_to_all | solution.py:610

commit v3 on v2

--- a/solution.py
+++ b/solution.py
@@ -163,8 +163,7 @@
     return weights
 
 
-def apply_weights(keys, read_weight, read_field, write, probes):
-    count = len(probes)
+def apply_weights(lanes, keys, read_weight, read_field, write, probes):
     sums = {}
     for r in sorted({r for r, _ in keys}):
         fields = [read_field(probe, r) for probe in probes]
@@ -172,30 +171,30 @@
             if (r, part) not in keys:
                 continue
             weight = read_weight(r, part)
-            for n in range(count):
+            for n in range(len(probes)):
                 for h in (0, 1):
                     term = weight[h] * fields[n][h]
                     key = (n, part, h)
                     sums[key] = sums[key] + term if key in sums else term
+    low = lanes.phase < 2
     for n, probe in enumerate(probes):
-        for part in range(3):
-            for h in (0, 1):
-                if (n, part, h) in sums:
-                    write(probe, part, h, sums[n, part, h])
-                else:
-                    write(probe, part, h, jnp.zeros((8, HALF), F32))
+        own, near, far = ([sums.get((n, part, h)) for h in (0, 1)] for part in range(3))
+        if far[0] is None:
+            down = [jnp.where(low, x, 0.0) for x in near]
+            up = [jnp.where(low, 0.0, x) for x in near]
+        else:
+            down = [jnp.where(low, x, y) for x, y in zip(near, far)]
+            up = [jnp.where(low, y, x) for x, y in zip(near, far)]
+        for h in (0, 1):
+            write(probe, 0, h, own[h])
+            write(probe, 1, h, down[h])
+            write(probe, 2, h, up[h])
 
 
 def pooling(parity):
-    row = lax.broadcasted_iota(jnp.int32, (3 * 256, HALF), 0)
-    column = lax.broadcasted_iota(jnp.int32, (3 * 256, HALF), 1) - 64 * parity
-    part, lat = row >> 8, row & 255
-    low = (lat & 3) < 2
-    shift = jnp.where(
-        part == 0, 0, jnp.where(part == 1, jnp.where(low, -1, 1), jnp.where(low, 1, -1))
-    )
-    hit = (column >= 0) & (column < 64) & ((lat >> 2) + shift == column)
-    return jnp.where(hit, 1.0 / 16.0, 0.0).astype(BF16)
+    row = lax.broadcasted_iota(jnp.int32, (256, HALF), 0)
+    column = lax.broadcasted_iota(jnp.int32, (256, HALF), 1)
+    return jnp.where((row >> 2) + 64 * parity == column, 1.0 / 16.0, 0.0).astype(BF16)
 
 
 def split3(x):
@@ -206,22 +205,30 @@
     return high, middle, low
 
 
-def pool_into(sums, rows, count, write):
+def pool_into(lanes, sums, rows, count, write):
     total = None
     for parity in (0, 1):
         matrix = pooling(parity)
-        pieces = [
-            jnp.concatenate(
-                [
-                    sums[piece, pl.ds(n * count * 8 + 2 * pair + parity, count, stride=8), :]
-                    for piece in range(6)
-                ],
-                axis=1,
-            )
-            for n in range(rows)
-            for pair in range(4)
-        ]
-        for part in split3(jnp.concatenate(pieces, axis=0)):
+        own, down, up = (
+            [
+                jnp.concatenate(
+                    [
+                        sums[2 * part + h, pl.ds(n * count * 8 + 2 * pair + parity, count, stride=8), :]
+                        for n in range(rows)
+                        for pair in range(4)
+                    ],
+                    axis=0,
+                )
+                for h in (0, 1)
+            ]
+            for part in range(3)
+        )
+        lane = lax.broadcasted_iota(jnp.int32, own[0].shape, 1)
+        d0, d1 = (pltpu.roll(x, HALF - 4, 1) for x in down)
+        u0, u1 = (pltpu.roll(x, 4, 1) for x in up)
+        low = own[0] + (jnp.where(lane >= HALF - 4, d1, d0) + jnp.where(lane < 4, u1, u0))
+        high = own[1] + (jnp.where(lane >= HALF - 4, d0, d1) + jnp.where(lane < 4, u0, u1))
+        for part in split3(jnp.concatenate([low, high], axis=1)):
             term = jnp.dot(part, matrix, preferred_element_type=F32)
             total = term if total is None else total + term
     for n in range(rows):
@@ -230,7 +237,7 @@
             write(n, pair, total[start : start + count])
 
 
-GROUP = 4
+GROUP = 8
 
 
 def fetch_all(copies):
@@ -239,36 +246,33 @@
     return copies
 
 
-def pack_kernel(winds, obs, low, high, sems):
+def pack_kernel(winds_hbm, obs_hbm, up, down, winds, obs, sems):
     lons = obs.shape[0]
     copies = fetch_all(
         [
-            pltpu.make_async_copy(winds.at[0, pl.ds(lons - 3, 3)], low.at[pl.ds(0, 3)], sems.at[0]),
-            pltpu.make_async_copy(winds.at[1, pl.ds(lons - 3, 3)], low.at[pl.ds(3, 3)], sems.at[1]),
-            pltpu.make_async_copy(obs.at[pl.ds(lons - 2, 2)], low.at[pl.ds(6, 2)], sems.at[2]),
-            pltpu.make_async_copy(winds.at[0, pl.ds(0, 4)], high.at[pl.ds(0, 4)], sems.at[3]),
-            pltpu.make_async_copy(winds.at[1, pl.ds(0, 4)], high.at[pl.ds(4, 4)], sems.at[4]),
-            pltpu.make_async_copy(obs.at[pl.ds(0, 2)], high.at[pl.ds(8, 2)], sems.at[5]),
+            pltpu.make_async_copy(winds_hbm, winds, sems.at[0]),
+            pltpu.make_async_copy(obs_hbm, obs, sems.at[1]),
         ]
     )
     for copy in copies:
         copy.wait()
+    up[0:3] = winds[0, lons - 3 :]
+    up[3:6] = winds[1, lons - 3 :]
+    up[6:8] = obs[lons - 2 :]
+    up[8:] = obs[lons - 4 :]
+    down[0:4] = winds[0, 0:4]
+    down[4:8] = winds[1, 0:4]
+    down[8:10] = obs[0:2]
 
 
 def interior_kernel(
-    winds_hbm, obs_hbm, field_hbm, out, winds, obs, coef, weights, sums, field, sems
+    winds, obs, field_hbm, out, coef, weights, sums, field, sem
 ):
     count, lons = field.shape[0], field.shape[1]
     blocks = lons // 4 - 2
-    wind_copy, obs_copy, field_copy = fetch_all(
-        [
-            pltpu.make_async_copy(winds_hbm, winds, sems.at[0]),
-            pltpu.make_async_copy(obs_hbm, obs, sems.at[1]),
-            pltpu.make_async_copy(field_hbm, field, sems.at[2]),
-        ]
-    )
+    field_copy = pltpu.make_async_copy(field_hbm, field, sem)
+    field_copy.start()
     lanes = Lanes()
-    wind_copy.wait()
 
     def coefficients(lon, carry):
         write_coefficients(
@@ -281,8 +285,7 @@
         )
         return carry
 
-    lax.fori_loop(0, lons, coefficients, 0)
-    obs_copy.wait()
+    lax.fori_loop(0, lons, coefficients, 0, unroll=4)
 
     def weigh(block, carry):
         base = (block + 1) * 4
@@ -311,6 +314,7 @@
             sums[2 * part + h, pl.ds(row, 8), :] = value
 
         apply_weights(
+            lanes,
             keys,
             lambda r, part: halves(weights, block, part, r + 4),
             lambda probe, r: halves(field, probe, block * 4 + 4 + r),
@@ -325,39 +329,27 @@
         column = (n * 4 + pair) * HALF
         out[:, column : column + HALF] = value
 
-    pool_into(sums, blocks, count, put)
+    pool_into(lanes, sums, blocks, count, put)
 
 
 def edge_kernel(
-    winds_hbm, obs_hbm, from_low, from_high, field_hbm,
+    winds, obs, from_low, from_high, field_hbm,
     to_low, own_low, own_high, to_high,
-    winds, obs, coef, weights, sums, field, sems,
+    coef, weights, sums, field, sems,
 ):
     count, lons = field_hbm.shape[0], field_hbm.shape[1]
-    sides = ((0, 0), (1, lons - 8))
-    copies = fetch_all(
-        [
-            pltpu.make_async_copy(
-                winds_hbm.at[:, pl.ds(start, 8)], winds.at[:, pl.ds(8 * side, 8)], sems.at[side]
-            )
-            for side, start in sides
-        ]
-        + [
-            pltpu.make_async_copy(
-                obs_hbm.at[pl.ds(start, 8)], obs.at[pl.ds(8 * side, 8)], sems.at[2 + side]
-            )
-            for side, start in sides
-        ]
-        + [
-            pltpu.make_async_copy(
-                field_hbm.at[:, pl.ds(start, 8)], field.at[:, pl.ds(8 * side, 8)], sems.at[4 + side]
-            )
-            for side, start in sides
-        ]
-    )
+    def fetch(side):
+        return pltpu.make_async_copy(
+            field_hbm.at[:, pl.ds(side * (lons - 8), 8)],
+            field.at[:, pl.ds(8 * side, 8)],
+            sems.at[side],
+        )
+
+    @pl.loop(0, 2)
+    def _(side):
+        fetch(side).start()
+
     lanes = Lanes()
-    for copy in copies[:4]:
-        copy.wait()
 
     def near(lon):
         return lon if lon < 8 else lon - (lons - 16)
@@ -367,14 +359,14 @@
             return halves(from_low, 3 * which + lon + 3)
         if lon >= lons:
             return halves(from_high, 4 * which + lon - lons)
-        return halves(winds, which, near(lon))
+        return halves(winds, which, lon)
 
     def weight_at(lon):
         if lon < 0:
             return halves(from_low, 6 + lon + 2)
         if lon >= lons:
             return halves(from_high, 8 + lon - lons)
-        return halves(obs, near(lon))
+        return halves(obs, lon)
 
     slots = {}
     for lon in list(range(-3, 8)) + list(range(lons - 8, lons + 4)):
@@ -401,33 +393,34 @@
         for (r, part), value in result.items():
             store(weights, value, n, part, r + 4)
         kept.append(set(result))
-    for copy in copies[4:]:
-        copy.wait()
-
-    def sweep(step, carry):
-        start = step * GROUP
-        for n, (base, first, last) in enumerate(jobs):
-
-            def write(probe, part, h, value):
-                row = pl.multiple_of((n * count + probe) * 8, 8)
-                sums[2 * part + h, pl.ds(row, 8), :] = value
-
-            apply_weights(
-                kept[n],
-                lambda r, part: halves(weights, n, part, r + 4),
-                lambda probe, r: halves(field, probe, near(base + r)),
-                write,
-                [start + k for k in range(GROUP)],
-            )
+
+    @pl.loop(0, 2)
+    def _(side):
+        fetch(side).wait()
+
+    def sweep(n, base, step, carry):
+        def write(probe, part, h, value):
+            row = pl.multiple_of((n * count + probe) * 8, 8)
+            sums[2 * part + h, pl.ds(row, 8), :] = value
+
+        apply_weights(
+            lanes,
+            kept[n],
+            lambda r, part: halves(weights, n, part, r + 4),
+            lambda probe, r: halves(field, probe, near(base + r)),
+            write,
+            [step * GROUP + k for k in range(GROUP)],
+        )
         return carry
 
-    lax.fori_loop(0, count // GROUP, sweep, 0)
+    for n, (base, _, _) in enumerate(jobs):
+        lax.fori_loop(0, count // GROUP, functools.partial(sweep, n, base), 0)
     outs = (to_low, own_low, own_high, to_high)
 
     def put(n, pair, value):
         outs[n][:, pair * HALF : (pair + 1) * HALF] = value
 
-    pool_into(sums, 4, count, put)
+    pool_into(lanes, sums, 4, count, put)
 
 
 def self_product(panel):
@@ -440,11 +433,22 @@
     )
 
 
-def inner_gram_kernel(panel, out):
+def assemble(where, pieces, panel):
+    rows = pieces[0].shape[0]
+    for k, piece in enumerate(pieces):
+        at = pl.multiple_of(lax.bitwise_xor(where[0], jnp.int32(k)) * rows, 8)
+        panel[pl.ds(at, rows)] = piece[...]
+
+
+def inner_gram_kernel(where, *refs):
+    pieces, (panel, out) = refs[:-2], refs[-2:]
+    assemble(where, pieces, panel)
     out[...] = self_product(panel[...])
 
 
-def gram_kernel(panel, inner, out):
+def gram_kernel(where, inner, *refs):
+    pieces, (panel, out) = refs[:-2], refs[-2:]
+    assemble(where, pieces, panel)
     gram = self_product(panel[...]) + inner[...]
     half = gram.shape[0] // 2
     packed = jnp.concatenate([gram[:half], gram[half:]], axis=1)
@@ -541,6 +545,15 @@
     )
 
 
+def gather_pieces(rows):
+    size = lax.axis_size("probe")
+    pieces = [rows]
+    for k in range(1, size):
+        source, step = (pieces[k - 1], 1) if k > 1 and k & 1 else (rows, k)
+        pieces.append(lax.ppermute(source, "probe", [(i, i ^ step) for i in range(size)]))
+    return pieces
+
+
 def body(increments, winds, obs_weight):
     count, lons, levels, lats = increments.shape
     blocks = lons // 4
@@ -548,16 +561,22 @@
     ring = lax.axis_size("lon")
     up = [(i, (i + 1) % ring) for i in range(ring)]
     down = [(i, (i - 1) % ring) for i in range(ring)]
+    where = lax.axis_index("probe").reshape(1).astype(jnp.int32)
     dma = pltpu.SemaphoreType.DMA
     increments, winds, obs_weight = (
         pltpu.with_memory_space_constraint(x, pltpu.HBM) for x in (increments, winds, obs_weight)
     )
-    pack_up, pack_down = call(
+    pack_up, pack_down, winds, obs_weight = call(
         pack_kernel,
         "pack",
-        (shape(8, levels, lats), shape(10, levels, lats)),
+        (
+            shape(12, levels, lats),
+            shape(10, levels, lats),
+            shape(2, lons, levels, lats),
+            shape(lons, levels, lats),
+        ),
         [HBM, HBM],
-        [dma((6,))],
+        [dma((2,))],
     )(winds, obs_weight)
     from_low = lax.ppermute(pack_up, "lon", up)
     from_high = lax.ppermute(pack_down, "lon", down)
@@ -565,48 +584,52 @@
         interior_kernel,
         "interior",
         shape(count, (blocks - 2) * 512),
-        [HBM, HBM, HBM],
+        [VMEM, VMEM, HBM],
         [
-            pltpu.VMEM((2, lons, levels, lats), F32),
-            pltpu.VMEM((lons, levels, lats), F32),
             pltpu.VMEM((PLANES, lons, levels, lats), F32),
             pltpu.VMEM((blocks - 2, 3, 12, levels, lats), F32),
             pltpu.VMEM((6, (blocks - 2) * count * 8, HALF), F32),
             pltpu.VMEM((count, lons, levels, lats), F32),
-            dma((3,)),
+            dma,
         ],
         200_000_000,
     )(winds, obs_weight, increments)
+    inner, from_low, from_high = lax.optimization_barrier((inner, from_low, from_high))
+    inner_pieces = gather_pieces(inner)
     edges = call(
         edge_kernel,
         "edges",
         (shape(count, 512),) * 4,
-        [HBM, HBM, VMEM, VMEM, HBM],
+        [VMEM, VMEM, VMEM, VMEM, HBM],
         [
-            pltpu.VMEM((2, 16, levels, lats), F32),
-            pltpu.VMEM((16, levels, lats), F32),
             pltpu.VMEM((PLANES, 23, levels, lats), F32),
             pltpu.VMEM((4, 3, 12, levels, lats), F32),
             pltpu.VMEM((6, 4 * count * 8, HALF), F32),
             pltpu.VMEM((count, 16, levels, lats), F32),
-            dma((6,)),
+            dma((2,)),
         ],
         100_000_000,
     )(winds, obs_weight, from_low, from_high, increments)
     to_low, own_low, own_high, to_high = edges
-    inner, own_low = lax.optimization_barrier((inner, own_low))
     own_low = own_low + lax.ppermute(to_high, "lon", up)
     own_high = own_high + lax.ppermute(to_low, "lon", down)
-    inner_panel = lax.all_gather(inner, "probe", axis=0, tiled=True)
-    inner_gram = call(
-        inner_gram_kernel, "inner_gram", shape(probes, probes), [VMEM], (), 25_000_000
-    )(inner_panel)
-    edge_panel = lax.all_gather(
-        jnp.concatenate([own_low, own_high], axis=1), "probe", axis=0, tiled=True
-    )
-    grams = call(
-        gram_kernel, "gram", shape(ring, probes // 2, 2 * probes), [VMEM, VMEM], (), 10_000_000
-    )(edge_panel, inner_gram)
+    edge_pieces = gather_pieces(jnp.concatenate([own_low, own_high], axis=1))
+    inner_panel, inner_gram = call(
+        inner_gram_kernel,
+        "inner_gram",
+        (shape(probes, inner.shape[1]), shape(probes, probes)),
+        [SMEM] + [VMEM] * len(inner_pieces),
+        (),
+        25_000_000,
+    )(where, *inner_pieces)
+    edge_panel, grams = call(
+        gram_kernel,
+        "gram",
+        (shape(probes, 1024), shape(ring, probes // 2, 2 * probes)),
+        [SMEM, VMEM] + [VMEM] * len(edge_pieces),
+        (),
+        10_000_000,
+    )(where, inner_gram, *edge_pieces)
     grams = lax.all_to_all(grams, "lon", 0, 0, tiled=True)
     basis, upper = call(
         factor_kernel,
@@ -615,7 +638,7 @@
         [SMEM, VMEM, VMEM, VMEM],
         [pltpu.VMEM((probes, probes), F32)],
         10_000_000,
-    )(lax.axis_index("probe").reshape(1).astype(jnp.int32), grams, inner_panel, edge_panel)
+    )(where, grams, inner_panel, edge_panel)
     return basis.transpose(1, 0, 2), upper
 
 

time: 52.4 us -> 45.6 us (0.87)
  Pallas kernels: 16.2 us -> 11.8 us
  waiting for transfers between devices: 7.87 us -> 6.42 us
  starting transfers between devices: 14.2 us -> 13.3 us
    all_to_all x0 -> x1, blocking collectives: none -> 13.1 us  [body(): grams = lax.all_to_all(grams, 'lon', 0, 0, tiled=True)]
    all_gather x2 -> x0, blocking collectives: 13 us -> none  [the longest x1 7.18 us: body(): inner_panel = lax.all_gather(inner, 'probe', axis=0, tiled=True)]
    all_to_all x1 -> x0, waiting for transfers between devices: 7.71 us -> none  [body(): grams = lax.all_to_all(grams, 'lon', 0, 0, tiled=True)]
    ppermute x0 -> x6, waiting for transfers between devices: none -> 4.53 us  [gather_pieces(): lax.ppermute(source, 'probe', [(i, i ^ step) for i in range(size)])]
    pallas_call x5, Pallas kernels: 13.1 us -> 8.67 us  [the longest x1 3.91 us: body(): call(interior_kernel, 'interior', shape(count, (blocks - 2) * 512), [VMEM...]
    all_to_all x1 -> x0, starting transfers between devices: 3.37 us -> none  [body(): grams = lax.all_to_all(grams, 'lon', 0, 0, tiled=True)]
    ppermute x1, starting transfers between devices: 0.01 us -> 2.99 us  [body(): from_low = lax.ppermute(pack_up, 'lon', up)]
    ppermute x1, starting transfers between devices: 6.03 us -> 3.1 us  [body(): from_high = lax.ppermute(pack_down, 'lon', down)]
  transfers between devices with their start and end apart: 5 -> 10, of which waited for: 2 -> 3; matrix products, arithmetic and copies ran while one was open for 0% -> 0% of each run, Pallas kernels for 14% -> 16%
where the time goes in v3:
time: 45.6 us; the launch traced here: 45.4 us
  starting transfers between devices  13.3 us (29%)
  blocking collectives  13.1 us (29%)
  Pallas kernels  11.8 us (26%)
  waiting for transfers between devices  6.42 us (14%)
  between operations  0.74 us (2%)
    all_to_all x1, blocking collectives, body(): grams = lax.all_to_all(grams, 'lon', 0, 0, tiled=True)  13.1 us
    ppermute x1, starting transfers between devices, body(): own_high = own_high + lax.ppermute(to_low, 'lon', down)  4.71 us
    ppermute x6, waiting for transfers between devices, gather_pieces(): lax.ppermute(source, 'probe', [(i, i ^ step) for i in range(size)])  4.53 us
    pallas_call x1, Pallas kernels, body(): call(interior_kernel, 'interior', shape(count, (blocks - 2) * 512), [VMEM...  3.91 us
    pallas_call x1, Pallas kernels, body(): call(factor_kernel, 'factor', (shape(blocks, count, 512), shape(probes, p...  3.14 us
    ppermute x1, starting transfers between devices, body(): from_high = lax.ppermute(pack_down, 'lon', down)  3.1 us
    ppermute x1, starting transfers between devices, body(): from_low = lax.ppermute(pack_up, 'lon', up)  2.99 us
    pallas_call x1, Pallas kernels, body(): call(edge_kernel, 'edges', (shape(count, 512),) * 4, [VMEM, VMEM, VMEM, V...  2.63 us
  transfers between devices with their start and end apart: 10, of which 3 were waited for; matrix products, arithmetic and copies ran while one was open for 0% of the time, Pallas kernels for 16%

profile of v3, /device:TPU:0, one launch (start us, length us, event | category | flops | bytes accessed | tf_op | source)
XLA Modules:
  0.0 45.4 jit_solution(3680347479911088889)
XLA Ops:
  0.6 1.1 %pack.1 = (f32[12,8,256]{2,1,0:T(8,128)S(1)}, f32[10,8,256]{2,1,0:T(8,128)S(1)}, f32[2,24,8,256]{3,2,1,0:T(8,128)S(1)}, f32[24,8,256]{2,1,0:T(8,128)S(1)}) custom-call(f32[2,24,8,256]{3,2,1,0:T(8,128)} %winds_hbm.1, f32[24,8,256]{2,1,0:T(8,128)} %obs_hbm.1), custom_call_target="tpu_custom_call" | custom-call | bytes 4000000 | tf_op jit(solution)/shard_map/pack/pallas_call | solution.py:569
  1.7 3.0 %collective-permute-start = (f32[12,8,256]{2,1,0:T(8,128)S(1)}, f32[12,8,256]{2,1,0:T(8,128)S(1)}, u32[]{:S(2)}, u32[]{:S(2)}) collective-permute-start(f32[12,8,256]{2,1,0:T(8,128)S(1)} %get-tuple-element.21), channel_id=1, source_target_pairs={{0,4},{4,8},{8,12},{12,16},{16,20},{20,24},{24,28},{28,0},{1,5},{5... | collective-permute-start | bytes 294920 | tf_op jit(solution)/shard_map/ppermute | solution.py:581
  4.7 3.1 %collective-permute-start.1 = (f32[10,8,256]{2,1,0:T(8,128)S(1)}, f32[10,8,256]{2,1,0:T(8,128)S(1)}, u32[]{:S(2)}, u32[]{:S(2)}) collective-permute-start(f32[10,8,256]{2,1,0:T(8,128)S(1)} %get-tuple-element.22), channel_id=1, source_target_pairs={{0,28},{4,0},{8,4},{12,8},{16,12},{20,16},{24,20},{28,24},{1,29},{... | collective-permute-start | bytes 245768 | tf_op jit(solution)/shard_map/ppermute | solution.py:582
  7.8 3.9 %interior.1.refs_0_ = f32[16,2048]{1,0:T(8,128)S(1)} custom-call(f32[2,24,8,256]{3,2,1,0:T(8,128)S(1)} %get-tuple-element.19.winds, f32[24,8,256]{2,1,0:T(8,128)S(1)} %get-tuple-element.20.obs, f32[16,24,8,256]{3,2,1,0:T(8,128)} %field_hbm.3), custom_call_target="tpu_custom_call" | custom-call | flops 200000000 | bytes 4000000 | tf_op jit(solution)/shard_map/interior/pallas_call | solution.py:583
  11.7 0.0 collective-permute-done.1.from_high
  11.7 0.0 collective-permute-done.from_low
  11.8 1.7 %collective-permute-start.3 = (f32[16,2048]{1,0:T(8,128)S(1)}, f32[16,2048]{1,0:T(8,128)S(1)}, u32[]{:S(2)}, u32[]{:S(2)}) collective-permute-start(f32[16,2048]{1,0:T(8,128)S(1)} %interior.1.refs_0_), channel_id=1, source_target_pairs={{0,2},{1,3},{2,0},{3,1},{4,6},{5,7},{6,4},{7,5},{8,10},{9,11},{10,... | collective-permute-start | bytes 393224 | tf_op jit(solution)/shard_map/ppermute | solution.py:553
  13.5 2.6 %edges.1 = (f32[16,512]{1,0:T(8,128)S(1)}, f32[16,512]{1,0:T(8,128)S(1)}, f32[16,512]{1,0:T(8,128)S(1)}, f32[16,512]{1,0:T(8,128)S(1)}) custom-call(f32[2,24,8,256]{3,2,1,0:T(8,128)S(1)} %get-tuple-element.19.winds, f32[24,8,256]{2,1,0:T(8,128)S(1)} %get-tuple-element.20.obs, f32[12,8,256]{2,1,0:T(8,128)S(1)} %collective-permute-done.from_low, ...), custom_call_target="tpu_custom_call" | custom-call | flops 100000000 | bytes 4000000 | tf_op jit(solution)/shard_map/edges/pallas_call | solution.py:599
  16.1 0.1 collective-permute-start.5
  16.2 4.7 %collective-permute-start.6 = (f32[16,512]{1,0:T(8,128)S(1)}, f32[16,512]{1,0:T(8,128)S(1)}, u32[]{:S(2)}, u32[]{:S(2)}) collective-permute-start(f32[16,512]{1,0:T(8,128)S(1)} %get-tuple-element.30), channel_id=1, source_target_pairs={{0,28},{4,0},{8,4},{12,8},{16,12},{20,16},{24,20},{28,24},{1,29},{... | collective-permute-start | bytes 98312 | tf_op jit(solution)/shard_map/ppermute | solution.py:615
  20.9 0.0 collective-permute-start.2
  20.9 1.9 %collective-permute-done.5 = f32[16,512]{1,0:T(8,128)S(1)} collective-permute-done((f32[16,512]{1,0:T(8,128)S(1)}, f32[16,512]{1,0:T(8,128)S(1)}, u32[]{:S(2)}, u32[]{:S(2)}) %collective-permute-start.5) | collective-permute-done | bytes 32800 | tf_op jit(solution)/shard_map/ppermute | solution.py:614
  22.8 0.0 collective-permute-done.6
  22.8 0.0 collective-permute-done.3.refs_2_
  22.8 0.1 collective-permute-start.4
  22.9 0.4 collective-permute-start.8
  23.3 0.2 collective-permute-start.7
  23.5 3.9 %collective-permute-done.8.refs_2_ = f32[16,1024]{1,0:T(8,128)S(1)} collective-permute-done((f32[16,1024]{1,0:T(8,128)S(1)}, f32[16,1024]{1,0:T(8,128)S(1)}, u32[]{:S(2)}, u32[]{:S(2)}) %collective-permute-start.8) | collective-permute-done | bytes 65568 | tf_op jit(solution)/shard_map/ppermute | solution.py:553
  27.4 0.0 collective-permute-start.9
  27.4 0.0 collective-permute-done.2.refs_1_
  27.4 0.0 collective-permute-done.4.refs_3_
  27.4 0.6 %inner_gram.1 = (f32[64,2048]{1,0:T(8,128)S(1)}, f32[64,64]{1,0:T(8,128)S(1)}) custom-call(s32[1]{0:T(128)} %bitcast.where, f32[16,2048]{1,0:T(8,128)S(1)} %interior.1.refs_0_, f32[16,2048]{1,0:T(8,128)S(1)} %collective-permute-done.2.refs_1_, f32[16,2048]{1,0:T(8,128)S(1)} %collective-permute-done.3.refs_2_, f32[16,2048]{1,0:T(8,128)S(1)} %collective-permute-done.4.refs_3_), custom_call_target="tpu_custom_call" | custom-call | flops 25000000 | bytes 4000000 | tf_op jit(solution)/shard_map/inner_gram/pallas_call | solution.py:617
  28.0 0.0 collective-permute-done.7.refs_1_
  28.0 0.6 %collective-permute-done.9.refs_3_ = f32[16,1024]{1,0:T(8,128)S(1)} collective-permute-done((f32[16,1024]{1,0:T(8,128)S(1)}, f32[16,1024]{1,0:T(8,128)S(1)}, u32[]{:S(2)}, u32[]{:S(2)}) %collective-permute-start.9) | collective-permute-done | bytes 65568 | tf_op jit(solution)/shard_map/ppermute | solution.py:553
  28.7 0.4 gram.1
  29.1 13.1 %all_to_all.5.grams = f32[8,32,128]{2,1,0:T(8,128)S(1)} all-to-all(f32[8,32,128]{2,1,0:T(8,128)S(1)} %get-tuple-element.31), channel_id=1, replica_groups=mesh['lon'=8,'probe'=4] {'lon'}, dimensions={0} | all-to-all | bytes 262144 | tf_op jit(solution)/shard_map/all_to_all | solution.py:633
  42.2 3.1 %factor.1 = (f32[6,16,512]{2,1,0:T(8,128)}, f32[64,64]{1,0:T(8,128)}) custom-call(s32[1]{0:T(128)} %bitcast.where, f32[8,32,128]{2,1,0:T(8,128)S(1)} %all_to_all.5.grams, f32[64,2048]{1,0:T(8,128)S(1)} %get-tuple-element.32.inner, f32[64,1024]{1,0:T(8,128)S(1)} %get-tuple-element.33.edge), custom_call_target="tpu_custom_call" | custom-call | flops 10000000 | bytes 4000000 | tf_op jit(solution)/shard_map/factor/pallas_call | solution.py:634
  (3 shorter events, 0.0 us)
Async XLA Ops:
  1.7 10.0 %collective-permute-start = (f32[12,8,256]{2,1,0:T(8,128)S(1)}, f32[12,8,256]{2,1,0:T(8,128)S(1)}, u32[]{:S(2)}, u32[]{:S(2)}) collective-permute-start(f32[12,8,256]{2,1,0:T(8,128)S(1)} %get-tuple-element.21), channel_id=1, source_target_pairs={{0,4},{4,8},{8,12},{12,16},{16,20},{20,24},{24,28},{28,0},{1,5},{5... | collective-permute-start | bytes 294920 | tf_op jit(solution)/shard_map/ppermute | solution.py:581
  4.7 7.0 %collective-permute-start.1 = (f32[10,8,256]{2,1,0:T(8,128)S(1)}, f32[10,8,256]{2,1,0:T(8,128)S(1)}, u32[]{:S(2)}, u32[]{:S(2)}) collective-permute-start(f32[10,8,256]{2,1,0:T(8,128)S(1)} %get-tuple-element.22), channel_id=1, source_target_pairs={{0,28},{4,0},{8,4},{12,8},{16,12},{20,16},{24,20},{28,24},{1,29},{... | collective-permute-start | bytes 245768 | tf_op jit(solution)/shard_map/ppermute | solution.py:582
  11.8 11.0 %collective-permute-start.3 = (f32[16,2048]{1,0:T(8,128)S(1)}, f32[16,2048]{1,0:T(8,128)S(1)}, u32[]{:S(2)}, u32[]{:S(2)}) collective-permute-start(f32[16,2048]{1,0:T(8,128)S(1)} %interior.1.refs_0_), channel_id=1, source_target_pairs={{0,2},{1,3},{2,0},{3,1},{4,6},{5,7},{6,4},{7,5},{8,10},{9,11},{10,... | collective-permute-start | bytes 393224 | tf_op jit(solution)/shard_map/ppermute | solution.py:553
  16.1 6.7 %collective-permute-start.5 = (f32[16,512]{1,0:T(8,128)S(1)}, f32[16,512]{1,0:T(8,128)S(1)}, u32[]{:S(2)}, u32[]{:S(2)}) collective-permute-start(f32[16,512]{1,0:T(8,128)S(1)} %get-tuple-element.28), channel_id=1, source_target_pairs={{0,4},{4,8},{8,12},{12,16},{16,20},{20,24},{24,28},{28,0},{1,5},{5... | collective-permute-start | bytes 98312 | tf_op jit(solution)/shard_map/ppermute | solution.py:614
  16.2 6.6 %collective-permute-start.6 = (f32[16,512]{1,0:T(8,128)S(1)}, f32[16,512]{1,0:T(8,128)S(1)}, u32[]{:S(2)}, u32[]{:S(2)}) collective-permute-start(f32[16,512]{1,0:T(8,128)S(1)} %get-tuple-element.30), channel_id=1, source_target_pairs={{0,28},{4,0},{8,4},{12,8},{16,12},{20,16},{24,20},{28,24},{1,29},{... | collective-permute-start | bytes 98312 | tf_op jit(solution)/shard_map/ppermute | solution.py:615
  20.9 6.5 %collective-permute-start.2 = (f32[16,2048]{1,0:T(8,128)S(1)}, f32[16,2048]{1,0:T(8,128)S(1)}, u32[]{:S(2)}, u32[]{:S(2)}) collective-permute-start(f32[16,2048]{1,0:T(8,128)S(1)} %interior.1.refs_0_), channel_id=1, source_target_pairs={{0,1},{1,0},{2,3},{3,2},{4,5},{5,4},{6,7},{7,6},{8,9},{9,8},{10,11... | collective-permute-start | bytes 393224 | tf_op jit(solution)/shard_map/ppermute | solution.py:553
  22.8 4.6 %collective-permute-start.4 = (f32[16,2048]{1,0:T(8,128)S(1)}, f32[16,2048]{1,0:T(8,128)S(1)}, u32[]{:S(2)}, u32[]{:S(2)}) collective-permute-start(f32[16,2048]{1,0:T(8,128)S(1)} %collective-permute-done.3.refs_2_), channel_id=1, source_target_pairs={{0,1},{1,0},{2,3},{3,2},{4,5},{5,4},{6,7},{7,6},{8,9},{9,8},{10,11... | collective-permute-start | bytes 393224 | tf_op jit(solution)/shard_map/ppermute | solution.py:553
  22.9 4.5 %collective-permute-start.8 = (f32[16,1024]{1,0:T(8,128)S(1)}, f32[16,1024]{1,0:T(8,128)S(1)}, u32[]{:S(2)}, u32[]{:S(2)}) collective-permute-start(f32[16,1024]{1,0:T(8,128)S(1)} %pad_maximum_fusion.refs_0_), channel_id=1, source_target_pairs={{0,2},{1,3},{2,0},{3,1},{4,6},{5,7},{6,4},{7,5},{8,10},{9,11},{10,... | collective-permute-start | bytes 196616 | tf_op jit(solution)/shard_map/ppermute | solution.py:553
  23.3 4.7 %collective-permute-start.7 = (f32[16,1024]{1,0:T(8,128)S(1)}, f32[16,1024]{1,0:T(8,128)S(1)}, u32[]{:S(2)}, u32[]{:S(2)}) collective-permute-start(f32[16,1024]{1,0:T(8,128)S(1)} %pad_maximum_fusion.refs_0_), channel_id=1, source_target_pairs={{0,1},{1,0},{2,3},{3,2},{4,5},{5,4},{6,7},{7,6},{8,9},{9,8},{10,11... | collective-permute-start | bytes 196616 | tf_op jit(solution)/shard_map/ppermute | solution.py:553
  27.4 1.3 %collective-permute-start.9 = (f32[16,1024]{1,0:T(8,128)S(1)}, f32[16,1024]{1,0:T(8,128)S(1)}, u32[]{:S(2)}, u32[]{:S(2)}) collective-permute-start(f32[16,1024]{1,0:T(8,128)S(1)} %collective-permute-done.8.refs_2_), channel_id=1, source_target_pairs={{0,1},{1,0},{2,3},{3,2},{4,5},{5,4},{6,7},{7,6},{8,9},{9,8},{10,11... | collective-permute-start | bytes 196616 | tf_op jit(solution)/shard_map/ppermute | solution.py:553

commit v4 on v3

--- a/solution.py
+++ b/solution.py
@@ -240,6 +240,15 @@
 GROUP = 8
 
 
+def weight_keys(first, last):
+    reach = {0: (-4, 7), 1: (-3, 6), 2: (-1, 4)}
+    return [
+        (r, part)
+        for part, (low, high) in reach.items()
+        for r in range(max(first, low), min(last, high) + 1)
+    ]
+
+
 def fetch_all(copies):
     for copy in copies:
         copy.start()
@@ -266,12 +275,20 @@
 
 
 def interior_kernel(
-    winds, obs, field_hbm, out, coef, weights, sums, field, sem
+    winds, obs, field_hbm, out, part_low, part_high, sides, coef, weights, sums, field, sems
 ):
     count, lons = field.shape[0], field.shape[1]
-    blocks = lons // 4 - 2
-    field_copy = pltpu.make_async_copy(field_hbm, field, sem)
+    blocks = lons // 4
+    field_copy = pltpu.make_async_copy(field_hbm, field, sems.at[0])
     field_copy.start()
+    side_copies = [
+        pltpu.make_async_copy(
+            field_hbm.at[:, pl.ds(start, 4)], sides.at[:, pl.ds(4 * n, 4)], sems.at[1 + n]
+        )
+        for n, start in enumerate((0, lons - 4))
+    ]
+    for copy in side_copies:
+        copy.start()
     lanes = Lanes()
 
     def coefficients(lon, carry):
@@ -287,25 +304,24 @@
 
     lax.fori_loop(0, lons, coefficients, 0, unroll=4)
 
-    def weigh(block, carry):
-        base = (block + 1) * 4
+    def weigh(first, last, block, carry):
+        base = block * 4
 
         def get(plane, r):
             return halves(coef, plane, base + r)
 
-        result = block_weights(lanes, get, lambda r: halves(obs, base + r), -4, 7)
+        result = block_weights(lanes, get, lambda r: halves(obs, base + r), first, last)
         for (r, part), value in result.items():
             store(weights, value, block, part, r + 4)
         return carry
 
-    lax.fori_loop(0, blocks, weigh, 0)
+    spans = ((0, 1, 2, 7), (1, blocks - 1, -4, 7), (blocks - 1, blocks, -4, -1))
+    for start, stop, first, last in spans:
+        lax.fori_loop(start, stop, functools.partial(weigh, first, last), 0)
     field_copy.wait()
-    keys = [(r, 0) for r in range(-4, 8)]
-    keys += [(r, 1) for r in range(-3, 7)]
-    keys += [(r, 2) for r in range(-1, 5)]
     groups = count // GROUP
 
-    def sweep(step, carry):
+    def sweep(first, last, step, carry):
         block = step // groups
         start = (step % groups) * GROUP
 
@@ -315,44 +331,34 @@
 
         apply_weights(
             lanes,
-            keys,
+            weight_keys(first, last),
             lambda r, part: halves(weights, block, part, r + 4),
-            lambda probe, r: halves(field, probe, block * 4 + 4 + r),
+            lambda probe, r: halves(field, probe, block * 4 + r),
             write,
             [start + n for n in range(GROUP)],
         )
         return carry
 
-    lax.fori_loop(0, blocks * groups, sweep, 0)
+    for start, stop, first, last in spans:
+        lax.fori_loop(start * groups, stop * groups, functools.partial(sweep, first, last), 0)
 
     def put(n, pair, value):
-        column = (n * 4 + pair) * HALF
-        out[:, column : column + HALF] = value
+        if n == 0:
+            part_low[:, pair * HALF : (pair + 1) * HALF] = value
+        elif n == blocks - 1:
+            part_high[:, pair * HALF : (pair + 1) * HALF] = value
+        else:
+            column = ((n - 1) * 4 + pair) * HALF
+            out[:, column : column + HALF] = value
 
     pool_into(lanes, sums, blocks, count, put)
-
-
-def edge_kernel(
-    winds, obs, from_low, from_high, field_hbm,
-    to_low, own_low, own_high, to_high,
-    coef, weights, sums, field, sems,
-):
-    count, lons = field_hbm.shape[0], field_hbm.shape[1]
-    def fetch(side):
-        return pltpu.make_async_copy(
-            field_hbm.at[:, pl.ds(side * (lons - 8), 8)],
-            field.at[:, pl.ds(8 * side, 8)],
-            sems.at[side],
-        )
-
-    @pl.loop(0, 2)
-    def _(side):
-        fetch(side).start()
-
+    for copy in side_copies:
+        copy.wait()
+
+
+def edge_sums(winds, obs, from_low, from_high, field, coef, weights, sums, spans, jobs, put):
+    count, lons = field.shape[0], obs.shape[0]
     lanes = Lanes()
-
-    def near(lon):
-        return lon if lon < 8 else lon - (lons - 16)
 
     def wind(which, lon):
         if lon < 0:
@@ -369,19 +375,12 @@
         return halves(obs, lon)
 
     slots = {}
-    for lon in list(range(-3, 8)) + list(range(lons - 8, lons + 4)):
-        slots[lon] = len(slots)
-        last = lon in (7, lons + 3)
-        write_coefficients(
-            coef, slots[lon], wind(0, lon), wind(0, lon if last else lon + 1), wind(1, lon), lanes
-        )
-    jobs = (
-        (-4, 4, 7),
-        (0, 0, 7),
-        (lons - 4, -4, 3),
-        (lons, -4, -1),
-    )
-    kept = []
+    for start, stop in spans:
+        for lon in range(start, stop + 1):
+            slots[lon] = len(slots)
+            write_coefficients(
+                coef, slots[lon], wind(0, lon), wind(0, min(lon + 1, stop)), wind(1, lon), lanes
+            )
     for n, (base, first, last) in enumerate(jobs):
         result = block_weights(
             lanes,
@@ -392,35 +391,62 @@
         )
         for (r, part), value in result.items():
             store(weights, value, n, part, r + 4)
-        kept.append(set(result))
-
-    @pl.loop(0, 2)
-    def _(side):
-        fetch(side).wait()
-
-    def sweep(n, base, step, carry):
-        def write(probe, part, h, value):
-            row = pl.multiple_of((n * count + probe) * 8, 8)
-            sums[2 * part + h, pl.ds(row, 8), :] = value
-
-        apply_weights(
-            lanes,
-            kept[n],
-            lambda r, part: halves(weights, n, part, r + 4),
-            lambda probe, r: halves(field, probe, near(base + r)),
-            write,
-            [step * GROUP + k for k in range(GROUP)],
-        )
+
+    def sweep(step, carry):
+        for n, (base, first, last) in enumerate(jobs):
+
+            def write(probe, part, h, value):
+                row = pl.multiple_of((n * count + probe) * 8, 8)
+                sums[2 * part + h, pl.ds(row, 8), :] = value
+
+            def read(probe, r):
+                lon = base + r
+                return halves(field, probe, lon if lon < 4 else lon - (lons - 8))
+
+            apply_weights(
+                lanes,
+                weight_keys(first, last),
+                lambda r, part: halves(weights, n, part, r + 4),
+                read,
+                write,
+                [step * GROUP + k for k in range(GROUP)],
+            )
         return carry
 
-    for n, (base, _, _) in enumerate(jobs):
-        lax.fori_loop(0, count // GROUP, functools.partial(sweep, n, base), 0)
-    outs = (to_low, own_low, own_high, to_high)
+    lax.fori_loop(0, count // GROUP, sweep, 0)
+    pool_into(lanes, sums, len(jobs), count, put)
+
+
+def share_kernel(winds, obs, from_low, from_high, field, to_low, to_high, coef, weights, sums):
+    lons = obs.shape[0]
 
     def put(n, pair, value):
-        outs[n][:, pair * HALF : (pair + 1) * HALF] = value
-
-    pool_into(lanes, sums, 4, count, put)
+        (to_low, to_high)[n][:, pair * HALF : (pair + 1) * HALF] = value
+
+    edge_sums(
+        winds, obs, from_low, from_high, field, coef, weights, sums,
+        ((-3, 3), (lons - 3, lons + 3)),
+        ((-4, 4, 7), (lons, -4, -1)),
+        put,
+    )
+
+
+def rest_kernel(
+    winds, obs, from_low, from_high, field, part_low, part_high, after,
+    own_low, own_high, coef, weights, sums,
+):
+    lons = obs.shape[0]
+
+    def put(n, pair, value):
+        columns = slice(pair * HALF, (pair + 1) * HALF)
+        (own_low, own_high)[n][:, columns] = value + (part_low, part_high)[n][:, columns]
+
+    edge_sums(
+        winds, obs, from_low, from_high, field, coef, weights, sums,
+        ((-2, 4), (lons - 5, lons + 1)),
+        ((0, 0, 1), (lons - 4, 0, 3)),
+        put,
+    )
 
 
 def self_product(panel):
@@ -525,14 +551,16 @@
 VMEM = pl.BlockSpec(memory_space=pltpu.VMEM)
 SMEM = pl.BlockSpec(memory_space=pltpu.SMEM)
 HBM = pl.BlockSpec(memory_space=pltpu.HBM)
+ANY = pl.BlockSpec(memory_space=pl.ANY)
 MIB = 1024 * 1024
+COST = 1_000_000
 
 
 def shape(*dims):
     return jax.ShapeDtypeStruct(dims, F32)
 
 
-def call(kernel, name, out_shape, in_specs, scratch=(), flops=0):
+def call(kernel, name, out_shape, in_specs, scratch=(), flops=1_000_000):
     return pl.pallas_call(
         kernel,
         out_shape=out_shape,
@@ -540,18 +568,13 @@
         out_specs=jax.tree.map(lambda _: VMEM, out_shape),
         scratch_shapes=scratch,
         compiler_params=pltpu.CompilerParams(vmem_limit_bytes=32 * MIB),
-        cost_estimate=pl.CostEstimate(flops=flops, bytes_accessed=4_000_000, transcendentals=0),
+        cost_estimate=pl.CostEstimate(flops=flops, bytes_accessed=100_000, transcendentals=0),
         name=name,
     )
 
 
-def gather_pieces(rows):
-    size = lax.axis_size("probe")
-    pieces = [rows]
-    for k in range(1, size):
-        source, step = (pieces[k - 1], 1) if k > 1 and k & 1 else (rows, k)
-        pieces.append(lax.ppermute(source, "probe", [(i, i ^ step) for i in range(size)]))
-    return pieces
+def swap_probes(value, step):
+    return lax.ppermute(value, "probe", [(i, i ^ step) for i in range(lax.axis_size("probe"))])
 
 
 def body(increments, winds, obs_weight):
@@ -580,47 +603,53 @@
     )(winds, obs_weight)
     from_low = lax.ppermute(pack_up, "lon", up)
     from_high = lax.ppermute(pack_down, "lon", down)
-    inner = call(
+    inner, part_low, part_high, sides = call(
         interior_kernel,
         "interior",
-        shape(count, (blocks - 2) * 512),
+        (
+            shape(count, (blocks - 2) * 512),
+            shape(count, 512),
+            shape(count, 512),
+            shape(count, 8, levels, lats),
+        ),
         [VMEM, VMEM, HBM],
         [
             pltpu.VMEM((PLANES, lons, levels, lats), F32),
-            pltpu.VMEM((blocks - 2, 3, 12, levels, lats), F32),
-            pltpu.VMEM((6, (blocks - 2) * count * 8, HALF), F32),
+            pltpu.VMEM((blocks, 3, 12, levels, lats), F32),
+            pltpu.VMEM((6, blocks * count * 8, HALF), F32),
             pltpu.VMEM((count, lons, levels, lats), F32),
-            dma,
+            dma((3,)),
         ],
-        200_000_000,
+        COST,
     )(winds, obs_weight, increments)
-    inner, from_low, from_high = lax.optimization_barrier((inner, from_low, from_high))
-    inner_pieces = gather_pieces(inner)
-    edges = call(
-        edge_kernel,
-        "edges",
-        (shape(count, 512),) * 4,
-        [VMEM, VMEM, VMEM, VMEM, HBM],
-        [
-            pltpu.VMEM((PLANES, 23, levels, lats), F32),
-            pltpu.VMEM((4, 3, 12, levels, lats), F32),
-            pltpu.VMEM((6, 4 * count * 8, HALF), F32),
-            pltpu.VMEM((count, 16, levels, lats), F32),
-            dma((2,)),
-        ],
-        100_000_000,
-    )(winds, obs_weight, from_low, from_high, increments)
-    to_low, own_low, own_high, to_high = edges
-    own_low = own_low + lax.ppermute(to_high, "lon", up)
-    own_high = own_high + lax.ppermute(to_low, "lon", down)
-    edge_pieces = gather_pieces(jnp.concatenate([own_low, own_high], axis=1))
+    edge_scratch = [
+        pltpu.VMEM((PLANES, 14, levels, lats), F32),
+        pltpu.VMEM((2, 3, 12, levels, lats), F32),
+        pltpu.VMEM((6, 2 * count * 8, HALF), F32),
+    ]
+    to_low, to_high = call(
+        share_kernel, "share", (shape(count, 512),) * 2, [VMEM] * 5, edge_scratch
+    )(winds, obs_weight, from_low, from_high, sides)
+    own_low, own_high = call(
+        rest_kernel, "rest", (shape(count, 512),) * 2, [VMEM] * 7 + [ANY], edge_scratch
+    )(winds, obs_weight, from_low, from_high, sides, part_low, part_high, to_low)
+    from_below = lax.ppermute(to_high, "lon", up)
+    from_above = lax.ppermute(to_low, "lon", down)
+    inner, own_low = lax.optimization_barrier((inner, own_low))
+    size = lax.axis_size("probe")
+    inner_pieces = [inner] + [swap_probes(inner, k) for k in range(1, size) if k & (k - 1) == 0]
+    edge = jnp.concatenate([own_low + from_below, own_high + from_above], axis=1)
+    edge_pieces = [edge] + [swap_probes(edge, k) for k in range(1, size) if k & (k - 1) == 0]
+    inner_pieces, edge_pieces = lax.optimization_barrier((inner_pieces, edge_pieces))
+    inner_pieces.append(swap_probes(inner_pieces[2], 1))
+    edge_pieces.append(swap_probes(edge_pieces[2], 1))
     inner_panel, inner_gram = call(
         inner_gram_kernel,
         "inner_gram",
         (shape(probes, inner.shape[1]), shape(probes, probes)),
         [SMEM] + [VMEM] * len(inner_pieces),
         (),
-        25_000_000,
+        COST,
     )(where, *inner_pieces)
     edge_panel, grams = call(
         gram_kernel,
@@ -628,7 +657,7 @@
         (shape(probes, 1024), shape(ring, probes // 2, 2 * probes)),
         [SMEM, VMEM] + [VMEM] * len(edge_pieces),
         (),
-        10_000_000,
+        COST,
     )(where, inner_gram, *edge_pieces)
     grams = lax.all_to_all(grams, "lon", 0, 0, tiled=True)
     basis, upper = call(
@@ -637,7 +666,7 @@
         (shape(blocks, count, 512), shape(probes, probes)),
         [SMEM, VMEM, VMEM, VMEM],
         [pltpu.VMEM((probes, probes), F32)],
-        10_000_000,
+        COST,
     )(where, grams, inner_panel, edge_panel)
     return basis.transpose(1, 0, 2), upper
 

time: 45.6 us -> 44 us (0.965)
  blocking collectives: 13.1 us -> 11.2 us
  waiting for transfers between devices: 6.42 us -> 5.61 us
  starting transfers between devices: 13.3 us -> 14 us
  Pallas kernels: 11.8 us -> 12.4 us
    all_to_all x1, blocking collectives: 13.1 us -> 11.2 us  [body(): grams = lax.all_to_all(grams, 'lon', 0, 0, tiled=True)]
    ppermute x8, waiting for transfers between devices: 6.41 us -> 5.6 us  [the longest x6 5.59 us: swap_probes(): lax.ppermute(value, 'probe', [(i, i ^ step) for i in range(lax.axis_size(...]
    ppermute x8, starting transfers between devices: 7.16 us -> 7.86 us  [the longest x1 4.71 us: body(): from_above = lax.ppermute(to_low, 'lon', down)]
    pallas_call x2 -> x3, Pallas kernels: 6.54 us -> 7.1 us  [the longest x1 5.05 us: body(): call(interior_kernel, 'interior', (shape(count, (blocks - 2) * 512), shap...]
  transfers between devices with their start and end apart: 10 -> 10, of which waited for: 3 -> 3; matrix products, arithmetic and copies ran while one was open for 0% -> 0% of each run, Pallas kernels for 16% -> 15%
where the time goes in v4:
time: 44 us; the launch traced here: 43.9 us
  starting transfers between devices  14 us (32%)
  Pallas kernels  12.4 us (28%)
  blocking collectives  11.2 us (25%)
  waiting for transfers between devices  5.61 us (13%)
  between operations  0.75 us (2%)
    all_to_all x1, blocking collectives, body(): grams = lax.all_to_all(grams, 'lon', 0, 0, tiled=True)  11.2 us
    ppermute x6, waiting for transfers between devices, swap_probes(): lax.ppermute(value, 'probe', [(i, i ^ step) for i in range(lax.axis_size(...  5.59 us
    pallas_call x1, Pallas kernels, body(): call(interior_kernel, 'interior', (shape(count, (blocks - 2) * 512), shap...  5.05 us
    ppermute x1, starting transfers between devices, body(): from_above = lax.ppermute(to_low, 'lon', down)  4.71 us
    pallas_call x1, Pallas kernels, body(): call(factor_kernel, 'factor', (shape(blocks, count, 512), shape(probes, p...  3.14 us
    ppermute x1, starting transfers between devices, body(): from_high = lax.ppermute(pack_down, 'lon', down)  3.1 us
    ppermute x6, starting transfers between devices, swap_probes(): lax.ppermute(value, 'probe', [(i, i ^ step) for i in range(lax.axis_size(...  3.09 us
    ppermute x1, starting transfers between devices, body(): from_low = lax.ppermute(pack_up, 'lon', up)  2.99 us
  transfers between devices with their start and end apart: 10, of which 3 were waited for; matrix products, arithmetic and copies ran while one was open for 0% of the time, Pallas kernels for 15%

profile of v4, /device:TPU:0, one launch (start us, length us, event | category | flops | bytes accessed | tf_op | source)
XLA Modules:
  0.0 43.9 jit_solution(7214751417489229305)
XLA Ops:
  0.6 1.1 %pack.1 = (f32[12,8,256]{2,1,0:T(8,128)S(1)}, f32[10,8,256]{2,1,0:T(8,128)S(1)}, f32[2,24,8,256]{3,2,1,0:T(8,128)S(1)}, f32[24,8,256]{2,1,0:T(8,128)S(1)}) custom-call(f32[2,24,8,256]{3,2,1,0:T(8,128)} %winds_hbm.1, f32[24,8,256]{2,1,0:T(8,128)} %obs_hbm.1), custom_call_target="tpu_custom_call" | custom-call | flops 1000000 | bytes 100000 | tf_op jit(solution)/shard_map/pack/pallas_call | solution.py:592
  1.7 3.0 %collective-permute-start = (f32[12,8,256]{2,1,0:T(8,128)S(1)}, f32[12,8,256]{2,1,0:T(8,128)S(1)}, u32[]{:S(2)}, u32[]{:S(2)}) collective-permute-start(f32[12,8,256]{2,1,0:T(8,128)S(1)} %get-tuple-element.31), channel_id=1, source_target_pairs={{0,4},{4,8},{8,12},{12,16},{16,20},{20,24},{24,28},{28,0},{1,5},{5... | collective-permute-start | bytes 294920 | tf_op jit(solution)/shard_map/ppermute | solution.py:604
  4.7 3.1 %collective-permute-start.1 = (f32[10,8,256]{2,1,0:T(8,128)S(1)}, f32[10,8,256]{2,1,0:T(8,128)S(1)}, u32[]{:S(2)}, u32[]{:S(2)}) collective-permute-start(f32[10,8,256]{2,1,0:T(8,128)S(1)} %get-tuple-element.32), channel_id=1, source_target_pairs={{0,28},{4,0},{8,4},{12,8},{16,12},{20,16},{24,20},{28,24},{1,29},{... | collective-permute-start | bytes 245768 | tf_op jit(solution)/shard_map/ppermute | solution.py:605
  7.8 5.1 %interior.1 = (f32[16,2048]{1,0:T(8,128)S(1)}, f32[16,512]{1,0:T(8,128)S(1)}, f32[16,512]{1,0:T(8,128)S(1)}, f32[16,8,8,256]{3,2,1,0:T(8,128)S(1)}) custom-call(f32[2,24,8,256]{3,2,1,0:T(8,128)S(1)} %get-tuple-element.28.winds, f32[24,8,256]{2,1,0:T(8,128)S(1)} %get-tuple-element.29.obs, f32[16,24,8,256]{3,2,1,0:T(8,128)} %field_hbm.1), custom_call_target="tpu_custom_call" | custom-call | flops 1000000 | bytes 100000 | tf_op jit(solution)/shard_map/interior/pallas_call | solution.py:606
  12.9 0.0 collective-permute-done.1.from_high
  12.9 0.0 collective-permute-done.from_low
  12.9 1.0 %share.1 = (f32[16,512]{1,0:T(8,128)S(1)}, f32[16,512]{1,0:T(8,128)S(1)}) custom-call(f32[2,24,8,256]{3,2,1,0:T(8,128)S(1)} %get-tuple-element.28.winds, f32[24,8,256]{2,1,0:T(8,128)S(1)} %get-tuple-element.29.obs, f32[12,8,256]{2,1,0:T(8,128)S(1)} %collective-permute-done.from_low, f32[10,8,256]{2,1,0:T(8,128)S(1)} %collective-permute-done.1.from_high, ...), custom_call_target="tpu_custom_call" | custom-call | flops 1000000 | bytes 100000 | tf_op jit(solution)/shard_map/share/pallas_call | solution.py:630
  13.9 0.1 collective-permute-start.4
  13.9 4.7 %collective-permute-start.5 = (f32[16,512]{1,0:T(8,128)S(1)}, f32[16,512]{1,0:T(8,128)S(1)}, u32[]{:S(2)}, u32[]{:S(2)}) collective-permute-start(f32[16,512]{1,0:T(8,128)S(1)} %get-tuple-element.36.after), channel_id=1, source_target_pairs={{0,28},{4,0},{8,4},{12,8},{16,12},{20,16},{24,20},{28,24},{1,29},{... | collective-permute-start | bytes 98312 | tf_op jit(solution)/shard_map/ppermute | solution.py:637
  18.6 1.1 %rest.1 = (f32[16,512]{1,0:T(8,128)S(1)}, f32[16,512]{1,0:T(8,128)S(1)}) custom-call(f32[2,24,8,256]{3,2,1,0:T(8,128)S(1)} %get-tuple-element.28.winds, f32[24,8,256]{2,1,0:T(8,128)S(1)} %get-tuple-element.29.obs, f32[12,8,256]{2,1,0:T(8,128)S(1)} %collective-permute-done.from_low, f32[10,8,256]{2,1,0:T(8,128)S(1)} %collective-permute-done.1.from_high, ...), custom_call_target="tpu_custom_call" | custom-call | flops 1000000 | bytes 100000 | tf_op jit(solution)/shard_map/rest/pallas_call | solution.py:633
  19.7 0.1 collective-permute-start.2
  19.8 1.7 %collective-permute-start.3 = (f32[16,2048]{1,0:T(8,128)S(1)}, f32[16,2048]{1,0:T(8,128)S(1)}, u32[]{:S(2)}, u32[]{:S(2)}) collective-permute-start(f32[16,2048]{1,0:T(8,128)S(1)} %get-tuple-element.42.refs_0_), channel_id=1, source_target_pairs={{0,2},{1,3},{2,0},{3,1},{4,6},{5,7},{6,4},{7,5},{8,10},{9,11},{10,... | collective-permute-start | bytes 393224 | tf_op jit(solution)/shard_map/ppermute | solution.py:577
  21.5 0.0 collective-permute-done.4
  21.5 0.0 collective-permute-done.5
  21.6 0.2 collective-permute-start.6
  21.8 0.6 %collective-permute-start.7 = (f32[16,1024]{1,0:T(8,128)S(1)}, f32[16,1024]{1,0:T(8,128)S(1)}, u32[]{:S(2)}, u32[]{:S(2)}) collective-permute-start(f32[16,1024]{1,0:T(8,128)S(1)} %pad_maximum_fusion.refs_0_), channel_id=1, source_target_pairs={{0,2},{1,3},{2,0},{3,1},{4,6},{5,7},{6,4},{7,5},{8,10},{9,11},{10,... | collective-permute-start | bytes 196616 | tf_op jit(solution)/shard_map/ppermute | solution.py:577
  22.4 0.5 %collective-permute-done.6.refs_1_ = f32[16,1024]{1,0:T(8,128)S(1)} collective-permute-done((f32[16,1024]{1,0:T(8,128)S(1)}, f32[16,1024]{1,0:T(8,128)S(1)}, u32[]{:S(2)}, u32[]{:S(2)}) %collective-permute-start.6) | collective-permute-done | bytes 65568 | tf_op jit(solution)/shard_map/ppermute | solution.py:577
  22.9 4.2 %collective-permute-done.7.refs_2_ = f32[16,1024]{1,0:T(8,128)S(1)} collective-permute-done((f32[16,1024]{1,0:T(8,128)S(1)}, f32[16,1024]{1,0:T(8,128)S(1)}, u32[]{:S(2)}, u32[]{:S(2)}) %collective-permute-start.7) | collective-permute-done | bytes 65568 | tf_op jit(solution)/shard_map/ppermute | solution.py:577
  27.1 0.0 collective-permute-done.2.refs_1_
  27.1 0.0 collective-permute-done.3.refs_2_
  27.1 0.0 collective-permute-start.8
  27.1 0.5 %collective-permute-start.9 = (f32[16,1024]{1,0:T(8,128)S(1)}, f32[16,1024]{1,0:T(8,128)S(1)}, u32[]{:S(2)}, u32[]{:S(2)}) collective-permute-start(f32[16,1024]{1,0:T(8,128)S(1)} %collective-permute-done.7.refs_2_), channel_id=1, source_target_pairs={{0,1},{1,0},{2,3},{3,2},{4,5},{5,4},{6,7},{7,6},{8,9},{9,8},{10,11... | collective-permute-start | bytes 196616 | tf_op jit(solution)/shard_map/ppermute | solution.py:577
  27.6 0.8 %collective-permute-done.8.refs_3_ = f32[16,2048]{1,0:T(8,128)S(1)} collective-permute-done((f32[16,2048]{1,0:T(8,128)S(1)}, f32[16,2048]{1,0:T(8,128)S(1)}, u32[]{:S(2)}, u32[]{:S(2)}) %collective-permute-start.8) | collective-permute-done | bytes 131104 | tf_op jit(solution)/shard_map/ppermute | solution.py:577
  28.5 0.6 %inner_gram.1 = (f32[64,2048]{1,0:T(8,128)S(1)}, f32[64,64]{1,0:T(8,128)S(1)}) custom-call(s32[1]{0:T(128)} %bitcast.where, f32[16,2048]{1,0:T(8,128)S(1)} %get-tuple-element.42.refs_0_, f32[16,2048]{1,0:T(8,128)S(1)} %collective-permute-done.2.refs_1_, f32[16,2048]{1,0:T(8,128)S(1)} %collective-permute-done.3.refs_2_, ...), custom_call_target="tpu_custom_call" | custom-call | flops 1000000 | bytes 100000 | tf_op jit(solution)/shard_map/inner_gram/pallas_call | solution.py:646
  29.1 0.0 collective-permute-done.9.refs_3_
  29.1 0.5 %gram.1 = (f32[64,1024]{1,0:T(8,128)S(1)}, f32[8,32,128]{2,1,0:T(8,128)S(1)}) custom-call(s32[1]{0:T(128)} %bitcast.where, f32[64,64]{1,0:T(8,128)S(1)} %get-tuple-element.45.inner, f32[16,1024]{1,0:T(8,128)S(1)} %pad_maximum_fusion.refs_0_, f32[16,1024]{1,0:T(8,128)S(1)} %collective-permute-done.6.refs_1_, f32[16,1024]{1,0:T(8,128)S(1)} %collective-permute-done.7.refs_2_, ...), custom_call_target="tpu_custom_call" | custom-call | flops 1000000 | bytes 100000 | tf_op jit(solution)/shard_map/gram/pallas_call | solution.py:654
  29.6 11.2 %all_to_all.5.grams = f32[8,32,128]{2,1,0:T(8,128)S(1)} all-to-all(f32[8,32,128]{2,1,0:T(8,128)S(1)} %get-tuple-element.49), channel_id=1, replica_groups=mesh['lon'=8,'probe'=4] {'lon'}, dimensions={0} | all-to-all | bytes 262144 | tf_op jit(solution)/shard_map/all_to_all | solution.py:662
  40.7 3.1 %factor.1 = (f32[6,16,512]{2,1,0:T(8,128)}, f32[64,64]{1,0:T(8,128)}) custom-call(s32[1]{0:T(128)} %bitcast.where, f32[8,32,128]{2,1,0:T(8,128)S(1)} %all_to_all.5.grams, f32[64,2048]{1,0:T(8,128)S(1)} %get-tuple-element.50.inner, f32[64,1024]{1,0:T(8,128)S(1)} %get-tuple-element.51.edge), custom_call_target="tpu_custom_call" | custom-call | flops 1000000 | bytes 100000 | tf_op jit(solution)/shard_map/factor/pallas_call | solution.py:663
  (3 shorter events, 0.0 us)
Async XLA Ops:
  1.7 11.2 %collective-permute-start = (f32[12,8,256]{2,1,0:T(8,128)S(1)}, f32[12,8,256]{2,1,0:T(8,128)S(1)}, u32[]{:S(2)}, u32[]{:S(2)}) collective-permute-start(f32[12,8,256]{2,1,0:T(8,128)S(1)} %get-tuple-element.31), channel_id=1, source_target_pairs={{0,4},{4,8},{8,12},{12,16},{16,20},{20,24},{24,28},{28,0},{1,5},{5... | collective-permute-start | bytes 294920 | tf_op jit(solution)/shard_map/ppermute | solution.py:604
  4.7 8.2 %collective-permute-start.1 = (f32[10,8,256]{2,1,0:T(8,128)S(1)}, f32[10,8,256]{2,1,0:T(8,128)S(1)}, u32[]{:S(2)}, u32[]{:S(2)}) collective-permute-start(f32[10,8,256]{2,1,0:T(8,128)S(1)} %get-tuple-element.32), channel_id=1, source_target_pairs={{0,28},{4,0},{8,4},{12,8},{16,12},{20,16},{24,20},{28,24},{1,29},{... | collective-permute-start | bytes 245768 | tf_op jit(solution)/shard_map/ppermute | solution.py:605
  13.9 7.6 %collective-permute-start.4 = (f32[16,512]{1,0:T(8,128)S(1)}, f32[16,512]{1,0:T(8,128)S(1)}, u32[]{:S(2)}, u32[]{:S(2)}) collective-permute-start(f32[16,512]{1,0:T(8,128)S(1)} %get-tuple-element.40), channel_id=1, source_target_pairs={{0,4},{4,8},{8,12},{12,16},{16,20},{20,24},{24,28},{28,0},{1,5},{5... | collective-permute-start | bytes 98312 | tf_op jit(solution)/shard_map/ppermute | solution.py:636
  13.9 7.6 %collective-permute-start.5 = (f32[16,512]{1,0:T(8,128)S(1)}, f32[16,512]{1,0:T(8,128)S(1)}, u32[]{:S(2)}, u32[]{:S(2)}) collective-permute-start(f32[16,512]{1,0:T(8,128)S(1)} %get-tuple-element.36.after), channel_id=1, source_target_pairs={{0,28},{4,0},{8,4},{12,8},{16,12},{20,16},{24,20},{28,24},{1,29},{... | collective-permute-start | bytes 98312 | tf_op jit(solution)/shard_map/ppermute | solution.py:637
  19.7 7.4 %collective-permute-start.2 = (f32[16,2048]{1,0:T(8,128)S(1)}, f32[16,2048]{1,0:T(8,128)S(1)}, u32[]{:S(2)}, u32[]{:S(2)}) collective-permute-start(f32[16,2048]{1,0:T(8,128)S(1)} %get-tuple-element.42.refs_0_), channel_id=1, source_target_pairs={{0,1},{1,0},{2,3},{3,2},{4,5},{5,4},{6,7},{7,6},{8,9},{9,8},{10,11... | collective-permute-start | bytes 393224 | tf_op jit(solution)/shard_map/ppermute | solution.py:577
  19.8 7.3 %collective-permute-start.3 = (f32[16,2048]{1,0:T(8,128)S(1)}, f32[16,2048]{1,0:T(8,128)S(1)}, u32[]{:S(2)}, u32[]{:S(2)}) collective-permute-start(f32[16,2048]{1,0:T(8,128)S(1)} %get-tuple-element.42.refs_0_), channel_id=1, source_target_pairs={{0,2},{1,3},{2,0},{3,1},{4,6},{5,7},{6,4},{7,5},{8,10},{9,11},{10,... | collective-permute-start | bytes 393224 | tf_op jit(solution)/shard_map/ppermute | solution.py:577
  21.6 1.3 %collective-permute-start.6 = (f32[16,1024]{1,0:T(8,128)S(1)}, f32[16,1024]{1,0:T(8,128)S(1)}, u32[]{:S(2)}, u32[]{:S(2)}) collective-permute-start(f32[16,1024]{1,0:T(8,128)S(1)} %pad_maximum_fusion.refs_0_), channel_id=1, source_target_pairs={{0,1},{1,0},{2,3},{3,2},{4,5},{5,4},{6,7},{7,6},{8,9},{9,8},{10,11... | collective-permute-start | bytes 196616 | tf_op jit(solution)/shard_map/ppermute | solution.py:577
  21.8 5.3 %collective-permute-start.7 = (f32[16,1024]{1,0:T(8,128)S(1)}, f32[16,1024]{1,0:T(8,128)S(1)}, u32[]{:S(2)}, u32[]{:S(2)}) collective-permute-start(f32[16,1024]{1,0:T(8,128)S(1)} %pad_maximum_fusion.refs_0_), channel_id=1, source_target_pairs={{0,2},{1,3},{2,0},{3,1},{4,6},{5,7},{6,4},{7,5},{8,10},{9,11},{10,... | collective-permute-start | bytes 196616 | tf_op jit(solution)/shard_map/ppermute | solution.py:577
  27.1 1.4 %collective-permute-start.8 = (f32[16,2048]{1,0:T(8,128)S(1)}, f32[16,2048]{1,0:T(8,128)S(1)}, u32[]{:S(2)}, u32[]{:S(2)}) collective-permute-start(f32[16,2048]{1,0:T(8,128)S(1)} %collective-permute-done.3.refs_2_), channel_id=1, source_target_pairs={{0,1},{1,0},{2,3},{3,2},{4,5},{5,4},{6,7},{7,6},{8,9},{9,8},{10,11... | collective-permute-start | bytes 393224 | tf_op jit(solution)/shard_map/ppermute | solution.py:577
  27.1 2.0 %collective-permute-start.9 = (f32[16,1024]{1,0:T(8,128)S(1)}, f32[16,1024]{1,0:T(8,128)S(1)}, u32[]{:S(2)}, u32[]{:S(2)}) collective-permute-start(f32[16,1024]{1,0:T(8,128)S(1)} %collective-permute-done.7.refs_2_), channel_id=1, source_target_pairs={{0,1},{1,0},{2,3},{3,2},{4,5},{5,4},{6,7},{7,6},{8,9},{9,8},{10,11... | collective-permute-start | bytes 196616 | tf_op jit(solution)/shard_map/ppermute | solution.py:577

commit v5 on v4

--- a/solution.py
+++ b/solution.py
@@ -302,7 +302,7 @@
         )
         return carry
 
-    lax.fori_loop(0, lons, coefficients, 0, unroll=4)
+    lax.fori_loop(0, lons, coefficients, 0, unroll=8)
 
     def weigh(first, last, block, carry):
         base = block * 4
@@ -317,7 +317,7 @@
 
     spans = ((0, 1, 2, 7), (1, blocks - 1, -4, 7), (blocks - 1, blocks, -4, -1))
     for start, stop, first, last in spans:
-        lax.fori_loop(start, stop, functools.partial(weigh, first, last), 0)
+        lax.fori_loop(start, stop, functools.partial(weigh, first, last), 0, unroll=stop - start)
     field_copy.wait()
     groups = count // GROUP
 
@@ -417,11 +417,23 @@
     pool_into(lanes, sums, len(jobs), count, put)
 
 
-def share_kernel(winds, obs, from_low, from_high, field, to_low, to_high, coef, weights, sums):
+def split_by_core(where, values, mine, other):
+    first = lax.rem(where[0], 2) == 0
+    for pair in range(4):
+        columns = slice(pair * HALF, (pair + 1) * HALF)
+        a, b = values[0, pair], values[1, pair]
+        mine[:, columns] = jnp.where(first, a, b)
+        other[:, columns] = jnp.where(first, b, a)
+
+
+def share_kernel(
+    where, winds, obs, from_low, from_high, field, mine, other, coef, weights, sums
+):
     lons = obs.shape[0]
+    values = {}
 
     def put(n, pair, value):
-        (to_low, to_high)[n][:, pair * HALF : (pair + 1) * HALF] = value
+        values[1 - n, pair] = value
 
     edge_sums(
         winds, obs, from_low, from_high, field, coef, weights, sums,
@@ -429,17 +441,19 @@
         ((-4, 4, 7), (lons, -4, -1)),
         put,
     )
+    split_by_core(where, values, mine, other)
 
 
 def rest_kernel(
-    winds, obs, from_low, from_high, field, part_low, part_high, after,
-    own_low, own_high, coef, weights, sums,
+    where, winds, obs, from_low, from_high, field, part_low, part_high, after,
+    mine, other, coef, weights, sums,
 ):
     lons = obs.shape[0]
+    values = {}
 
     def put(n, pair, value):
         columns = slice(pair * HALF, (pair + 1) * HALF)
-        (own_low, own_high)[n][:, columns] = value + (part_low, part_high)[n][:, columns]
+        values[n, pair] = value + (part_low, part_high)[n][:, columns]
 
     edge_sums(
         winds, obs, from_low, from_high, field, coef, weights, sums,
@@ -447,6 +461,7 @@
         ((0, 0, 1), (lons - 4, 0, 3)),
         put,
     )
+    split_by_core(where, values, mine, other)
 
 
 def self_product(panel):
@@ -472,10 +487,14 @@
     out[...] = self_product(panel[...])
 
 
-def gram_kernel(where, inner, *refs):
-    pieces, (panel, out) = refs[:-2], refs[-2:]
-    assemble(where, pieces, panel)
-    gram = self_product(panel[...]) + inner[...]
+def gram_kernel(where, inner, chip, far, chip_other, far_other, panel, out):
+    rows = chip.shape[0] // 2
+    core = lax.rem(where[0], 2)
+    for side, pieces, flip in ((core, (chip, far), 0), (1 - core, (chip_other, far_other), 1)):
+        for k in range(4):
+            at = pl.multiple_of(lax.bitwise_xor(where[0], jnp.int32(k ^ flip)) * rows, 8)
+            panel[side, pl.ds(at, rows)] = pieces[k // 2][(k % 2) * rows : (k % 2 + 1) * rows]
+    gram = self_product(panel[0]) + self_product(panel[1]) + inner[...]
     half = gram.shape[0] // 2
     packed = jnp.concatenate([gram[:half], gram[half:]], axis=1)
     for n in range(out.shape[0]):
@@ -542,10 +561,10 @@
             own_rows, columns, precision=lax.Precision.HIGHEST, preferred_element_type=F32
         )
 
-    basis[0] = project(edge[:, :width])
+    basis[0] = project(edge[0])
     for n in range(blocks - 2):
         basis[n + 1] = project(inner[:, n * width : (n + 1) * width])
-    basis[blocks - 1] = project(edge[:, width:])
+    basis[blocks - 1] = project(edge[1])
 
 
 VMEM = pl.BlockSpec(memory_space=pltpu.VMEM)
@@ -627,22 +646,31 @@
         pltpu.VMEM((2, 3, 12, levels, lats), F32),
         pltpu.VMEM((6, 2 * count * 8, HALF), F32),
     ]
-    to_low, to_high = call(
-        share_kernel, "share", (shape(count, 512),) * 2, [VMEM] * 5, edge_scratch
-    )(winds, obs_weight, from_low, from_high, sides)
-    own_low, own_high = call(
-        rest_kernel, "rest", (shape(count, 512),) * 2, [VMEM] * 7 + [ANY], edge_scratch
-    )(winds, obs_weight, from_low, from_high, sides, part_low, part_high, to_low)
-    from_below = lax.ppermute(to_high, "lon", up)
-    from_above = lax.ppermute(to_low, "lon", down)
-    inner, own_low = lax.optimization_barrier((inner, own_low))
+    share, share_other = call(
+        share_kernel, "share", (shape(count, 512),) * 2, [SMEM] + [VMEM] * 5, edge_scratch
+    )(where, winds, obs_weight, from_low, from_high, sides)
+    share = jnp.concatenate([share, swap_probes(share_other, 1)], axis=0)
     size = lax.axis_size("probe")
-    inner_pieces = [inner] + [swap_probes(inner, k) for k in range(1, size) if k & (k - 1) == 0]
-    edge = jnp.concatenate([own_low + from_below, own_high + from_above], axis=1)
-    edge_pieces = [edge] + [swap_probes(edge, k) for k in range(1, size) if k & (k - 1) == 0]
-    inner_pieces, edge_pieces = lax.optimization_barrier((inner_pieces, edge_pieces))
+    arrived = lax.ppermute(
+        share,
+        ("lon", "probe"),
+        [
+            (i * size + p, (up, down)[p & 1][i][1] * size + p)
+            for i in range(ring)
+            for p in range(size)
+        ],
+    )
+    rest, rest_other = call(
+        rest_kernel, "rest", (shape(count, 512),) * 2, [SMEM] + [VMEM] * 7 + [ANY], edge_scratch
+    )(where, winds, obs_weight, from_low, from_high, sides, part_low, part_high, share)
+    inner, rest = lax.optimization_barrier((inner, rest))
+    inner_pieces = [inner, swap_probes(inner, 1), swap_probes(inner, 2)]
+    chip = jnp.concatenate([rest, swap_probes(rest_other, 1)], axis=0) + arrived
+    far = swap_probes(chip, 2)
+    chip_other = swap_probes(chip, 1)
+    inner_pieces, far = lax.optimization_barrier((inner_pieces, far))
     inner_pieces.append(swap_probes(inner_pieces[2], 1))
-    edge_pieces.append(swap_probes(edge_pieces[2], 1))
+    edge_pieces = [chip, far, chip_other, swap_probes(far, 1)]
     inner_panel, inner_gram = call(
         inner_gram_kernel,
         "inner_gram",
@@ -654,7 +682,7 @@
     edge_panel, grams = call(
         gram_kernel,
         "gram",
-        (shape(probes, 1024), shape(ring, probes // 2, 2 * probes)),
+        (shape(2, probes, 512), shape(ring, probes // 2, 2 * probes)),
         [SMEM, VMEM] + [VMEM] * len(edge_pieces),
         (),
         COST,

time: 44 us -> 42 us (0.955)
  starting transfers between devices: 14 us -> 12.7 us
  blocking collectives: 11.2 us -> 10.3 us
  waiting for transfers between devices: 5.61 us -> 6.23 us
  Pallas kernels: 12.4 us -> 11.8 us
    ppermute x2 -> x1, starting transfers between devices: 4.77 us -> 0.01 us  [body(): lax.ppermute(share, ('lon', 'probe'), [(i * size + p, (up, down)[p & 1][i...]
    ppermute x6 -> x8, starting transfers between devices: 3.09 us -> 6.59 us  [swap_probes(): lax.ppermute(value, 'probe', [(i, i ^ step) for i in range(lax.axis_size(...]
    ppermute x2 -> x1, waiting for transfers between devices: 0.01 us -> 1.64 us  [body(): lax.ppermute(share, ('lon', 'probe'), [(i * size + p, (up, down)[p & 1][i...]
    ppermute x6 -> x8, waiting for transfers between devices: 5.59 us -> 4.58 us  [swap_probes(): lax.ppermute(value, 'probe', [(i, i ^ step) for i in range(lax.axis_size(...]
    all_to_all x1, blocking collectives: 11.2 us -> 10.3 us  [body(): grams = lax.all_to_all(grams, 'lon', 0, 0, tiled=True)]
    pallas_call x1, Pallas kernels: 5.05 us -> 4.47 us  [body(): call(interior_kernel, 'interior', (shape(count, (blocks - 2) * 512), shap...]
  transfers between devices with their start and end apart: 10 -> 11, of which waited for: 3 -> 4; matrix products, arithmetic and copies ran while one was open for 0% -> 0% of each run, Pallas kernels for 15% -> 15%
where the time goes in v5:
time: 42 us; the launch traced here: 41.8 us
  starting transfers between devices  12.7 us (30%)
  Pallas kernels  11.8 us (28%)
  blocking collectives  10.3 us (25%)
  waiting for transfers between devices  6.23 us (15%)
  between operations  0.73 us (2%)
    all_to_all x1, blocking collectives, body(): grams = lax.all_to_all(grams, 'lon', 0, 0, tiled=True)  10.3 us
    ppermute x8, starting transfers between devices, swap_probes(): lax.ppermute(value, 'probe', [(i, i ^ step) for i in range(lax.axis_size(...  6.59 us
    ppermute x8, waiting for transfers between devices, swap_probes(): lax.ppermute(value, 'probe', [(i, i ^ step) for i in range(lax.axis_size(...  4.58 us
    pallas_call x1, Pallas kernels, body(): call(interior_kernel, 'interior', (shape(count, (blocks - 2) * 512), shap...  4.47 us
    pallas_call x1, Pallas kernels, body(): call(factor_kernel, 'factor', (shape(blocks, count, 512), shape(probes, p...  3.14 us
    ppermute x1, starting transfers between devices, body(): from_high = lax.ppermute(pack_down, 'lon', down)  3.1 us
    ppermute x1, starting transfers between devices, body(): from_low = lax.ppermute(pack_up, 'lon', up)  2.99 us
    ppermute x1, waiting for transfers between devices, body(): lax.ppermute(share, ('lon', 'probe'), [(i * size + p, (up, down)[p & 1][i...  1.64 us
  transfers between devices with their start and end apart: 11, of which 4 were waited for; matrix products, arithmetic and copies ran while one was open for 0% of the time, Pallas kernels for 15%

profile of v5, /device:TPU:0, one launch (start us, length us, event | category | flops | bytes accessed | tf_op | source)
XLA Modules:
  0.0 41.8 jit_solution(7544636629880996784)
XLA Ops:
  0.6 1.1 %pack.1 = (f32[12,8,256]{2,1,0:T(8,128)S(1)}, f32[10,8,256]{2,1,0:T(8,128)S(1)}, f32[2,24,8,256]{3,2,1,0:T(8,128)S(1)}, f32[24,8,256]{2,1,0:T(8,128)S(1)}) custom-call(f32[2,24,8,256]{3,2,1,0:T(8,128)} %winds_hbm.1, f32[24,8,256]{2,1,0:T(8,128)} %obs_hbm.1), custom_call_target="tpu_custom_call" | custom-call | flops 1000000 | bytes 100000 | tf_op jit(solution)/shard_map/pack/pallas_call | solution.py:611
  1.7 3.0 %collective-permute-start = (f32[12,8,256]{2,1,0:T(8,128)S(1)}, f32[12,8,256]{2,1,0:T(8,128)S(1)}, u32[]{:S(2)}, u32[]{:S(2)}) collective-permute-start(f32[12,8,256]{2,1,0:T(8,128)S(1)} %get-tuple-element.29), channel_id=1, source_target_pairs={{0,4},{4,8},{8,12},{12,16},{16,20},{20,24},{24,28},{28,0},{1,5},{5... | collective-permute-start | bytes 294920 | tf_op jit(solution)/shard_map/ppermute | solution.py:623
  4.7 3.1 %collective-permute-start.1 = (f32[10,8,256]{2,1,0:T(8,128)S(1)}, f32[10,8,256]{2,1,0:T(8,128)S(1)}, u32[]{:S(2)}, u32[]{:S(2)}) collective-permute-start(f32[10,8,256]{2,1,0:T(8,128)S(1)} %get-tuple-element.30), channel_id=1, source_target_pairs={{0,28},{4,0},{8,4},{12,8},{16,12},{20,16},{24,20},{28,24},{1,29},{... | collective-permute-start | bytes 245768 | tf_op jit(solution)/shard_map/ppermute | solution.py:624
  7.8 4.5 %interior.1 = (f32[16,2048]{1,0:T(8,128)S(1)}, f32[16,512]{1,0:T(8,128)S(1)}, f32[16,512]{1,0:T(8,128)S(1)}, f32[16,8,8,256]{3,2,1,0:T(8,128)S(1)}) custom-call(f32[2,24,8,256]{3,2,1,0:T(8,128)S(1)} %get-tuple-element.26.winds, f32[24,8,256]{2,1,0:T(8,128)S(1)} %get-tuple-element.27.obs, f32[16,24,8,256]{3,2,1,0:T(8,128)} %field_hbm.1), custom_call_target="tpu_custom_call" | custom-call | flops 1000000 | bytes 100000 | tf_op jit(solution)/shard_map/interior/pallas_call | solution.py:625
  12.3 0.0 collective-permute-done.1.from_high
  12.3 0.0 collective-permute-done.from_low
  12.3 1.0 %share.1 = (f32[16,512]{1,0:T(8,128)S(1)}, f32[16,512]{1,0:T(8,128)S(1)}) custom-call(s32[1]{0:T(128)} %bitcast.where, f32[2,24,8,256]{3,2,1,0:T(8,128)S(1)} %get-tuple-element.26.winds, f32[24,8,256]{2,1,0:T(8,128)S(1)} %get-tuple-element.27.obs, f32[12,8,256]{2,1,0:T(8,128)S(1)} %collective-permute-done.from_low, ...), custom_call_target="tpu_custom_call" | custom-call | flops 1000000 | bytes 100000 | tf_op jit(solution)/shard_map/share/pallas_call | solution.py:649
  13.3 0.1 collective-permute-start.2
  13.4 1.2 %collective-permute-done.2 = f32[16,512]{1,0:T(8,128)S(1)} collective-permute-done((f32[16,512]{1,0:T(8,128)S(1)}, f32[16,512]{1,0:T(8,128)S(1)}, u32[]{:S(2)}, u32[]{:S(2)}) %collective-permute-start.2) | collective-permute-done | bytes 32800 | tf_op jit(solution)/shard_map/ppermute | solution.py:596
  14.6 0.0 collective-permute-start.6
  14.6 1.1 %rest.1 = (f32[16,512]{1,0:T(8,128)S(1)}, f32[16,512]{1,0:T(8,128)S(1)}) custom-call(s32[1]{0:T(128)} %bitcast.where, f32[2,24,8,256]{3,2,1,0:T(8,128)S(1)} %get-tuple-element.26.winds, f32[24,8,256]{2,1,0:T(8,128)S(1)} %get-tuple-element.27.obs, f32[12,8,256]{2,1,0:T(8,128)S(1)} %collective-permute-done.from_low, ...), custom_call_target="tpu_custom_call" | custom-call | flops 1000000 | bytes 100000 | tf_op jit(solution)/shard_map/rest/pallas_call | solution.py:663
  15.7 2.6 %collective-permute-start.5 = (f32[16,512]{1,0:T(8,128)S(1)}, f32[16,512]{1,0:T(8,128)S(1)}, u32[]{:S(2)}, u32[]{:S(2)}) collective-permute-start(f32[16,512]{1,0:T(8,128)S(1)} %get-tuple-element.39), channel_id=1, source_target_pairs={{0,1},{1,0},{2,3},{3,2},{4,5},{5,4},{6,7},{7,6},{8,9},{9,8},{10,11... | collective-permute-start | bytes 98312 | tf_op jit(solution)/shard_map/ppermute | solution.py:596
  18.3 1.6 %collective-permute-start.4 = (f32[16,2048]{1,0:T(8,128)S(1)}, f32[16,2048]{1,0:T(8,128)S(1)}, u32[]{:S(2)}, u32[]{:S(2)}) collective-permute-start(f32[16,2048]{1,0:T(8,128)S(1)} %get-tuple-element.40.refs_0_), channel_id=1, source_target_pairs={{0,2},{1,3},{2,0},{3,1},{4,6},{5,7},{6,4},{7,5},{8,10},{9,11},{10,... | collective-permute-start | bytes 393224 | tf_op jit(solution)/shard_map/ppermute | solution.py:596
  19.9 0.0 collective-permute-start.3
  19.9 0.0 collective-permute-done.5
  19.9 1.6 %collective-permute-done.6 = f32[32,512]{1,0:T(8,128)S(1)} collective-permute-done((f32[32,512]{1,0:T(8,128)S(1)}, f32[32,512]{1,0:T(8,128)S(1)}, u32[]{:S(2)}, u32[]{:S(2)}) %collective-permute-start.6) | collective-permute-done | bytes 65568 | tf_op jit(solution)/shard_map/ppermute | solution.py:654
  21.6 1.7 %collective-permute-start.7 = (f32[32,512]{1,0:T(8,128)S(1)}, f32[32,512]{1,0:T(8,128)S(1)}, u32[]{:S(2)}, u32[]{:S(2)}) collective-permute-start(f32[32,512]{1,0:T(8,128)S(1)} %maximum_add_fusion.chip), channel_id=1, source_target_pairs={{0,2},{1,3},{2,0},{3,1},{4,6},{5,7},{6,4},{7,5},{8,10},{9,11},{10,... | collective-permute-start | bytes 196616 | tf_op jit(solution)/shard_map/ppermute | solution.py:596
  23.3 2.6 %collective-permute-done.7.far = f32[32,512]{1,0:T(8,128)S(1)} collective-permute-done((f32[32,512]{1,0:T(8,128)S(1)}, f32[32,512]{1,0:T(8,128)S(1)}, u32[]{:S(2)}, u32[]{:S(2)}) %collective-permute-start.7) | collective-permute-done | bytes 65568 | tf_op jit(solution)/shard_map/ppermute | solution.py:596
  25.9 0.0 collective-permute-done.4.refs_2_
  25.9 0.0 collective-permute-done.3.refs_1_
  25.9 0.0 collective-permute-start.8
  25.9 0.5 %collective-permute-start.9 = (f32[32,512]{1,0:T(8,128)S(1)}, f32[32,512]{1,0:T(8,128)S(1)}, u32[]{:S(2)}, u32[]{:S(2)}) collective-permute-start(f32[32,512]{1,0:T(8,128)S(1)} %maximum_add_fusion.chip), channel_id=1, source_target_pairs={{0,1},{1,0},{2,3},{3,2},{4,5},{5,4},{6,7},{7,6},{8,9},{9,8},{10,11... | collective-permute-start | bytes 196616 | tf_op jit(solution)/shard_map/ppermute | solution.py:596
  26.4 0.1 collective-permute-start.10
  26.5 0.8 %collective-permute-done.8.refs_3_ = f32[16,2048]{1,0:T(8,128)S(1)} collective-permute-done((f32[16,2048]{1,0:T(8,128)S(1)}, f32[16,2048]{1,0:T(8,128)S(1)}, u32[]{:S(2)}, u32[]{:S(2)}) %collective-permute-start.8) | collective-permute-done | bytes 131104 | tf_op jit(solution)/shard_map/ppermute | solution.py:596
  27.3 0.6 %inner_gram.1 = (f32[64,2048]{1,0:T(8,128)S(1)}, f32[64,64]{1,0:T(8,128)S(1)}) custom-call(s32[1]{0:T(128)} %bitcast.where, f32[16,2048]{1,0:T(8,128)S(1)} %get-tuple-element.40.refs_0_, f32[16,2048]{1,0:T(8,128)S(1)} %collective-permute-done.3.refs_1_, f32[16,2048]{1,0:T(8,128)S(1)} %collective-permute-done.4.refs_2_, ...), custom_call_target="tpu_custom_call" | custom-call | flops 1000000 | bytes 100000 | tf_op jit(solution)/shard_map/inner_gram/pallas_call | solution.py:674
  27.9 0.0 collective-permute-done.9.chip_other
  27.9 0.0 collective-permute-done.10.far_other
  27.9 0.5 %gram.1 = (f32[2,64,512]{2,1,0:T(8,128)S(1)}, f32[8,32,128]{2,1,0:T(8,128)S(1)}) custom-call(s32[1]{0:T(128)} %bitcast.where, f32[64,64]{1,0:T(8,128)S(1)} %get-tuple-element.43.inner, f32[32,512]{1,0:T(8,128)S(1)} %maximum_add_fusion.chip, f32[32,512]{1,0:T(8,128)S(1)} %collective-permute-done.7.far, f32[32,512]{1,0:T(8,128)S(1)} %collective-permute-done.9.chip_other, ...), custom_call_target="tpu_custom_call" | custom-call | flops 1000000 | bytes 100000 | tf_op jit(solution)/shard_map/gram/pallas_call | solution.py:682
  28.3 10.3 %all_to_all.5.grams = f32[8,32,128]{2,1,0:T(8,128)S(1)} all-to-all(f32[8,32,128]{2,1,0:T(8,128)S(1)} %get-tuple-element.45), channel_id=1, replica_groups=mesh['lon'=8,'probe'=4] {'lon'}, dimensions={0} | all-to-all | bytes 262144 | tf_op jit(solution)/shard_map/all_to_all | solution.py:690
  38.7 3.1 %factor.1 = (f32[6,16,512]{2,1,0:T(8,128)}, f32[64,64]{1,0:T(8,128)}) custom-call(s32[1]{0:T(128)} %bitcast.where, f32[8,32,128]{2,1,0:T(8,128)S(1)} %all_to_all.5.grams, f32[64,2048]{1,0:T(8,128)S(1)} %get-tuple-element.46.inner, f32[2,64,512]{2,1,0:T(8,128)S(1)} %get-tuple-element.47.edge), custom_call_target="tpu_custom_call" | custom-call | flops 1000000 | bytes 100000 | tf_op jit(solution)/shard_map/factor/pallas_call | solution.py:691
  (3 shorter events, 0.0 us)
Async XLA Ops:
  1.7 10.6 %collective-permute-start = (f32[12,8,256]{2,1,0:T(8,128)S(1)}, f32[12,8,256]{2,1,0:T(8,128)S(1)}, u32[]{:S(2)}, u32[]{:S(2)}) collective-permute-start(f32[12,8,256]{2,1,0:T(8,128)S(1)} %get-tuple-element.29), channel_id=1, source_target_pairs={{0,4},{4,8},{8,12},{12,16},{16,20},{20,24},{24,28},{28,0},{1,5},{5... | collective-permute-start | bytes 294920 | tf_op jit(solution)/shard_map/ppermute | solution.py:623
  4.7 7.6 %collective-permute-start.1 = (f32[10,8,256]{2,1,0:T(8,128)S(1)}, f32[10,8,256]{2,1,0:T(8,128)S(1)}, u32[]{:S(2)}, u32[]{:S(2)}) collective-permute-start(f32[10,8,256]{2,1,0:T(8,128)S(1)} %get-tuple-element.30), channel_id=1, source_target_pairs={{0,28},{4,0},{8,4},{12,8},{16,12},{20,16},{24,20},{28,24},{1,29},{... | collective-permute-start | bytes 245768 | tf_op jit(solution)/shard_map/ppermute | solution.py:624
  13.3 1.3 %collective-permute-start.2 = (f32[16,512]{1,0:T(8,128)S(1)}, f32[16,512]{1,0:T(8,128)S(1)}, u32[]{:S(2)}, u32[]{:S(2)}) collective-permute-start(f32[16,512]{1,0:T(8,128)S(1)} %get-tuple-element.35), channel_id=1, source_target_pairs={{0,1},{1,0},{2,3},{3,2},{4,5},{5,4},{6,7},{7,6},{8,9},{9,8},{10,11... | collective-permute-start | bytes 98312 | tf_op jit(solution)/shard_map/ppermute | solution.py:596
  14.6 7.0 %collective-permute-start.6 = (f32[32,512]{1,0:T(8,128)S(1)}, f32[32,512]{1,0:T(8,128)S(1)}, u32[]{:S(2)}, u32[]{:S(2)}) collective-permute-start(f32[32,512]{1,0:T(8,128)S(1)} %constant_dynamic-update-slice_fusion.after), channel_id=1, source_target_pairs={{0,4},{1,29},{2,6},{3,31},{4,8},{5,1},{6,10},{7,3},{8,12},{9,5},{1... | collective-permute-start | bytes 196616 | tf_op jit(solution)/shard_map/ppermute | solution.py:654
  15.7 4.2 %collective-permute-start.5 = (f32[16,512]{1,0:T(8,128)S(1)}, f32[16,512]{1,0:T(8,128)S(1)}, u32[]{:S(2)}, u32[]{:S(2)}) collective-permute-start(f32[16,512]{1,0:T(8,128)S(1)} %get-tuple-element.39), channel_id=1, source_target_pairs={{0,1},{1,0},{2,3},{3,2},{4,5},{5,4},{6,7},{7,6},{8,9},{9,8},{10,11... | collective-permute-start | bytes 98312 | tf_op jit(solution)/shard_map/ppermute | solution.py:596
  18.3 7.6 %collective-permute-start.4 = (f32[16,2048]{1,0:T(8,128)S(1)}, f32[16,2048]{1,0:T(8,128)S(1)}, u32[]{:S(2)}, u32[]{:S(2)}) collective-permute-start(f32[16,2048]{1,0:T(8,128)S(1)} %get-tuple-element.40.refs_0_), channel_id=1, source_target_pairs={{0,2},{1,3},{2,0},{3,1},{4,6},{5,7},{6,4},{7,5},{8,10},{9,11},{10,... | collective-permute-start | bytes 393224 | tf_op jit(solution)/shard_map/ppermute | solution.py:596
  19.9 6.0 %collective-permute-start.3 = (f32[16,2048]{1,0:T(8,128)S(1)}, f32[16,2048]{1,0:T(8,128)S(1)}, u32[]{:S(2)}, u32[]{:S(2)}) collective-permute-start(f32[16,2048]{1,0:T(8,128)S(1)} %get-tuple-element.40.refs_0_), channel_id=1, source_target_pairs={{0,1},{1,0},{2,3},{3,2},{4,5},{5,4},{6,7},{7,6},{8,9},{9,8},{10,11... | collective-permute-start | bytes 393224 | tf_op jit(solution)/shard_map/ppermute | solution.py:596
  21.6 4.3 %collective-permute-start.7 = (f32[32,512]{1,0:T(8,128)S(1)}, f32[32,512]{1,0:T(8,128)S(1)}, u32[]{:S(2)}, u32[]{:S(2)}) collective-permute-start(f32[32,512]{1,0:T(8,128)S(1)} %maximum_add_fusion.chip), channel_id=1, source_target_pairs={{0,2},{1,3},{2,0},{3,1},{4,6},{5,7},{6,4},{7,5},{8,10},{9,11},{10,... | collective-permute-start | bytes 196616 | tf_op jit(solution)/shard_map/ppermute | solution.py:596
  25.9 1.4 %collective-permute-start.8 = (f32[16,2048]{1,0:T(8,128)S(1)}, f32[16,2048]{1,0:T(8,128)S(1)}, u32[]{:S(2)}, u32[]{:S(2)}) collective-permute-start(f32[16,2048]{1,0:T(8,128)S(1)} %collective-permute-done.4.refs_2_), channel_id=1, source_target_pairs={{0,1},{1,0},{2,3},{3,2},{4,5},{5,4},{6,7},{7,6},{8,9},{9,8},{10,11... | collective-permute-start | bytes 393224 | tf_op jit(solution)/shard_map/ppermute | solution.py:596
  25.9 2.0 %collective-permute-start.9 = (f32[32,512]{1,0:T(8,128)S(1)}, f32[32,512]{1,0:T(8,128)S(1)}, u32[]{:S(2)}, u32[]{:S(2)}) collective-permute-start(f32[32,512]{1,0:T(8,128)S(1)} %maximum_add_fusion.chip), channel_id=1, source_target_pairs={{0,1},{1,0},{2,3},{3,2},{4,5},{5,4},{6,7},{7,6},{8,9},{9,8},{10,11... | collective-permute-start | bytes 196616 | tf_op jit(solution)/shard_map/ppermute | solution.py:596
  26.4 1.5 %collective-permute-start.10 = (f32[32,512]{1,0:T(8,128)S(1)}, f32[32,512]{1,0:T(8,128)S(1)}, u32[]{:S(2)}, u32[]{:S(2)}) collective-permute-start(f32[32,512]{1,0:T(8,128)S(1)} %collective-permute-done.7.far), channel_id=1, source_target_pairs={{0,1},{1,0},{2,3},{3,2},{4,5},{5,4},{6,7},{7,6},{8,9},{9,8},{10,11... | collective-permute-start | bytes 196616 | tf_op jit(solution)/shard_map/ppermute | solution.py:596

commit v6 on v5

--- a/solution.py
+++ b/solution.py
@@ -268,14 +268,24 @@
     up[0:3] = winds[0, lons - 3 :]
     up[3:6] = winds[1, lons - 3 :]
     up[6:8] = obs[lons - 2 :]
-    up[8:] = obs[lons - 4 :]
+    up[8:10] = obs[lons - 2 :]
     down[0:4] = winds[0, 0:4]
-    down[4:8] = winds[1, 0:4]
-    down[8:10] = obs[0:2]
+    down[4:7] = winds[1, 0:3]
+    down[7:9] = obs[0:2]
+
+
+def split_by_core(where, values, mine, other):
+    first = lax.rem(where[0], 2) == 0
+    for pair in range(mine.shape[1] // HALF):
+        columns = slice(pair * HALF, (pair + 1) * HALF)
+        a, b = values[0, pair], values[1, pair]
+        mine[:, columns] = jnp.where(first, a, b)
+        other[:, columns] = jnp.where(first, b, a)
 
 
 def interior_kernel(
-    winds, obs, field_hbm, out, part_low, part_high, sides, coef, weights, sums, field, sems
+    where, winds, obs, field_hbm, mine, other, part_low, part_high, sides,
+    coef, weights, sums, field, sems,
 ):
     count, lons = field.shape[0], field.shape[1]
     blocks = lons // 4
@@ -348,10 +358,12 @@
         elif n == blocks - 1:
             part_high[:, pair * HALF : (pair + 1) * HALF] = value
         else:
-            column = ((n - 1) * 4 + pair) * HALF
-            out[:, column : column + HALF] = value
-
+            values[divmod((n - 1) * 4 + pair, pieces)] = value
+
+    values = {}
+    pieces = mine.shape[1] // HALF
     pool_into(lanes, sums, blocks, count, put)
+    split_by_core(where, values, mine, other)
     for copy in side_copies:
         copy.wait()
 
@@ -364,14 +376,14 @@
         if lon < 0:
             return halves(from_low, 3 * which + lon + 3)
         if lon >= lons:
-            return halves(from_high, 4 * which + lon - lons)
+            return halves(from_high, min(4 * which + lon - lons, 6))
         return halves(winds, which, lon)
 
     def weight_at(lon):
         if lon < 0:
             return halves(from_low, 6 + lon + 2)
         if lon >= lons:
-            return halves(from_high, 8 + lon - lons)
+            return halves(from_high, 7 + lon - lons)
         return halves(obs, lon)
 
     slots = {}
@@ -417,15 +429,6 @@
     pool_into(lanes, sums, len(jobs), count, put)
 
 
-def split_by_core(where, values, mine, other):
-    first = lax.rem(where[0], 2) == 0
-    for pair in range(4):
-        columns = slice(pair * HALF, (pair + 1) * HALF)
-        a, b = values[0, pair], values[1, pair]
-        mine[:, columns] = jnp.where(first, a, b)
-        other[:, columns] = jnp.where(first, b, a)
-
-
 def share_kernel(
     where, winds, obs, from_low, from_high, field, mine, other, coef, weights, sums
 ):
@@ -474,34 +477,31 @@
     )
 
 
-def assemble(where, pieces, panel):
-    rows = pieces[0].shape[0]
-    for k, piece in enumerate(pieces):
+def assemble(where, chip, far, panel):
+    rows = chip.shape[0] // 2
+    for k in range(4):
         at = pl.multiple_of(lax.bitwise_xor(where[0], jnp.int32(k)) * rows, 8)
-        panel[pl.ds(at, rows)] = piece[...]
-
-
-def inner_gram_kernel(where, *refs):
-    pieces, (panel, out) = refs[:-2], refs[-2:]
-    assemble(where, pieces, panel)
-    out[...] = self_product(panel[...])
-
-
-def gram_kernel(where, inner, chip, far, chip_other, far_other, panel, out):
-    rows = chip.shape[0] // 2
-    core = lax.rem(where[0], 2)
-    for side, pieces, flip in ((core, (chip, far), 0), (1 - core, (chip_other, far_other), 1)):
-        for k in range(4):
-            at = pl.multiple_of(lax.bitwise_xor(where[0], jnp.int32(k ^ flip)) * rows, 8)
-            panel[side, pl.ds(at, rows)] = pieces[k // 2][(k % 2) * rows : (k % 2 + 1) * rows]
-    gram = self_product(panel[0]) + self_product(panel[1]) + inner[...]
+        panel[pl.ds(at, rows)] = (chip, far)[k // 2][(k % 2) * rows : (k % 2 + 1) * rows]
+
+
+def gram_kernel(where, inner_chip, inner_far, edge_chip, edge_far, panel, out):
+    width = inner_chip.shape[1]
+    assemble(where, inner_chip, inner_far, panel.at[:, :width])
+    assemble(where, edge_chip, edge_far, panel.at[:, width:])
+    gram = self_product(panel[...])
     half = gram.shape[0] // 2
-    packed = jnp.concatenate([gram[:half], gram[half:]], axis=1)
+    out[...] = jnp.concatenate([gram[:half], gram[half:]], axis=1)
+
+
+def copies_kernel(mine, other, out):
+    total = mine[...] + other[...]
     for n in range(out.shape[0]):
-        out[n] = packed
-
-
-def factor_kernel(where, grams, inner, edge, basis, upper, inverse):
+        out[n] = total
+
+
+def factor_kernel(
+    where, grams, panel, panel_other, basis, upper, inverse
+):
     packed = grams[0]
     for n in range(1, grams.shape[0]):
         packed = packed + grams[n]
@@ -561,10 +561,12 @@
             own_rows, columns, precision=lax.Precision.HIGHEST, preferred_element_type=F32
         )
 
-    basis[0] = project(edge[0])
-    for n in range(blocks - 2):
-        basis[n + 1] = project(inner[:, n * width : (n + 1) * width])
-    basis[blocks - 1] = project(edge[1])
+    core = lax.rem(where[0], 2)
+    half = (blocks - 2) // 2
+    for side, part in ((core, panel), (1 - core, panel_other)):
+        for n in range(half):
+            basis[1 + side * half + n] = project(part[:, n * width : (n + 1) * width])
+        basis[side * (blocks - 1)] = project(part[:, half * width :])
 
 
 VMEM = pl.BlockSpec(memory_space=pltpu.VMEM)
@@ -572,7 +574,6 @@
 HBM = pl.BlockSpec(memory_space=pltpu.HBM)
 ANY = pl.BlockSpec(memory_space=pl.ANY)
 MIB = 1024 * 1024
-COST = 1_000_000
 
 
 def shape(*dims):
@@ -612,8 +613,8 @@
         pack_kernel,
         "pack",
         (
-            shape(12, levels, lats),
             shape(10, levels, lats),
+            shape(9, levels, lats),
             shape(2, lons, levels, lats),
             shape(lons, levels, lats),
         ),
@@ -622,16 +623,17 @@
     )(winds, obs_weight)
     from_low = lax.ppermute(pack_up, "lon", up)
     from_high = lax.ppermute(pack_down, "lon", down)
-    inner, part_low, part_high, sides = call(
+    inner, inner_other, part_low, part_high, sides = call(
         interior_kernel,
         "interior",
         (
-            shape(count, (blocks - 2) * 512),
+            shape(count, (blocks - 2) * 256),
+            shape(count, (blocks - 2) * 256),
             shape(count, 512),
             shape(count, 512),
             shape(count, 8, levels, lats),
         ),
-        [VMEM, VMEM, HBM],
+        [SMEM, VMEM, VMEM, HBM],
         [
             pltpu.VMEM((PLANES, lons, levels, lats), F32),
             pltpu.VMEM((blocks, 3, 12, levels, lats), F32),
@@ -639,8 +641,7 @@
             pltpu.VMEM((count, lons, levels, lats), F32),
             dma((3,)),
         ],
-        COST,
-    )(winds, obs_weight, increments)
+    )(where, winds, obs_weight, increments)
     edge_scratch = [
         pltpu.VMEM((PLANES, 14, levels, lats), F32),
         pltpu.VMEM((2, 3, 12, levels, lats), F32),
@@ -663,39 +664,30 @@
     rest, rest_other = call(
         rest_kernel, "rest", (shape(count, 512),) * 2, [SMEM] + [VMEM] * 7 + [ANY], edge_scratch
     )(where, winds, obs_weight, from_low, from_high, sides, part_low, part_high, share)
-    inner, rest = lax.optimization_barrier((inner, rest))
-    inner_pieces = [inner, swap_probes(inner, 1), swap_probes(inner, 2)]
-    chip = jnp.concatenate([rest, swap_probes(rest_other, 1)], axis=0) + arrived
-    far = swap_probes(chip, 2)
-    chip_other = swap_probes(chip, 1)
-    inner_pieces, far = lax.optimization_barrier((inner_pieces, far))
-    inner_pieces.append(swap_probes(inner_pieces[2], 1))
-    edge_pieces = [chip, far, chip_other, swap_probes(far, 1)]
-    inner_panel, inner_gram = call(
-        inner_gram_kernel,
-        "inner_gram",
-        (shape(probes, inner.shape[1]), shape(probes, probes)),
-        [SMEM] + [VMEM] * len(inner_pieces),
-        (),
-        COST,
-    )(where, *inner_pieces)
-    edge_panel, grams = call(
+    inner_chip = jnp.concatenate([inner, swap_probes(inner_other, 1)], axis=0)
+    inner_chip, rest = lax.optimization_barrier((inner_chip, rest))
+    inner_far = swap_probes(inner_chip, 2)
+    edge_chip = jnp.concatenate([rest, swap_probes(rest_other, 1)], axis=0) + arrived
+    edge_far = swap_probes(edge_chip, 2)
+    inner_far, edge_far = lax.optimization_barrier((inner_far, edge_far))
+    panel, gram = call(
         gram_kernel,
         "gram",
-        (shape(2, probes, 512), shape(ring, probes // 2, 2 * probes)),
-        [SMEM, VMEM] + [VMEM] * len(edge_pieces),
-        (),
-        COST,
-    )(where, inner_gram, *edge_pieces)
+        (shape(probes, blocks * 256), shape(probes // 2, 2 * probes)),
+        [SMEM] + [VMEM] * 4,
+    )(where, inner_chip, inner_far, edge_chip, edge_far)
+    panel, gram_other = lax.optimization_barrier((panel, swap_probes(gram, 1)))
+    grams = call(copies_kernel, "copies", shape(ring, probes // 2, 2 * probes), [VMEM] * 2)(
+        gram, gram_other
+    )
     grams = lax.all_to_all(grams, "lon", 0, 0, tiled=True)
     basis, upper = call(
         factor_kernel,
         "factor",
         (shape(blocks, count, 512), shape(probes, probes)),
-        [SMEM, VMEM, VMEM, VMEM],
+        [SMEM] + [VMEM] * 3,
         [pltpu.VMEM((probes, probes), F32)],
-        COST,
-    )(where, grams, inner_panel, edge_panel)
+    )(where, grams, panel, swap_probes(panel, 1))
     return basis.transpose(1, 0, 2), upper
 
 

time: 42 us -> 41.9 us (level)
  Pallas kernels: 11.8 us -> 11.3 us
    pallas_call x4, Pallas kernels: 6.61 us -> 6.11 us  [the longest x1 4.47 us: body(): call(interior_kernel, 'interior', (shape(count, (blocks - 2) * 256), shap...]
    ppermute x8 -> x7, starting transfers between devices: 6.59 us -> 6.51 us  [swap_probes(): lax.ppermute(value, 'probe', [(i, i ^ step) for i in range(lax.axis_size(...]
    ppermute x8 -> x7, waiting for transfers between devices: 4.58 us -> 4.66 us  [swap_probes(): lax.ppermute(value, 'probe', [(i, i ^ step) for i in range(lax.axis_size(...]
  transfers between devices with their start and end apart: 11 -> 10, of which waited for: 4 -> 4; matrix products, arithmetic and copies ran while one was open for 0% -> 0% of each run, Pallas kernels for 15% -> 16%
where the time goes in v6:
time: 41.9 us; the launch traced here: 41.7 us
  starting transfers between devices  12.6 us (30%)
  Pallas kernels  11.3 us (27%)
  blocking collectives  10.5 us (25%)
  waiting for transfers between devices  6.52 us (16%)
  between operations  0.71 us (2%)
    all_to_all x1, blocking collectives, body(): grams = lax.all_to_all(grams, 'lon', 0, 0, tiled=True)  10.5 us
    ppermute x7, starting transfers between devices, swap_probes(): lax.ppermute(value, 'probe', [(i, i ^ step) for i in range(lax.axis_size(...  6.51 us
    ppermute x7, waiting for transfers between devices, swap_probes(): lax.ppermute(value, 'probe', [(i, i ^ step) for i in range(lax.axis_size(...  4.66 us
    pallas_call x1, Pallas kernels, body(): call(interior_kernel, 'interior', (shape(count, (blocks - 2) * 256), shap...  4.47 us
    pallas_call x1, Pallas kernels, body(): call(factor_kernel, 'factor', (shape(blocks, count, 512), shape(probes, p...  3.14 us
    ppermute x1, starting transfers between devices, body(): from_high = lax.ppermute(pack_down, 'lon', down)  3.1 us
    ppermute x1, starting transfers between devices, body(): from_low = lax.ppermute(pack_up, 'lon', up)  2.99 us
    ppermute x1, waiting for transfers between devices, body(): lax.ppermute(share, ('lon', 'probe'), [(i * size + p, (up, down)[p & 1][i...  1.86 us
  transfers between devices with their start and end apart: 10, of which 4 were waited for; matrix products, arithmetic and copies ran while one was open for 0% of the time, Pallas kernels for 16%

profile of v6, /device:TPU:0, one launch (start us, length us, event | category | flops | bytes accessed | tf_op | source)
XLA Modules:
  0.0 41.7 jit_solution(16814852841334809152)
XLA Ops:
  0.6 1.1 %pack.1 = (f32[10,8,256]{2,1,0:T(8,128)S(1)}, f32[9,8,256]{2,1,0:T(8,128)S(1)}, f32[2,24,8,256]{3,2,1,0:T(8,128)S(1)}, f32[24,8,256]{2,1,0:T(8,128)S(1)}) custom-call(f32[2,24,8,256]{3,2,1,0:T(8,128)} %winds_hbm.1, f32[24,8,256]{2,1,0:T(8,128)} %obs_hbm.1), custom_call_target="tpu_custom_call" | custom-call | flops 1000000 | bytes 100000 | tf_op jit(solution)/shard_map/pack/pallas_call | solution.py:612
  1.7 3.0 %collective-permute-start.1 = (f32[10,8,256]{2,1,0:T(8,128)S(1)}, f32[10,8,256]{2,1,0:T(8,128)S(1)}, u32[]{:S(2)}, u32[]{:S(2)}) collective-permute-start(f32[10,8,256]{2,1,0:T(8,128)S(1)} %get-tuple-element.29), channel_id=1, source_target_pairs={{0,4},{4,8},{8,12},{12,16},{16,20},{20,24},{24,28},{28,0},{1,5},{5... | collective-permute-start | bytes 245768 | tf_op jit(solution)/shard_map/ppermute | solution.py:624
  4.7 3.1 %collective-permute-start.2 = (f32[9,8,256]{2,1,0:T(8,128)S(1)}, f32[9,8,256]{2,1,0:T(8,128)S(1)}, u32[]{:S(2)}, u32[]{:S(2)}) collective-permute-start(f32[9,8,256]{2,1,0:T(8,128)S(1)} %get-tuple-element.30), channel_id=1, source_target_pairs={{0,28},{4,0},{8,4},{12,8},{16,12},{20,16},{24,20},{28,24},{1,29},{... | collective-permute-start | bytes 221192 | tf_op jit(solution)/shard_map/ppermute | solution.py:625
  7.8 4.5 %interior.1 = (f32[16,1024]{1,0:T(8,128)S(1)}, f32[16,1024]{1,0:T(8,128)S(1)}, f32[16,512]{1,0:T(8,128)S(1)}, f32[16,512]{1,0:T(8,128)S(1)}, f32[16,8,8,256]{3,2,1,0:T(8,128)S(1)}) custom-call(s32[1]{0:T(128)} %bitcast.where, f32[2,24,8,256]{3,2,1,0:T(8,128)S(1)} %get-tuple-element.25.winds, f32[24,8,256]{2,1,0:T(8,128)S(1)} %get-tuple-element.26.obs, ...), custom_call_target="tpu_custom_call" | custom-call | flops 1000000 | bytes 100000 | tf_op jit(solution)/shard_map/interior/pallas_call | solution.py:626
  12.3 0.1 collective-permute-start
  12.4 0.0 collective-permute-done.2.from_high
  12.4 0.0 collective-permute-done.1.from_low
  12.4 1.0 %share.1 = (f32[16,512]{1,0:T(8,128)S(1)}, f32[16,512]{1,0:T(8,128)S(1)}) custom-call(s32[1]{0:T(128)} %bitcast.where, f32[2,24,8,256]{3,2,1,0:T(8,128)S(1)} %get-tuple-element.25.winds, f32[24,8,256]{2,1,0:T(8,128)S(1)} %get-tuple-element.26.obs, f32[10,8,256]{2,1,0:T(8,128)S(1)} %collective-permute-done.1.from_low, ...), custom_call_target="tpu_custom_call" | custom-call | flops 1000000 | bytes 100000 | tf_op jit(solution)/shard_map/share/pallas_call | solution.py:650
  13.4 0.5 %collective-permute-start.3 = (f32[16,512]{1,0:T(8,128)S(1)}, f32[16,512]{1,0:T(8,128)S(1)}, u32[]{:S(2)}, u32[]{:S(2)}) collective-permute-start(f32[16,512]{1,0:T(8,128)S(1)} %get-tuple-element.35), channel_id=1, source_target_pairs={{0,1},{1,0},{2,3},{3,2},{4,5},{5,4},{6,7},{7,6},{8,9},{9,8},{10,11... | collective-permute-start | bytes 98312 | tf_op jit(solution)/shard_map/ppermute | solution.py:597
  13.9 0.9 %collective-permute-done.3 = f32[16,512]{1,0:T(8,128)S(1)} collective-permute-done((f32[16,512]{1,0:T(8,128)S(1)}, f32[16,512]{1,0:T(8,128)S(1)}, u32[]{:S(2)}, u32[]{:S(2)}) %collective-permute-start.3) | collective-permute-done | bytes 32800 | tf_op jit(solution)/shard_map/ppermute | solution.py:597
  14.8 0.0 collective-permute-start.6
  14.8 1.1 %rest.1 = (f32[16,512]{1,0:T(8,128)S(1)}, f32[16,512]{1,0:T(8,128)S(1)}) custom-call(s32[1]{0:T(128)} %bitcast.where, f32[2,24,8,256]{3,2,1,0:T(8,128)S(1)} %get-tuple-element.25.winds, f32[24,8,256]{2,1,0:T(8,128)S(1)} %get-tuple-element.26.obs, f32[10,8,256]{2,1,0:T(8,128)S(1)} %collective-permute-done.1.from_low, ...), custom_call_target="tpu_custom_call" | custom-call | flops 1000000 | bytes 100000 | tf_op jit(solution)/shard_map/rest/pallas_call | solution.py:664
  15.9 2.3 %collective-permute-start.5 = (f32[16,512]{1,0:T(8,128)S(1)}, f32[16,512]{1,0:T(8,128)S(1)}, u32[]{:S(2)}, u32[]{:S(2)}) collective-permute-start(f32[16,512]{1,0:T(8,128)S(1)} %get-tuple-element.39), channel_id=1, source_target_pairs={{0,1},{1,0},{2,3},{3,2},{4,5},{5,4},{6,7},{7,6},{8,9},{9,8},{10,11... | collective-permute-start | bytes 98312 | tf_op jit(solution)/shard_map/ppermute | solution.py:597
  18.2 0.0 collective-permute-done
  18.2 1.7 %collective-permute-start.4 = (f32[32,1024]{1,0:T(8,128)S(1)}, f32[32,1024]{1,0:T(8,128)S(1)}, u32[]{:S(2)}, u32[]{:S(2)}) collective-permute-start(f32[32,1024]{1,0:T(8,128)S(1)} %pad_maximum_fusion.inner_chip), channel_id=1, source_target_pairs={{0,2},{1,3},{2,0},{3,1},{4,6},{5,7},{6,4},{7,5},{8,10},{9,11},{10,... | collective-permute-start | bytes 393224 | tf_op jit(solution)/shard_map/ppermute | solution.py:597
  19.9 0.0 collective-permute-done.5
  19.9 1.9 %collective-permute-done.6 = f32[32,512]{1,0:T(8,128)S(1)} collective-permute-done((f32[32,512]{1,0:T(8,128)S(1)}, f32[32,512]{1,0:T(8,128)S(1)}, u32[]{:S(2)}, u32[]{:S(2)}) %collective-permute-start.6) | collective-permute-done | bytes 65568 | tf_op jit(solution)/shard_map/ppermute | solution.py:655
  21.8 1.7 %collective-permute-start.7 = (f32[32,512]{1,0:T(8,128)S(1)}, f32[32,512]{1,0:T(8,128)S(1)}, u32[]{:S(2)}, u32[]{:S(2)}) collective-permute-start(f32[32,512]{1,0:T(8,128)S(1)} %maximum_add_fusion.edge_chip), channel_id=1, source_target_pairs={{0,2},{1,3},{2,0},{3,1},{4,6},{5,7},{6,4},{7,5},{8,10},{9,11},{10,... | collective-permute-start | bytes 196616 | tf_op jit(solution)/shard_map/ppermute | solution.py:597
  23.5 2.6 %collective-permute-done.7.edge_far = f32[32,512]{1,0:T(8,128)S(1)} collective-permute-done((f32[32,512]{1,0:T(8,128)S(1)}, f32[32,512]{1,0:T(8,128)S(1)}, u32[]{:S(2)}, u32[]{:S(2)}) %collective-permute-start.7) | collective-permute-done | bytes 65568 | tf_op jit(solution)/shard_map/ppermute | solution.py:597
  26.1 0.0 collective-permute-done.4.inner_far
  26.1 0.5 %gram.1 = (f32[64,1536]{1,0:T(8,128)S(1)}, f32[32,128]{1,0:T(8,128)S(1)}) custom-call(s32[1]{0:T(128)} %bitcast.where, f32[32,1024]{1,0:T(8,128)S(1)} %pad_maximum_fusion.inner_chip, f32[32,1024]{1,0:T(8,128)S(1)} %collective-permute-done.4.inner_far, f32[32,512]{1,0:T(8,128)S(1)} %maximum_add_fusion.edge_chip, f32[32,512]{1,0:T(8,128)S(1)} %collective-permute-done.7.edge_far), custom_call_target="tpu_custom_call" | custom-call | flops 1000000 | bytes 100000 | tf_op jit(solution)/shard_map/gram/pallas_call | solution.py:673
  26.6 0.0 collective-permute-start.8
  26.7 1.2 %collective-permute-done.8.other = f32[32,128]{1,0:T(8,128)S(1)} collective-permute-done((f32[32,128]{1,0:T(8,128)S(1)}, f32[32,128]{1,0:T(8,128)S(1)}, u32[]{:S(2)}, u32[]{:S(2)}) %collective-permute-start.8) | collective-permute-done | bytes 16416 | tf_op jit(solution)/shard_map/ppermute | solution.py:597
  27.8 0.2 collective-permute-start.9
  28.0 10.5 %all_to_all.5.grams = f32[8,32,128]{2,1,0:T(8,128)S(1)} all-to-all(f32[8,32,128]{2,1,0:T(8,128)S(1)} %copies.1), channel_id=1, replica_groups=mesh['lon'=8,'probe'=4] {'lon'}, dimensions={0} | all-to-all | bytes 262144 | tf_op jit(solution)/shard_map/all_to_all | solution.py:683
  38.6 0.0 collective-permute-done.9.panel_other
  38.6 3.1 %factor.1 = (f32[6,16,512]{2,1,0:T(8,128)}, f32[64,64]{1,0:T(8,128)}) custom-call(s32[1]{0:T(128)} %bitcast.where, f32[8,32,128]{2,1,0:T(8,128)S(1)} %all_to_all.5.grams, f32[64,1536]{1,0:T(8,128)S(1)} %get-tuple-element.45.panel, f32[64,1536]{1,0:T(8,128)S(1)} %collective-permute-done.9.panel_other), custom_call_target="tpu_custom_call" | custom-call | flops 1000000 | bytes 100000 | tf_op jit(solution)/shard_map/factor/pallas_call | solution.py:684
  (5 shorter events, 0.0 us)
Async XLA Ops:
  1.7 10.7 %collective-permute-start.1 = (f32[10,8,256]{2,1,0:T(8,128)S(1)}, f32[10,8,256]{2,1,0:T(8,128)S(1)}, u32[]{:S(2)}, u32[]{:S(2)}) collective-permute-start(f32[10,8,256]{2,1,0:T(8,128)S(1)} %get-tuple-element.29), channel_id=1, source_target_pairs={{0,4},{4,8},{8,12},{12,16},{16,20},{20,24},{24,28},{28,0},{1,5},{5... | collective-permute-start | bytes 245768 | tf_op jit(solution)/shard_map/ppermute | solution.py:624
  4.7 7.7 %collective-permute-start.2 = (f32[9,8,256]{2,1,0:T(8,128)S(1)}, f32[9,8,256]{2,1,0:T(8,128)S(1)}, u32[]{:S(2)}, u32[]{:S(2)}) collective-permute-start(f32[9,8,256]{2,1,0:T(8,128)S(1)} %get-tuple-element.30), channel_id=1, source_target_pairs={{0,28},{4,0},{8,4},{12,8},{16,12},{20,16},{24,20},{28,24},{1,29},{... | collective-permute-start | bytes 221192 | tf_op jit(solution)/shard_map/ppermute | solution.py:625
  12.3 5.9 %collective-permute-start = (f32[16,1024]{1,0:T(8,128)S(1)}, f32[16,1024]{1,0:T(8,128)S(1)}, u32[]{:S(2)}, u32[]{:S(2)}) collective-permute-start(f32[16,1024]{1,0:T(8,128)S(1)} %get-tuple-element.28), channel_id=1, source_target_pairs={{0,1},{1,0},{2,3},{3,2},{4,5},{5,4},{6,7},{7,6},{8,9},{9,8},{10,11... | collective-permute-start | bytes 196616 | tf_op jit(solution)/shard_map/ppermute | solution.py:597
  13.4 1.4 %collective-permute-start.3 = (f32[16,512]{1,0:T(8,128)S(1)}, f32[16,512]{1,0:T(8,128)S(1)}, u32[]{:S(2)}, u32[]{:S(2)}) collective-permute-start(f32[16,512]{1,0:T(8,128)S(1)} %get-tuple-element.35), channel_id=1, source_target_pairs={{0,1},{1,0},{2,3},{3,2},{4,5},{5,4},{6,7},{7,6},{8,9},{9,8},{10,11... | collective-permute-start | bytes 98312 | tf_op jit(solution)/shard_map/ppermute | solution.py:597
  14.8 7.0 %collective-permute-start.6 = (f32[32,512]{1,0:T(8,128)S(1)}, f32[32,512]{1,0:T(8,128)S(1)}, u32[]{:S(2)}, u32[]{:S(2)}) collective-permute-start(f32[32,512]{1,0:T(8,128)S(1)} %constant_dynamic-update-slice_fusion.after), channel_id=1, source_target_pairs={{0,4},{1,29},{2,6},{3,31},{4,8},{5,1},{6,10},{7,3},{8,12},{9,5},{1... | collective-permute-start | bytes 196616 | tf_op jit(solution)/shard_map/ppermute | solution.py:655
  15.9 4.0 %collective-permute-start.5 = (f32[16,512]{1,0:T(8,128)S(1)}, f32[16,512]{1,0:T(8,128)S(1)}, u32[]{:S(2)}, u32[]{:S(2)}) collective-permute-start(f32[16,512]{1,0:T(8,128)S(1)} %get-tuple-element.39), channel_id=1, source_target_pairs={{0,1},{1,0},{2,3},{3,2},{4,5},{5,4},{6,7},{7,6},{8,9},{9,8},{10,11... | collective-permute-start | bytes 98312 | tf_op jit(solution)/shard_map/ppermute | solution.py:597
  18.2 7.9 %collective-permute-start.4 = (f32[32,1024]{1,0:T(8,128)S(1)}, f32[32,1024]{1,0:T(8,128)S(1)}, u32[]{:S(2)}, u32[]{:S(2)}) collective-permute-start(f32[32,1024]{1,0:T(8,128)S(1)} %pad_maximum_fusion.inner_chip), channel_id=1, source_target_pairs={{0,2},{1,3},{2,0},{3,1},{4,6},{5,7},{6,4},{7,5},{8,10},{9,11},{10,... | collective-permute-start | bytes 393224 | tf_op jit(solution)/shard_map/ppermute | solution.py:597
  21.8 4.3 %collective-permute-start.7 = (f32[32,512]{1,0:T(8,128)S(1)}, f32[32,512]{1,0:T(8,128)S(1)}, u32[]{:S(2)}, u32[]{:S(2)}) collective-permute-start(f32[32,512]{1,0:T(8,128)S(1)} %maximum_add_fusion.edge_chip), channel_id=1, source_target_pairs={{0,2},{1,3},{2,0},{3,1},{4,6},{5,7},{6,4},{7,5},{8,10},{9,11},{10,... | collective-permute-start | bytes 196616 | tf_op jit(solution)/shard_map/ppermute | solution.py:597
  26.6 1.2 %collective-permute-start.8 = (f32[32,128]{1,0:T(8,128)S(1)}, f32[32,128]{1,0:T(8,128)S(1)}, u32[]{:S(2)}, u32[]{:S(2)}) collective-permute-start(f32[32,128]{1,0:T(8,128)S(1)} %get-tuple-element.42.mine), channel_id=1, source_target_pairs={{0,1},{1,0},{2,3},{3,2},{4,5},{5,4},{6,7},{7,6},{8,9},{9,8},{10,11... | collective-permute-start | bytes 49160 | tf_op jit(solution)/shard_map/ppermute | solution.py:597
  27.8 10.7 %collective-permute-start.9 = (f32[64,1536]{1,0:T(8,128)S(1)}, f32[64,1536]{1,0:T(8,128)S(1)}, u32[]{:S(2)}, u32[]{:S(2)}) collective-permute-start(f32[64,1536]{1,0:T(8,128)S(1)} %get-tuple-element.45.panel), channel_id=1, source_target_pairs={{0,1},{1,0},{2,3},{3,2},{4,5},{5,4},{6,7},{7,6},{8,9},{9,8},{10,11... | collective-permute-start | bytes 1179656 | tf_op jit(solution)/shard_map/ppermute | solution.py:597

commit v7 on v6

--- a/solution.py
+++ b/solution.py
@@ -238,6 +238,7 @@
 
 
 GROUP = 8
+EDGE_GROUP = 16
 
 
 def weight_keys(first, last):
@@ -421,11 +422,11 @@
                 lambda r, part: halves(weights, n, part, r + 4),
                 read,
                 write,
-                [step * GROUP + k for k in range(GROUP)],
+                [step * EDGE_GROUP + k for k in range(EDGE_GROUP)],
             )
         return carry
 
-    lax.fori_loop(0, count // GROUP, sweep, 0)
+    lax.fori_loop(0, count // EDGE_GROUP, sweep, 0)
     pool_into(lanes, sums, len(jobs), count, put)
 
 
@@ -484,13 +485,18 @@
         panel[pl.ds(at, rows)] = (chip, far)[k // 2][(k % 2) * rows : (k % 2 + 1) * rows]
 
 
-def gram_kernel(where, inner_chip, inner_far, edge_chip, edge_far, panel, out):
+def inner_gram_kernel(where, chip, far, out, panel):
+    assemble(where, chip, far, panel)
+    out[...] = self_product(panel[...])
+
+
+def gram_kernel(where, inner_gram, inner_chip, inner_far, edge_chip, edge_far, panel, out):
     width = inner_chip.shape[1]
-    assemble(where, inner_chip, inner_far, panel.at[:, :width])
     assemble(where, edge_chip, edge_far, panel.at[:, width:])
-    gram = self_product(panel[...])
+    gram = self_product(panel[:, width:]) + inner_gram[...]
     half = gram.shape[0] // 2
     out[...] = jnp.concatenate([gram[:half], gram[half:]], axis=1)
+    assemble(where, inner_chip, inner_far, panel.at[:, :width])
 
 
 def copies_kernel(mine, other, out):
@@ -563,6 +569,7 @@
 
     core = lax.rem(where[0], 2)
     half = (blocks - 2) // 2
+
     for side, part in ((core, panel), (1 - core, panel_other)):
         for n in range(half):
             basis[1 + side * half + n] = project(part[:, n * width : (n + 1) * width])
@@ -665,17 +672,22 @@
         rest_kernel, "rest", (shape(count, 512),) * 2, [SMEM] + [VMEM] * 7 + [ANY], edge_scratch
     )(where, winds, obs_weight, from_low, from_high, sides, part_low, part_high, share)
     inner_chip = jnp.concatenate([inner, swap_probes(inner_other, 1)], axis=0)
-    inner_chip, rest = lax.optimization_barrier((inner_chip, rest))
     inner_far = swap_probes(inner_chip, 2)
+    inner_gram = call(
+        inner_gram_kernel,
+        "inner_gram",
+        shape(probes, probes),
+        [SMEM, VMEM, VMEM],
+        [pltpu.VMEM((probes, (blocks - 2) * 256), F32)],
+    )(where, inner_chip, inner_far)
     edge_chip = jnp.concatenate([rest, swap_probes(rest_other, 1)], axis=0) + arrived
     edge_far = swap_probes(edge_chip, 2)
-    inner_far, edge_far = lax.optimization_barrier((inner_far, edge_far))
     panel, gram = call(
         gram_kernel,
         "gram",
         (shape(probes, blocks * 256), shape(probes // 2, 2 * probes)),
-        [SMEM] + [VMEM] * 4,
-    )(where, inner_chip, inner_far, edge_chip, edge_far)
+        [SMEM] + [VMEM] * 5,
+    )(where, inner_gram, inner_chip, inner_far, edge_chip, edge_far)
     panel, gram_other = lax.optimization_barrier((panel, swap_probes(gram, 1)))
     grams = call(copies_kernel, "copies", shape(ring, probes // 2, 2 * probes), [VMEM] * 2)(
         gram, gram_other

time: 41.9 us -> 41.6 us (level)
  transfers between devices with their start and end apart: 10 -> 10, of which waited for: 4 -> 5; matrix products, arithmetic and copies ran while one was open for 0% -> 0% of each run, Pallas kernels for 16% -> 16%
where the time goes in v7:
time: 41.6 us; the launch traced here: 41.4 us
  starting transfers between devices  12.6 us (30%)
  Pallas kernels  11.4 us (27%)
  blocking collectives  10.5 us (25%)
  waiting for transfers between devices  6.21 us (15%)
  between operations  0.73 us (2%)
    all_to_all x1, blocking collectives, body(): grams = lax.all_to_all(grams, 'lon', 0, 0, tiled=True)  10.5 us
    ppermute x7, starting transfers between devices, swap_probes(): lax.ppermute(value, 'probe', [(i, i ^ step) for i in range(lax.axis_size(...  6.49 us
    pallas_call x1, Pallas kernels, body(): call(interior_kernel, 'interior', (shape(count, (blocks - 2) * 256), shap...  4.47 us
    ppermute x7, waiting for transfers between devices, swap_probes(): lax.ppermute(value, 'probe', [(i, i ^ step) for i in range(lax.axis_size(...  4.27 us
    pallas_call x1, Pallas kernels, body(): call(factor_kernel, 'factor', (shape(blocks, count, 512), shape(probes, p...  3.14 us
    ppermute x1, starting transfers between devices, body(): from_high = lax.ppermute(pack_down, 'lon', down)  3.1 us
    ppermute x1, starting transfers between devices, body(): from_low = lax.ppermute(pack_up, 'lon', up)  2.99 us
    ppermute x1, waiting for transfers between devices, body(): lax.ppermute(share, ('lon', 'probe'), [(i * size + p, (up, down)[p & 1][i...  1.93 us
  transfers between devices with their start and end apart: 10, of which 5 were waited for; matrix products, arithmetic and copies ran while one was open for 0% of the time, Pallas kernels for 16%

profile of v7, /device:TPU:0, one launch (start us, length us, event | category | flops | bytes accessed | tf_op | source)
XLA Modules:
  0.0 41.4 jit_solution(18357857157807171905)
XLA Ops:
  0.6 1.1 %pack.1 = (f32[10,8,256]{2,1,0:T(8,128)S(1)}, f32[9,8,256]{2,1,0:T(8,128)S(1)}, f32[2,24,8,256]{3,2,1,0:T(8,128)S(1)}, f32[24,8,256]{2,1,0:T(8,128)S(1)}) custom-call(f32[2,24,8,256]{3,2,1,0:T(8,128)} %winds_hbm.1, f32[24,8,256]{2,1,0:T(8,128)} %obs_hbm.1), custom_call_target="tpu_custom_call" | custom-call | flops 1000000 | bytes 100000 | tf_op jit(solution)/shard_map/pack/pallas_call | solution.py:619
  1.7 3.0 %collective-permute-start.2 = (f32[10,8,256]{2,1,0:T(8,128)S(1)}, f32[10,8,256]{2,1,0:T(8,128)S(1)}, u32[]{:S(2)}, u32[]{:S(2)}) collective-permute-start(f32[10,8,256]{2,1,0:T(8,128)S(1)} %get-tuple-element.25), channel_id=1, source_target_pairs={{0,4},{4,8},{8,12},{12,16},{16,20},{20,24},{24,28},{28,0},{1,5},{5... | collective-permute-start | bytes 245768 | tf_op jit(solution)/shard_map/ppermute | solution.py:631
  4.7 3.1 %collective-permute-start.3 = (f32[9,8,256]{2,1,0:T(8,128)S(1)}, f32[9,8,256]{2,1,0:T(8,128)S(1)}, u32[]{:S(2)}, u32[]{:S(2)}) collective-permute-start(f32[9,8,256]{2,1,0:T(8,128)S(1)} %get-tuple-element.26), channel_id=1, source_target_pairs={{0,28},{4,0},{8,4},{12,8},{16,12},{20,16},{24,20},{28,24},{1,29},{... | collective-permute-start | bytes 221192 | tf_op jit(solution)/shard_map/ppermute | solution.py:632
  7.8 4.5 %interior.1 = (f32[16,1024]{1,0:T(8,128)S(1)}, f32[16,1024]{1,0:T(8,128)S(1)}, f32[16,512]{1,0:T(8,128)S(1)}, f32[16,512]{1,0:T(8,128)S(1)}, f32[16,8,8,256]{3,2,1,0:T(8,128)S(1)}) custom-call(s32[1]{0:T(128)} %bitcast.where, f32[2,24,8,256]{3,2,1,0:T(8,128)S(1)} %get-tuple-element.21.winds, f32[24,8,256]{2,1,0:T(8,128)S(1)} %get-tuple-element.22.obs, ...), custom_call_target="tpu_custom_call" | custom-call | flops 1000000 | bytes 100000 | tf_op jit(solution)/shard_map/interior/pallas_call | solution.py:633
  12.3 0.1 collective-permute-start
  12.4 0.0 collective-permute-done.3.from_high
  12.4 0.0 collective-permute-done.2.from_low
  12.4 0.9 %share.1 = (f32[16,512]{1,0:T(8,128)S(1)}, f32[16,512]{1,0:T(8,128)S(1)}) custom-call(s32[1]{0:T(128)} %bitcast.where, f32[2,24,8,256]{3,2,1,0:T(8,128)S(1)} %get-tuple-element.21.winds, f32[24,8,256]{2,1,0:T(8,128)S(1)} %get-tuple-element.22.obs, f32[10,8,256]{2,1,0:T(8,128)S(1)} %collective-permute-done.2.from_low, ...), custom_call_target="tpu_custom_call" | custom-call | flops 1000000 | bytes 100000 | tf_op jit(solution)/shard_map/share/pallas_call | solution.py:657
  13.3 0.5 %collective-permute-start.4 = (f32[16,512]{1,0:T(8,128)S(1)}, f32[16,512]{1,0:T(8,128)S(1)}, u32[]{:S(2)}, u32[]{:S(2)}) collective-permute-start(f32[16,512]{1,0:T(8,128)S(1)} %get-tuple-element.31), channel_id=1, source_target_pairs={{0,1},{1,0},{2,3},{3,2},{4,5},{5,4},{6,7},{7,6},{8,9},{9,8},{10,11... | collective-permute-start | bytes 98312 | tf_op jit(solution)/shard_map/ppermute | solution.py:604
  13.9 0.9 %collective-permute-done.4 = f32[16,512]{1,0:T(8,128)S(1)} collective-permute-done((f32[16,512]{1,0:T(8,128)S(1)}, f32[16,512]{1,0:T(8,128)S(1)}, u32[]{:S(2)}, u32[]{:S(2)}) %collective-permute-start.4) | collective-permute-done | bytes 32800 | tf_op jit(solution)/shard_map/ppermute | solution.py:604
  14.7 0.0 collective-permute-start.6
  14.7 1.0 %rest.1 = (f32[16,512]{1,0:T(8,128)S(1)}, f32[16,512]{1,0:T(8,128)S(1)}) custom-call(s32[1]{0:T(128)} %bitcast.where, f32[2,24,8,256]{3,2,1,0:T(8,128)S(1)} %get-tuple-element.21.winds, f32[24,8,256]{2,1,0:T(8,128)S(1)} %get-tuple-element.22.obs, f32[10,8,256]{2,1,0:T(8,128)S(1)} %collective-permute-done.2.from_low, ...), custom_call_target="tpu_custom_call" | custom-call | flops 1000000 | bytes 100000 | tf_op jit(solution)/shard_map/rest/pallas_call | solution.py:671
  15.8 2.3 %collective-permute-start.5 = (f32[16,512]{1,0:T(8,128)S(1)}, f32[16,512]{1,0:T(8,128)S(1)}, u32[]{:S(2)}, u32[]{:S(2)}) collective-permute-start(f32[16,512]{1,0:T(8,128)S(1)} %get-tuple-element.33), channel_id=1, source_target_pairs={{0,1},{1,0},{2,3},{3,2},{4,5},{5,4},{6,7},{7,6},{8,9},{9,8},{10,11... | collective-permute-start | bytes 98312 | tf_op jit(solution)/shard_map/ppermute | solution.py:604
  18.0 0.0 collective-permute-done
  18.0 1.7 %collective-permute-start.1 = (f32[32,1024]{1,0:T(8,128)S(1)}, f32[32,1024]{1,0:T(8,128)S(1)}, u32[]{:S(2)}, u32[]{:S(2)}) collective-permute-start(f32[32,1024]{1,0:T(8,128)S(1)} %constant_dynamic-update-slice_fusion.chip.inner_chip), channel_id=1, source_target_pairs={{0,2},{1,3},{2,0},{3,1},{4,6},{5,7},{6,4},{7,5},{8,10},{9,11},{10,... | collective-permute-start | bytes 393224 | tf_op jit(solution)/shard_map/ppermute | solution.py:604
  19.8 0.0 collective-permute-done.5
  19.8 1.9 %collective-permute-done.6 = f32[32,512]{1,0:T(8,128)S(1)} collective-permute-done((f32[32,512]{1,0:T(8,128)S(1)}, f32[32,512]{1,0:T(8,128)S(1)}, u32[]{:S(2)}, u32[]{:S(2)}) %collective-permute-start.6) | collective-permute-done | bytes 65568 | tf_op jit(solution)/shard_map/ppermute | solution.py:662
  21.7 1.7 %collective-permute-start.7 = (f32[32,512]{1,0:T(8,128)S(1)}, f32[32,512]{1,0:T(8,128)S(1)}, u32[]{:S(2)}, u32[]{:S(2)}) collective-permute-start(f32[32,512]{1,0:T(8,128)S(1)} %maximum_add_fusion.edge_chip), channel_id=1, source_target_pairs={{0,2},{1,3},{2,0},{3,1},{4,6},{5,7},{6,4},{7,5},{8,10},{9,11},{10,... | collective-permute-start | bytes 196616 | tf_op jit(solution)/shard_map/ppermute | solution.py:604
  23.4 0.8 %collective-permute-done.1.far.inner_far = f32[32,1024]{1,0:T(8,128)S(1)} collective-permute-done((f32[32,1024]{1,0:T(8,128)S(1)}, f32[32,1024]{1,0:T(8,128)S(1)}, u32[]{:S(2)}, u32[]{:S(2)}) %collective-permute-start.1) | collective-permute-done | bytes 131104 | tf_op jit(solution)/shard_map/ppermute | solution.py:604
  24.2 0.4 inner_gram.1
  24.6 1.4 %collective-permute-done.7.edge_far = f32[32,512]{1,0:T(8,128)S(1)} collective-permute-done((f32[32,512]{1,0:T(8,128)S(1)}, f32[32,512]{1,0:T(8,128)S(1)}, u32[]{:S(2)}, u32[]{:S(2)}) %collective-permute-start.7) | collective-permute-done | bytes 65568 | tf_op jit(solution)/shard_map/ppermute | solution.py:604
  26.0 0.4 gram.1
  26.4 0.0 collective-permute-start.8
  26.4 1.2 %collective-permute-done.8.other = f32[32,128]{1,0:T(8,128)S(1)} collective-permute-done((f32[32,128]{1,0:T(8,128)S(1)}, f32[32,128]{1,0:T(8,128)S(1)}, u32[]{:S(2)}, u32[]{:S(2)}) %collective-permute-start.8) | collective-permute-done | bytes 16416 | tf_op jit(solution)/shard_map/ppermute | solution.py:604
  27.6 0.2 collective-permute-start.9
  27.8 10.5 %all_to_all.5.grams = f32[8,32,128]{2,1,0:T(8,128)S(1)} all-to-all(f32[8,32,128]{2,1,0:T(8,128)S(1)} %copies.1), channel_id=1, replica_groups=mesh['lon'=8,'probe'=4] {'lon'}, dimensions={0} | all-to-all | bytes 262144 | tf_op jit(solution)/shard_map/all_to_all | solution.py:695
  38.2 0.0 collective-permute-done.9.panel_other
  38.2 3.1 %factor.1 = (f32[6,16,512]{2,1,0:T(8,128)}, f32[64,64]{1,0:T(8,128)}) custom-call(s32[1]{0:T(128)} %bitcast.where, f32[8,32,128]{2,1,0:T(8,128)S(1)} %all_to_all.5.grams, f32[64,1536]{1,0:T(8,128)S(1)} %get-tuple-element.37.panel, f32[64,1536]{1,0:T(8,128)S(1)} %collective-permute-done.9.panel_other), custom_call_target="tpu_custom_call" | custom-call | flops 1000000 | bytes 100000 | tf_op jit(solution)/shard_map/factor/pallas_call | solution.py:696
  (6 shorter events, 0.0 us)
Async XLA Ops:
  1.7 10.7 %collective-permute-start.2 = (f32[10,8,256]{2,1,0:T(8,128)S(1)}, f32[10,8,256]{2,1,0:T(8,128)S(1)}, u32[]{:S(2)}, u32[]{:S(2)}) collective-permute-start(f32[10,8,256]{2,1,0:T(8,128)S(1)} %get-tuple-element.25), channel_id=1, source_target_pairs={{0,4},{4,8},{8,12},{12,16},{16,20},{20,24},{24,28},{28,0},{1,5},{5... | collective-permute-start | bytes 245768 | tf_op jit(solution)/shard_map/ppermute | solution.py:631
  4.7 7.7 %collective-permute-start.3 = (f32[9,8,256]{2,1,0:T(8,128)S(1)}, f32[9,8,256]{2,1,0:T(8,128)S(1)}, u32[]{:S(2)}, u32[]{:S(2)}) collective-permute-start(f32[9,8,256]{2,1,0:T(8,128)S(1)} %get-tuple-element.26), channel_id=1, source_target_pairs={{0,28},{4,0},{8,4},{12,8},{16,12},{20,16},{24,20},{28,24},{1,29},{... | collective-permute-start | bytes 221192 | tf_op jit(solution)/shard_map/ppermute | solution.py:632
  12.3 5.7 %collective-permute-start = (f32[16,1024]{1,0:T(8,128)S(1)}, f32[16,1024]{1,0:T(8,128)S(1)}, u32[]{:S(2)}, u32[]{:S(2)}) collective-permute-start(f32[16,1024]{1,0:T(8,128)S(1)} %get-tuple-element.24), channel_id=1, source_target_pairs={{0,1},{1,0},{2,3},{3,2},{4,5},{5,4},{6,7},{7,6},{8,9},{9,8},{10,11... | collective-permute-start | bytes 196616 | tf_op jit(solution)/shard_map/ppermute | solution.py:604
  13.3 1.4 %collective-permute-start.4 = (f32[16,512]{1,0:T(8,128)S(1)}, f32[16,512]{1,0:T(8,128)S(1)}, u32[]{:S(2)}, u32[]{:S(2)}) collective-permute-start(f32[16,512]{1,0:T(8,128)S(1)} %get-tuple-element.31), channel_id=1, source_target_pairs={{0,1},{1,0},{2,3},{3,2},{4,5},{5,4},{6,7},{7,6},{8,9},{9,8},{10,11... | collective-permute-start | bytes 98312 | tf_op jit(solution)/shard_map/ppermute | solution.py:604
  14.7 7.0 %collective-permute-start.6 = (f32[32,512]{1,0:T(8,128)S(1)}, f32[32,512]{1,0:T(8,128)S(1)}, u32[]{:S(2)}, u32[]{:S(2)}) collective-permute-start(f32[32,512]{1,0:T(8,128)S(1)} %constant_dynamic-update-slice_fusion.2.after), channel_id=1, source_target_pairs={{0,4},{1,29},{2,6},{3,31},{4,8},{5,1},{6,10},{7,3},{8,12},{9,5},{1... | collective-permute-start | bytes 196616 | tf_op jit(solution)/shard_map/ppermute | solution.py:662
  15.8 4.0 %collective-permute-start.5 = (f32[16,512]{1,0:T(8,128)S(1)}, f32[16,512]{1,0:T(8,128)S(1)}, u32[]{:S(2)}, u32[]{:S(2)}) collective-permute-start(f32[16,512]{1,0:T(8,128)S(1)} %get-tuple-element.33), channel_id=1, source_target_pairs={{0,1},{1,0},{2,3},{3,2},{4,5},{5,4},{6,7},{7,6},{8,9},{9,8},{10,11... | collective-permute-start | bytes 98312 | tf_op jit(solution)/shard_map/ppermute | solution.py:604
  18.0 6.2 %collective-permute-start.1 = (f32[32,1024]{1,0:T(8,128)S(1)}, f32[32,1024]{1,0:T(8,128)S(1)}, u32[]{:S(2)}, u32[]{:S(2)}) collective-permute-start(f32[32,1024]{1,0:T(8,128)S(1)} %constant_dynamic-update-slice_fusion.chip.inner_chip), channel_id=1, source_target_pairs={{0,2},{1,3},{2,0},{3,1},{4,6},{5,7},{6,4},{7,5},{8,10},{9,11},{10,... | collective-permute-start | bytes 393224 | tf_op jit(solution)/shard_map/ppermute | solution.py:604
  21.7 4.3 %collective-permute-start.7 = (f32[32,512]{1,0:T(8,128)S(1)}, f32[32,512]{1,0:T(8,128)S(1)}, u32[]{:S(2)}, u32[]{:S(2)}) collective-permute-start(f32[32,512]{1,0:T(8,128)S(1)} %maximum_add_fusion.edge_chip), channel_id=1, source_target_pairs={{0,2},{1,3},{2,0},{3,1},{4,6},{5,7},{6,4},{7,5},{8,10},{9,11},{10,... | collective-permute-start | bytes 196616 | tf_op jit(solution)/shard_map/ppermute | solution.py:604
  26.4 1.2 %collective-permute-start.8 = (f32[32,128]{1,0:T(8,128)S(1)}, f32[32,128]{1,0:T(8,128)S(1)}, u32[]{:S(2)}, u32[]{:S(2)}) collective-permute-start(f32[32,128]{1,0:T(8,128)S(1)} %get-tuple-element.34.mine), channel_id=1, source_target_pairs={{0,1},{1,0},{2,3},{3,2},{4,5},{5,4},{6,7},{7,6},{8,9},{9,8},{10,11... | collective-permute-start | bytes 49160 | tf_op jit(solution)/shard_map/ppermute | solution.py:604
  27.6 10.7 %collective-permute-start.9 = (f32[64,1536]{1,0:T(8,128)S(1)}, f32[64,1536]{1,0:T(8,128)S(1)}, u32[]{:S(2)}, u32[]{:S(2)}) collective-permute-start(f32[64,1536]{1,0:T(8,128)S(1)} %get-tuple-element.37.panel), channel_id=1, source_target_pairs={{0,1},{1,0},{2,3},{3,2},{4,5},{5,4},{6,7},{7,6},{8,9},{9,8},{10,11... | collective-permute-start | bytes 1179656 | tf_op jit(solution)/shard_map/ppermute | solution.py:604

commit v8 on v7

--- a/solution.py
+++ b/solution.py
@@ -256,12 +256,16 @@
     return copies
 
 
-def pack_kernel(winds_hbm, obs_hbm, up, down, winds, obs, sems):
+def pack_kernel(
+    where, winds_hbm, obs_hbm, field_hbm, up, down, winds, obs, lent, sems
+):
     lons = obs.shape[0]
+    outer = field_hbm.at[:, pl.ds(lax.rem(where[0], 2) * (lons - 4), 4)]
     copies = fetch_all(
         [
             pltpu.make_async_copy(winds_hbm, winds, sems.at[0]),
             pltpu.make_async_copy(obs_hbm, obs, sems.at[1]),
+            pltpu.make_async_copy(outer, lent, sems.at[2]),
         ]
     )
     for copy in copies:
@@ -285,7 +289,7 @@
 
 
 def interior_kernel(
-    where, winds, obs, field_hbm, mine, other, part_low, part_high, sides,
+    where, winds, obs, field_hbm, after, mine, other, part_low, part_high, sides,
     coef, weights, sums, field, sems,
 ):
     count, lons = field.shape[0], field.shape[1]
@@ -369,8 +373,9 @@
         copy.wait()
 
 
-def edge_sums(winds, obs, from_low, from_high, field, coef, weights, sums, spans, jobs, put):
-    count, lons = field.shape[0], obs.shape[0]
+def edge_sums(winds, obs, from_low, from_high, sources, coef, weights, sums, spans, jobs, put):
+    count, lons = sources[0][0].shape[0], obs.shape[0]
+    total = count * len(sources)
     lanes = Lanes()
 
     def wind(which, lon):
@@ -405,51 +410,57 @@
         for (r, part), value in result.items():
             store(weights, value, n, part, r + 4)
 
-    def sweep(step, carry):
+    def sweep(source, step, carry):
+        field, index = sources[source]
         for n, (base, first, last) in enumerate(jobs):
 
             def write(probe, part, h, value):
-                row = pl.multiple_of((n * count + probe) * 8, 8)
+                row = pl.multiple_of((n * total + source * count + probe) * 8, 8)
                 sums[2 * part + h, pl.ds(row, 8), :] = value
-
-            def read(probe, r):
-                lon = base + r
-                return halves(field, probe, lon if lon < 4 else lon - (lons - 8))
 
             apply_weights(
                 lanes,
                 weight_keys(first, last),
                 lambda r, part: halves(weights, n, part, r + 4),
-                read,
+                lambda probe, r: halves(field, probe, index(base + r)),
                 write,
                 [step * EDGE_GROUP + k for k in range(EDGE_GROUP)],
             )
         return carry
 
-    lax.fori_loop(0, count // EDGE_GROUP, sweep, 0)
-    pool_into(lanes, sums, len(jobs), count, put)
+    for source in range(len(sources)):
+        lax.fori_loop(0, count // EDGE_GROUP, functools.partial(sweep, source), 0)
+    pool_into(lanes, sums, len(jobs), total, put)
 
 
 def share_kernel(
-    where, winds, obs, from_low, from_high, field, mine, other, coef, weights, sums
+    where, winds, obs, from_low, from_high, field, borrowed, out, coef, weights, sums
 ):
     lons = obs.shape[0]
-    values = {}
+    core = lax.rem(where[0], 2)
 
     def put(n, pair, value):
-        values[1 - n, pair] = value
-
-    edge_sums(
-        winds, obs, from_low, from_high, field, coef, weights, sums,
-        ((-3, 3), (lons - 3, lons + 3)),
-        ((-4, 4, 7), (lons, -4, -1)),
-        put,
-    )
-    split_by_core(where, values, mine, other)
+        out[:, pair * HALF : (pair + 1) * HALF] = value
+
+    @pl.when(core == 0)
+    def _():
+        edge_sums(
+            winds, obs, from_low, from_high,
+            ((field, lambda lon: lon - (lons - 8)), (borrowed, lambda lon: lon - (lons - 4))),
+            coef, weights, sums, ((lons - 3, lons + 3),), ((lons, -4, -1),), put,
+        )
+
+    @pl.when(core == 1)
+    def _():
+        edge_sums(
+            winds, obs, from_low, from_high,
+            ((field, lambda lon: lon), (borrowed, lambda lon: lon)),
+            coef, weights, sums, ((-3, 3),), ((-4, 4, 7),), put,
+        )
 
 
 def rest_kernel(
-    where, winds, obs, from_low, from_high, field, part_low, part_high, after,
+    where, winds, obs, from_low, from_high, field, part_low, part_high, after, after_inner,
     mine, other, coef, weights, sums,
 ):
     lons = obs.shape[0]
@@ -460,7 +471,9 @@
         values[n, pair] = value + (part_low, part_high)[n][:, columns]
 
     edge_sums(
-        winds, obs, from_low, from_high, field, coef, weights, sums,
+        winds, obs, from_low, from_high,
+        ((field, lambda lon: lon if lon < 4 else lon - (lons - 8)),),
+        coef, weights, sums,
         ((-2, 4), (lons - 5, lons + 1)),
         ((0, 0, 1), (lons - 4, 0, 3)),
         put,
@@ -616,7 +629,7 @@
     increments, winds, obs_weight = (
         pltpu.with_memory_space_constraint(x, pltpu.HBM) for x in (increments, winds, obs_weight)
     )
-    pack_up, pack_down, winds, obs_weight = call(
+    pack_up, pack_down, winds, obs_weight, lent = call(
         pack_kernel,
         "pack",
         (
@@ -624,10 +637,12 @@
             shape(9, levels, lats),
             shape(2, lons, levels, lats),
             shape(lons, levels, lats),
+            shape(count, 4, levels, lats),
         ),
-        [HBM, HBM],
-        [dma((2,))],
-    )(winds, obs_weight)
+        [SMEM, HBM, HBM, HBM],
+        [dma((3,))],
+    )(where, winds, obs_weight, increments)
+    borrowed = swap_probes(lent, 1)
     from_low = lax.ppermute(pack_up, "lon", up)
     from_high = lax.ppermute(pack_down, "lon", down)
     inner, inner_other, part_low, part_high, sides = call(
@@ -640,7 +655,7 @@
             shape(count, 512),
             shape(count, 8, levels, lats),
         ),
-        [SMEM, VMEM, VMEM, HBM],
+        [SMEM, VMEM, VMEM, HBM, ANY],
         [
             pltpu.VMEM((PLANES, lons, levels, lats), F32),
             pltpu.VMEM((blocks, 3, 12, levels, lats), F32),
@@ -648,16 +663,15 @@
             pltpu.VMEM((count, lons, levels, lats), F32),
             dma((3,)),
         ],
-    )(where, winds, obs_weight, increments)
+    )(where, winds, obs_weight, increments, borrowed)
     edge_scratch = [
         pltpu.VMEM((PLANES, 14, levels, lats), F32),
         pltpu.VMEM((2, 3, 12, levels, lats), F32),
         pltpu.VMEM((6, 2 * count * 8, HALF), F32),
     ]
-    share, share_other = call(
-        share_kernel, "share", (shape(count, 512),) * 2, [SMEM] + [VMEM] * 5, edge_scratch
-    )(where, winds, obs_weight, from_low, from_high, sides)
-    share = jnp.concatenate([share, swap_probes(share_other, 1)], axis=0)
+    share = call(
+        share_kernel, "share", shape(2 * count, 512), [SMEM] + [VMEM] * 6, edge_scratch
+    )(where, winds, obs_weight, from_low, from_high, sides, borrowed)
     size = lax.axis_size("probe")
     arrived = lax.ppermute(
         share,
@@ -668,10 +682,10 @@
             for p in range(size)
         ],
     )
+    inner_chip = jnp.concatenate([inner, swap_probes(inner_other, 1)], axis=0)
     rest, rest_other = call(
-        rest_kernel, "rest", (shape(count, 512),) * 2, [SMEM] + [VMEM] * 7 + [ANY], edge_scratch
-    )(where, winds, obs_weight, from_low, from_high, sides, part_low, part_high, share)
-    inner_chip = jnp.concatenate([inner, swap_probes(inner_other, 1)], axis=0)
+        rest_kernel, "rest", (shape(count, 512),) * 2, [SMEM] + [VMEM] * 7 + [ANY, ANY], edge_scratch
+    )(where, winds, obs_weight, from_low, from_high, sides, part_low, part_high, share, inner_chip)
     inner_far = swap_probes(inner_chip, 2)
     inner_gram = call(
         inner_gram_kernel,

time: 41.6 us -> 40.5 us (0.974)
  starting transfers between devices: 12.6 us -> 11.6 us
    ppermute x7, starting transfers between devices: 6.49 us -> 5.91 us  [swap_probes(): lax.ppermute(value, 'probe', [(i, i ^ step) for i in range(lax.axis_size(...]
    ppermute x7, waiting for transfers between devices: 4.27 us -> 3.73 us  [swap_probes(): lax.ppermute(value, 'probe', [(i, i ^ step) for i in range(lax.axis_size(...]
    ppermute x1, starting transfers between devices: 2.99 us -> 2.55 us  [body(): from_low = lax.ppermute(pack_up, 'lon', up)]
  transfers between devices with their start and end apart: 10 -> 10, of which waited for: 5 -> 5; matrix products, arithmetic and copies ran while one was open for 0% -> 0% of each run, Pallas kernels for 16% -> 17%
where the time goes in v8:
time: 40.5 us; the launch traced here: 40.3 us
  starting transfers between devices  11.6 us (29%)
  Pallas kernels  11.5 us (28%)
  blocking collectives  10.5 us (26%)
  waiting for transfers between devices  5.95 us (15%)
  between operations  0.71 us (2%)
    all_to_all x1, blocking collectives, body(): grams = lax.all_to_all(grams, 'lon', 0, 0, tiled=True)  10.5 us
    ppermute x7, starting transfers between devices, swap_probes(): lax.ppermute(value, 'probe', [(i, i ^ step) for i in range(lax.axis_size(...  5.91 us
    pallas_call x1, Pallas kernels, body(): call(interior_kernel, 'interior', (shape(count, (blocks - 2) * 256), shap...  4.48 us
    ppermute x7, waiting for transfers between devices, swap_probes(): lax.ppermute(value, 'probe', [(i, i ^ step) for i in range(lax.axis_size(...  3.73 us
    pallas_call x1, Pallas kernels, body(): call(factor_kernel, 'factor', (shape(blocks, count, 512), shape(probes, p...  3.14 us
    ppermute x1, starting transfers between devices, body(): from_high = lax.ppermute(pack_down, 'lon', down)  3.12 us
    ppermute x1, starting transfers between devices, body(): from_low = lax.ppermute(pack_up, 'lon', up)  2.55 us
    ppermute x1, waiting for transfers between devices, body(): lax.ppermute(share, ('lon', 'probe'), [(i * size + p, (up, down)[p & 1][i...  2.22 us
  transfers between devices with their start and end apart: 10, of which 5 were waited for; matrix products, arithmetic and copies ran while one was open for 0% of the time, Pallas kernels for 17%

profile of v8, /device:TPU:0, one launch (start us, length us, event | category | flops | bytes accessed | tf_op | source)
XLA Modules:
  0.0 40.3 jit_solution(7043128490531671241)
XLA Ops:
  0.6 1.3 %pack.1 = (f32[10,8,256]{2,1,0:T(8,128)S(1)}, f32[9,8,256]{2,1,0:T(8,128)S(1)}, f32[2,24,8,256]{3,2,1,0:T(8,128)S(1)}, f32[24,8,256]{2,1,0:T(8,128)S(1)}, f32[16,4,8,256]{3,2,1,0:T(8,128)S(1)}) custom-call(s32[1]{0:T(128)} %bitcast.where, f32[2,24,8,256]{3,2,1,0:T(8,128)} %winds_hbm.1, f32[24,8,256]{2,1,0:T(8,128)} %obs_hbm.1, f32[16,24,8,256]{3,2,1,0:T(8,128)} %field_hbm.3), custom_call_target="tpu_custom_call" | custom-call | flops 1000000 | bytes 100000 | tf_op jit(solution)/shard_map/pack/pallas_call | solution.py:632
  1.9 0.5 %collective-permute-start = (f32[16,4,8,256]{3,2,1,0:T(8,128)S(1)}, f32[16,4,8,256]{3,2,1,0:T(8,128)S(1)}, u32[]{:S(2)}, u32[]{:S(2)}) collective-permute-start(f32[16,4,8,256]{3,2,1,0:T(8,128)S(1)} %get-tuple-element.22), channel_id=1, source_target_pairs={{0,1},{1,0},{2,3},{3,2},{4,5},{5,4},{6,7},{7,6},{8,9},{9,8},{10,11... | collective-permute-start | bytes 1572872 | tf_op jit(solution)/shard_map/ppermute | solution.py:617
  2.5 2.6 %collective-permute-start.3 = (f32[10,8,256]{2,1,0:T(8,128)S(1)}, f32[10,8,256]{2,1,0:T(8,128)S(1)}, u32[]{:S(2)}, u32[]{:S(2)}) collective-permute-start(f32[10,8,256]{2,1,0:T(8,128)S(1)} %get-tuple-element.25), channel_id=1, source_target_pairs={{0,4},{4,8},{8,12},{12,16},{16,20},{20,24},{24,28},{28,0},{1,5},{5... | collective-permute-start | bytes 245768 | tf_op jit(solution)/shard_map/ppermute | solution.py:646
  5.0 3.1 %collective-permute-start.4 = (f32[9,8,256]{2,1,0:T(8,128)S(1)}, f32[9,8,256]{2,1,0:T(8,128)S(1)}, u32[]{:S(2)}, u32[]{:S(2)}) collective-permute-start(f32[9,8,256]{2,1,0:T(8,128)S(1)} %get-tuple-element.26), channel_id=1, source_target_pairs={{0,28},{4,0},{8,4},{12,8},{16,12},{20,16},{24,20},{28,24},{1,29},{... | collective-permute-start | bytes 221192 | tf_op jit(solution)/shard_map/ppermute | solution.py:647
  8.1 0.0 collective-permute-done.after.borrowed
  8.1 4.5 %interior.1 = (f32[16,1024]{1,0:T(8,128)S(1)}, f32[16,1024]{1,0:T(8,128)S(1)}, f32[16,512]{1,0:T(8,128)S(1)}, f32[16,512]{1,0:T(8,128)S(1)}, f32[16,8,8,256]{3,2,1,0:T(8,128)S(1)}) custom-call(s32[1]{0:T(128)} %bitcast.where, f32[2,24,8,256]{3,2,1,0:T(8,128)S(1)} %get-tuple-element.20.winds, f32[24,8,256]{2,1,0:T(8,128)S(1)} %get-tuple-element.21.obs, ...), custom_call_target="tpu_custom_call" | custom-call | flops 1000000 | bytes 100000 | tf_op jit(solution)/shard_map/interior/pallas_call | solution.py:648
  12.6 0.1 collective-permute-start.1
  12.8 0.0 collective-permute-done.4.from_high
  12.8 0.0 collective-permute-done.3.from_low
  12.8 0.8 %share.1.after = f32[32,512]{1,0:T(8,128)S(1)} custom-call(s32[1]{0:T(128)} %bitcast.where, f32[2,24,8,256]{3,2,1,0:T(8,128)S(1)} %get-tuple-element.20.winds, f32[24,8,256]{2,1,0:T(8,128)S(1)} %get-tuple-element.21.obs, f32[10,8,256]{2,1,0:T(8,128)S(1)} %collective-permute-done.3.from_low, f32[9,8,256]{2,1,0:T(8,128)S(1)} %collective-permute-done.4.from_high, ...), custom_call_target="tpu_custom_call" | custom-call | flops 1000000 | bytes 100000 | tf_op jit(solution)/shard_map/share/pallas_call | solution.py:672
  13.6 0.1 collective-permute-start.6
  13.7 0.3 collective-permute-done.1
  13.9 1.0 %rest.1 = (f32[16,512]{1,0:T(8,128)S(1)}, f32[16,512]{1,0:T(8,128)S(1)}) custom-call(s32[1]{0:T(128)} %bitcast.where, f32[2,24,8,256]{3,2,1,0:T(8,128)S(1)} %get-tuple-element.20.winds, f32[24,8,256]{2,1,0:T(8,128)S(1)} %get-tuple-element.21.obs, f32[10,8,256]{2,1,0:T(8,128)S(1)} %collective-permute-done.3.from_low, ...), custom_call_target="tpu_custom_call" | custom-call | flops 1000000 | bytes 100000 | tf_op jit(solution)/shard_map/rest/pallas_call | solution.py:686
  15.0 1.9 %collective-permute-start.5 = (f32[16,512]{1,0:T(8,128)S(1)}, f32[16,512]{1,0:T(8,128)S(1)}, u32[]{:S(2)}, u32[]{:S(2)}) collective-permute-start(f32[16,512]{1,0:T(8,128)S(1)} %get-tuple-element.31), channel_id=1, source_target_pairs={{0,1},{1,0},{2,3},{3,2},{4,5},{5,4},{6,7},{7,6},{8,9},{9,8},{10,11... | collective-permute-start | bytes 98312 | tf_op jit(solution)/shard_map/ppermute | solution.py:617
  16.9 1.5 %collective-permute-start.2 = (f32[32,1024]{1,0:T(8,128)S(1)}, f32[32,1024]{1,0:T(8,128)S(1)}, u32[]{:S(2)}, u32[]{:S(2)}) collective-permute-start(f32[32,1024]{1,0:T(8,128)S(1)} %constant_dynamic-update-slice_fusion.chip.after_inner.inner_chip), channel_id=1, source_target_pairs={{0,2},{1,3},{2,0},{3,1},{4,6},{5,7},{6,4},{7,5},{8,10},{9,11},{10,... | collective-permute-start | bytes 393224 | tf_op jit(solution)/shard_map/ppermute | solution.py:617
  18.4 2.2 %collective-permute-done.6 = f32[32,512]{1,0:T(8,128)S(1)} collective-permute-done((f32[32,512]{1,0:T(8,128)S(1)}, f32[32,512]{1,0:T(8,128)S(1)}, u32[]{:S(2)}, u32[]{:S(2)}) %collective-permute-start.6) | collective-permute-done | bytes 65568 | tf_op jit(solution)/shard_map/ppermute | solution.py:676
  20.6 0.0 collective-permute-done.5
  20.6 1.6 %collective-permute-start.7 = (f32[32,512]{1,0:T(8,128)S(1)}, f32[32,512]{1,0:T(8,128)S(1)}, u32[]{:S(2)}, u32[]{:S(2)}) collective-permute-start(f32[32,512]{1,0:T(8,128)S(1)} %maximum_add_fusion.edge_chip), channel_id=1, source_target_pairs={{0,2},{1,3},{2,0},{3,1},{4,6},{5,7},{6,4},{7,5},{8,10},{9,11},{10,... | collective-permute-start | bytes 196616 | tf_op jit(solution)/shard_map/ppermute | solution.py:617
  22.3 0.8 %collective-permute-done.2.far.inner_far = f32[32,1024]{1,0:T(8,128)S(1)} collective-permute-done((f32[32,1024]{1,0:T(8,128)S(1)}, f32[32,1024]{1,0:T(8,128)S(1)}, u32[]{:S(2)}, u32[]{:S(2)}) %collective-permute-start.2) | collective-permute-done | bytes 131104 | tf_op jit(solution)/shard_map/ppermute | solution.py:617
  23.1 0.4 inner_gram.1
  23.5 1.5 %collective-permute-done.7.edge_far = f32[32,512]{1,0:T(8,128)S(1)} collective-permute-done((f32[32,512]{1,0:T(8,128)S(1)}, f32[32,512]{1,0:T(8,128)S(1)}, u32[]{:S(2)}, u32[]{:S(2)}) %collective-permute-start.7) | collective-permute-done | bytes 65568 | tf_op jit(solution)/shard_map/ppermute | solution.py:617
  25.0 0.4 gram.1
  25.3 0.0 collective-permute-start.8
  25.4 1.2 %collective-permute-done.8.other = f32[32,128]{1,0:T(8,128)S(1)} collective-permute-done((f32[32,128]{1,0:T(8,128)S(1)}, f32[32,128]{1,0:T(8,128)S(1)}, u32[]{:S(2)}, u32[]{:S(2)}) %collective-permute-start.8) | collective-permute-done | bytes 16416 | tf_op jit(solution)/shard_map/ppermute | solution.py:617
  26.5 0.2 collective-permute-start.9
  26.7 10.5 %all_to_all.5.grams = f32[8,32,128]{2,1,0:T(8,128)S(1)} all-to-all(f32[8,32,128]{2,1,0:T(8,128)S(1)} %copies.1), channel_id=1, replica_groups=mesh['lon'=8,'probe'=4] {'lon'}, dimensions={0} | all-to-all | bytes 262144 | tf_op jit(solution)/shard_map/all_to_all | solution.py:709
  37.2 0.0 collective-permute-done.9.panel_other
  37.2 3.1 %factor.1 = (f32[6,16,512]{2,1,0:T(8,128)}, f32[64,64]{1,0:T(8,128)}) custom-call(s32[1]{0:T(128)} %bitcast.where, f32[8,32,128]{2,1,0:T(8,128)S(1)} %all_to_all.5.grams, f32[64,1536]{1,0:T(8,128)S(1)} %get-tuple-element.35.panel, f32[64,1536]{1,0:T(8,128)S(1)} %collective-permute-done.9.panel_other), custom_call_target="tpu_custom_call" | custom-call | flops 1000000 | bytes 100000 | tf_op jit(solution)/shard_map/factor/pallas_call | solution.py:710
  (4 shorter events, 0.0 us)
Async XLA Ops:
  1.9 6.2 %collective-permute-start = (f32[16,4,8,256]{3,2,1,0:T(8,128)S(1)}, f32[16,4,8,256]{3,2,1,0:T(8,128)S(1)}, u32[]{:S(2)}, u32[]{:S(2)}) collective-permute-start(f32[16,4,8,256]{3,2,1,0:T(8,128)S(1)} %get-tuple-element.22), channel_id=1, source_target_pairs={{0,1},{1,0},{2,3},{3,2},{4,5},{5,4},{6,7},{7,6},{8,9},{9,8},{10,11... | collective-permute-start | bytes 1572872 | tf_op jit(solution)/shard_map/ppermute | solution.py:617
  2.5 10.3 %collective-permute-start.3 = (f32[10,8,256]{2,1,0:T(8,128)S(1)}, f32[10,8,256]{2,1,0:T(8,128)S(1)}, u32[]{:S(2)}, u32[]{:S(2)}) collective-permute-start(f32[10,8,256]{2,1,0:T(8,128)S(1)} %get-tuple-element.25), channel_id=1, source_target_pairs={{0,4},{4,8},{8,12},{12,16},{16,20},{20,24},{24,28},{28,0},{1,5},{5... | collective-permute-start | bytes 245768 | tf_op jit(solution)/shard_map/ppermute | solution.py:646
  5.0 7.8 %collective-permute-start.4 = (f32[9,8,256]{2,1,0:T(8,128)S(1)}, f32[9,8,256]{2,1,0:T(8,128)S(1)}, u32[]{:S(2)}, u32[]{:S(2)}) collective-permute-start(f32[9,8,256]{2,1,0:T(8,128)S(1)} %get-tuple-element.26), channel_id=1, source_target_pairs={{0,28},{4,0},{8,4},{12,8},{16,12},{20,16},{24,20},{28,24},{1,29},{... | collective-permute-start | bytes 221192 | tf_op jit(solution)/shard_map/ppermute | solution.py:647
  12.6 1.3 %collective-permute-start.1 = (f32[16,1024]{1,0:T(8,128)S(1)}, f32[16,1024]{1,0:T(8,128)S(1)}, u32[]{:S(2)}, u32[]{:S(2)}) collective-permute-start(f32[16,1024]{1,0:T(8,128)S(1)} %get-tuple-element.24), channel_id=1, source_target_pairs={{0,1},{1,0},{2,3},{3,2},{4,5},{5,4},{6,7},{7,6},{8,9},{9,8},{10,11... | collective-permute-start | bytes 196616 | tf_op jit(solution)/shard_map/ppermute | solution.py:617
  13.6 7.0 %collective-permute-start.6 = (f32[32,512]{1,0:T(8,128)S(1)}, f32[32,512]{1,0:T(8,128)S(1)}, u32[]{:S(2)}, u32[]{:S(2)}) collective-permute-start(f32[32,512]{1,0:T(8,128)S(1)} %share.1.after), channel_id=1, source_target_pairs={{0,4},{1,29},{2,6},{3,31},{4,8},{5,1},{6,10},{7,3},{8,12},{9,5},{1... | collective-permute-start | bytes 196616 | tf_op jit(solution)/shard_map/ppermute | solution.py:676
  15.0 5.6 %collective-permute-start.5 = (f32[16,512]{1,0:T(8,128)S(1)}, f32[16,512]{1,0:T(8,128)S(1)}, u32[]{:S(2)}, u32[]{:S(2)}) collective-permute-start(f32[16,512]{1,0:T(8,128)S(1)} %get-tuple-element.31), channel_id=1, source_target_pairs={{0,1},{1,0},{2,3},{3,2},{4,5},{5,4},{6,7},{7,6},{8,9},{9,8},{10,11... | collective-permute-start | bytes 98312 | tf_op jit(solution)/shard_map/ppermute | solution.py:617
  16.9 6.2 %collective-permute-start.2 = (f32[32,1024]{1,0:T(8,128)S(1)}, f32[32,1024]{1,0:T(8,128)S(1)}, u32[]{:S(2)}, u32[]{:S(2)}) collective-permute-start(f32[32,1024]{1,0:T(8,128)S(1)} %constant_dynamic-update-slice_fusion.chip.after_inner.inner_chip), channel_id=1, source_target_pairs={{0,2},{1,3},{2,0},{3,1},{4,6},{5,7},{6,4},{7,5},{8,10},{9,11},{10,... | collective-permute-start | bytes 393224 | tf_op jit(solution)/shard_map/ppermute | solution.py:617
  20.6 4.3 %collective-permute-start.7 = (f32[32,512]{1,0:T(8,128)S(1)}, f32[32,512]{1,0:T(8,128)S(1)}, u32[]{:S(2)}, u32[]{:S(2)}) collective-permute-start(f32[32,512]{1,0:T(8,128)S(1)} %maximum_add_fusion.edge_chip), channel_id=1, source_target_pairs={{0,2},{1,3},{2,0},{3,1},{4,6},{5,7},{6,4},{7,5},{8,10},{9,11},{10,... | collective-permute-start | bytes 196616 | tf_op jit(solution)/shard_map/ppermute | solution.py:617
  25.3 1.2 %collective-permute-start.8 = (f32[32,128]{1,0:T(8,128)S(1)}, f32[32,128]{1,0:T(8,128)S(1)}, u32[]{:S(2)}, u32[]{:S(2)}) collective-permute-start(f32[32,128]{1,0:T(8,128)S(1)} %get-tuple-element.32.mine), channel_id=1, source_target_pairs={{0,1},{1,0},{2,3},{3,2},{4,5},{5,4},{6,7},{7,6},{8,9},{9,8},{10,11... | collective-permute-start | bytes 49160 | tf_op jit(solution)/shard_map/ppermute | solution.py:617
  26.5 10.6 %collective-permute-start.9 = (f32[64,1536]{1,0:T(8,128)S(1)}, f32[64,1536]{1,0:T(8,128)S(1)}, u32[]{:S(2)}, u32[]{:S(2)}) collective-permute-start(f32[64,1536]{1,0:T(8,128)S(1)} %get-tuple-element.35.panel), channel_id=1, source_target_pairs={{0,1},{1,0},{2,3},{3,2},{4,5},{5,4},{6,7},{7,6},{8,9},{9,8},{10,11... | collective-permute-start | bytes 1179656 | tf_op jit(solution)/shard_map/ppermute | solution.py:617

commit v9 on v8

--- a/solution.py
+++ b/solution.py
@@ -508,7 +508,12 @@
     assemble(where, edge_chip, edge_far, panel.at[:, width:])
     gram = self_product(panel[:, width:]) + inner_gram[...]
     half = gram.shape[0] // 2
-    out[...] = jnp.concatenate([gram[:half], gram[half:]], axis=1)
+    quarters = (gram[:half, :half], gram[half:, :half], gram[half:, half:])
+    rows = out.shape[0] // 3
+    for n, quarter in enumerate(quarters):
+        out[n * rows : (n + 1) * rows] = jnp.concatenate(
+            [quarter[k : k + rows] for k in range(0, half, rows)], axis=1
+        )
     assemble(where, inner_chip, inner_far, panel.at[:, :width])
 
 
@@ -524,8 +529,22 @@
     packed = grams[0]
     for n in range(1, grams.shape[0]):
         packed = packed + grams[n]
-    size = 2 * packed.shape[0]
-    gram = jnp.concatenate([packed[:, :size], packed[:, size:]], axis=0)
+    rows = packed.shape[0] // 3
+    half = upper.shape[0] // 2
+    size = 2 * half
+    first, cross, second = (
+        jnp.concatenate(
+            [packed[n * rows : (n + 1) * rows, k : k + half] for k in range(0, HALF, half)], axis=0
+        )
+        for n in range(3)
+    )
+    gram = jnp.concatenate(
+        [
+            jnp.concatenate([first, cross.T], axis=1),
+            jnp.concatenate([cross, second], axis=1),
+        ],
+        axis=0,
+    )
     row = lax.broadcasted_iota(jnp.int32, (size, size), 0)
     column = lax.broadcasted_iota(jnp.int32, (size, size), 1)
     state = jnp.concatenate([gram, jnp.where(row == column, 1.0, 0.0).astype(F32)], axis=1)
@@ -696,14 +715,15 @@
     )(where, inner_chip, inner_far)
     edge_chip = jnp.concatenate([rest, swap_probes(rest_other, 1)], axis=0) + arrived
     edge_far = swap_probes(edge_chip, 2)
+    packing = (3 * (probes // 2) ** 2 // HALF, HALF)
     panel, gram = call(
         gram_kernel,
         "gram",
-        (shape(probes, blocks * 256), shape(probes // 2, 2 * probes)),
+        (shape(probes, blocks * 256), shape(*packing)),
         [SMEM] + [VMEM] * 5,
     )(where, inner_gram, inner_chip, inner_far, edge_chip, edge_far)
     panel, gram_other = lax.optimization_barrier((panel, swap_probes(gram, 1)))
-    grams = call(copies_kernel, "copies", shape(ring, probes // 2, 2 * probes), [VMEM] * 2)(
+    grams = call(copies_kernel, "copies", shape(ring, *packing), [VMEM] * 2)(
         gram, gram_other
     )
     grams = lax.all_to_all(grams, "lon", 0, 0, tiled=True)

time: 40.5 us -> 40.3 us (level)
  no operation moved by 1% of the time
where the time goes in v9:
time: 40.3 us; the launch traced here: 40.1 us
  Pallas kernels  11.7 us (29%)
  starting transfers between devices  11.7 us (29%)
  blocking collectives  10.1 us (25%)
  waiting for transfers between devices  5.95 us (15%)
  between operations  0.71 us (2%)
    all_to_all x1, blocking collectives, body(): grams = lax.all_to_all(grams, 'lon', 0, 0, tiled=True)  10.1 us
    ppermute x7, starting transfers between devices, swap_probes(): lax.ppermute(value, 'probe', [(i, i ^ step) for i in range(lax.axis_size(...  5.93 us
    pallas_call x1, Pallas kernels, body(): call(interior_kernel, 'interior', (shape(count, (blocks - 2) * 256), shap...  4.48 us
    ppermute x7, waiting for transfers between devices, swap_probes(): lax.ppermute(value, 'probe', [(i, i ^ step) for i in range(lax.axis_size(...  3.73 us
    pallas_call x1, Pallas kernels, body(): call(factor_kernel, 'factor', (shape(blocks, count, 512), shape(probes, p...  3.32 us
    ppermute x1, starting transfers between devices, body(): from_high = lax.ppermute(pack_down, 'lon', down)  3.12 us
    ppermute x1, starting transfers between devices, body(): from_low = lax.ppermute(pack_up, 'lon', up)  2.55 us
    ppermute x1, waiting for transfers between devices, body(): lax.ppermute(share, ('lon', 'probe'), [(i * size + p, (up, down)[p & 1][i...  2.22 us
  transfers between devices with their start and end apart: 10, of which 5 were waited for; matrix products, arithmetic and copies ran while one was open for 0% of the time, Pallas kernels for 17%

profile of v9, /device:TPU:0, one launch (start us, length us, event | category | flops | bytes accessed | tf_op | source)
XLA Modules:
  0.0 40.1 jit_solution(11079616989603283635)
XLA Ops:
  0.6 1.3 %pack.1 = (f32[10,8,256]{2,1,0:T(8,128)S(1)}, f32[9,8,256]{2,1,0:T(8,128)S(1)}, f32[2,24,8,256]{3,2,1,0:T(8,128)S(1)}, f32[24,8,256]{2,1,0:T(8,128)S(1)}, f32[16,4,8,256]{3,2,1,0:T(8,128)S(1)}) custom-call(s32[1]{0:T(128)} %bitcast.where, f32[2,24,8,256]{3,2,1,0:T(8,128)} %winds_hbm.1, f32[24,8,256]{2,1,0:T(8,128)} %obs_hbm.1, f32[16,24,8,256]{3,2,1,0:T(8,128)} %field_hbm.3), custom_call_target="tpu_custom_call" | custom-call | flops 1000000 | bytes 100000 | tf_op jit(solution)/shard_map/pack/pallas_call | solution.py:651
  1.9 0.5 %collective-permute-start = (f32[16,4,8,256]{3,2,1,0:T(8,128)S(1)}, f32[16,4,8,256]{3,2,1,0:T(8,128)S(1)}, u32[]{:S(2)}, u32[]{:S(2)}) collective-permute-start(f32[16,4,8,256]{3,2,1,0:T(8,128)S(1)} %get-tuple-element.22), channel_id=1, source_target_pairs={{0,1},{1,0},{2,3},{3,2},{4,5},{5,4},{6,7},{7,6},{8,9},{9,8},{10,11... | collective-permute-start | bytes 1572872 | tf_op jit(solution)/shard_map/ppermute | solution.py:636
  2.5 2.6 %collective-permute-start.3 = (f32[10,8,256]{2,1,0:T(8,128)S(1)}, f32[10,8,256]{2,1,0:T(8,128)S(1)}, u32[]{:S(2)}, u32[]{:S(2)}) collective-permute-start(f32[10,8,256]{2,1,0:T(8,128)S(1)} %get-tuple-element.25), channel_id=1, source_target_pairs={{0,4},{4,8},{8,12},{12,16},{16,20},{20,24},{24,28},{28,0},{1,5},{5... | collective-permute-start | bytes 245768 | tf_op jit(solution)/shard_map/ppermute | solution.py:665
  5.0 3.1 %collective-permute-start.4 = (f32[9,8,256]{2,1,0:T(8,128)S(1)}, f32[9,8,256]{2,1,0:T(8,128)S(1)}, u32[]{:S(2)}, u32[]{:S(2)}) collective-permute-start(f32[9,8,256]{2,1,0:T(8,128)S(1)} %get-tuple-element.26), channel_id=1, source_target_pairs={{0,28},{4,0},{8,4},{12,8},{16,12},{20,16},{24,20},{28,24},{1,29},{... | collective-permute-start | bytes 221192 | tf_op jit(solution)/shard_map/ppermute | solution.py:666
  8.1 0.0 collective-permute-done.after.borrowed
  8.1 4.5 %interior.1 = (f32[16,1024]{1,0:T(8,128)S(1)}, f32[16,1024]{1,0:T(8,128)S(1)}, f32[16,512]{1,0:T(8,128)S(1)}, f32[16,512]{1,0:T(8,128)S(1)}, f32[16,8,8,256]{3,2,1,0:T(8,128)S(1)}) custom-call(s32[1]{0:T(128)} %bitcast.where, f32[2,24,8,256]{3,2,1,0:T(8,128)S(1)} %get-tuple-element.20.winds, f32[24,8,256]{2,1,0:T(8,128)S(1)} %get-tuple-element.21.obs, ...), custom_call_target="tpu_custom_call" | custom-call | flops 1000000 | bytes 100000 | tf_op jit(solution)/shard_map/interior/pallas_call | solution.py:667
  12.6 0.1 collective-permute-start.1
  12.8 0.0 collective-permute-done.4.from_high
  12.8 0.0 collective-permute-done.3.from_low
  12.8 0.8 %share.1.after = f32[32,512]{1,0:T(8,128)S(1)} custom-call(s32[1]{0:T(128)} %bitcast.where, f32[2,24,8,256]{3,2,1,0:T(8,128)S(1)} %get-tuple-element.20.winds, f32[24,8,256]{2,1,0:T(8,128)S(1)} %get-tuple-element.21.obs, f32[10,8,256]{2,1,0:T(8,128)S(1)} %collective-permute-done.3.from_low, f32[9,8,256]{2,1,0:T(8,128)S(1)} %collective-permute-done.4.from_high, ...), custom_call_target="tpu_custom_call" | custom-call | flops 1000000 | bytes 100000 | tf_op jit(solution)/shard_map/share/pallas_call | solution.py:691
  13.6 0.1 collective-permute-start.6
  13.7 0.3 collective-permute-done.1
  13.9 1.0 %rest.1 = (f32[16,512]{1,0:T(8,128)S(1)}, f32[16,512]{1,0:T(8,128)S(1)}) custom-call(s32[1]{0:T(128)} %bitcast.where, f32[2,24,8,256]{3,2,1,0:T(8,128)S(1)} %get-tuple-element.20.winds, f32[24,8,256]{2,1,0:T(8,128)S(1)} %get-tuple-element.21.obs, f32[10,8,256]{2,1,0:T(8,128)S(1)} %collective-permute-done.3.from_low, ...), custom_call_target="tpu_custom_call" | custom-call | flops 1000000 | bytes 100000 | tf_op jit(solution)/shard_map/rest/pallas_call | solution.py:705
  15.0 1.9 %collective-permute-start.5 = (f32[16,512]{1,0:T(8,128)S(1)}, f32[16,512]{1,0:T(8,128)S(1)}, u32[]{:S(2)}, u32[]{:S(2)}) collective-permute-start(f32[16,512]{1,0:T(8,128)S(1)} %get-tuple-element.31), channel_id=1, source_target_pairs={{0,1},{1,0},{2,3},{3,2},{4,5},{5,4},{6,7},{7,6},{8,9},{9,8},{10,11... | collective-permute-start | bytes 98312 | tf_op jit(solution)/shard_map/ppermute | solution.py:636
  16.9 1.5 %collective-permute-start.2 = (f32[32,1024]{1,0:T(8,128)S(1)}, f32[32,1024]{1,0:T(8,128)S(1)}, u32[]{:S(2)}, u32[]{:S(2)}) collective-permute-start(f32[32,1024]{1,0:T(8,128)S(1)} %constant_dynamic-update-slice_fusion.chip.after_inner.inner_chip), channel_id=1, source_target_pairs={{0,2},{1,3},{2,0},{3,1},{4,6},{5,7},{6,4},{7,5},{8,10},{9,11},{10,... | collective-permute-start | bytes 393224 | tf_op jit(solution)/shard_map/ppermute | solution.py:636
  18.4 2.2 %collective-permute-done.6 = f32[32,512]{1,0:T(8,128)S(1)} collective-permute-done((f32[32,512]{1,0:T(8,128)S(1)}, f32[32,512]{1,0:T(8,128)S(1)}, u32[]{:S(2)}, u32[]{:S(2)}) %collective-permute-start.6) | collective-permute-done | bytes 65568 | tf_op jit(solution)/shard_map/ppermute | solution.py:695
  20.6 0.0 collective-permute-done.5
  20.6 1.6 %collective-permute-start.7 = (f32[32,512]{1,0:T(8,128)S(1)}, f32[32,512]{1,0:T(8,128)S(1)}, u32[]{:S(2)}, u32[]{:S(2)}) collective-permute-start(f32[32,512]{1,0:T(8,128)S(1)} %maximum_add_fusion.edge_chip), channel_id=1, source_target_pairs={{0,2},{1,3},{2,0},{3,1},{4,6},{5,7},{6,4},{7,5},{8,10},{9,11},{10,... | collective-permute-start | bytes 196616 | tf_op jit(solution)/shard_map/ppermute | solution.py:636
  22.3 0.8 %collective-permute-done.2.far.inner_far = f32[32,1024]{1,0:T(8,128)S(1)} collective-permute-done((f32[32,1024]{1,0:T(8,128)S(1)}, f32[32,1024]{1,0:T(8,128)S(1)}, u32[]{:S(2)}, u32[]{:S(2)}) %collective-permute-start.2) | collective-permute-done | bytes 131104 | tf_op jit(solution)/shard_map/ppermute | solution.py:636
  23.1 0.4 inner_gram.1
  23.5 1.5 %collective-permute-done.7.edge_far = f32[32,512]{1,0:T(8,128)S(1)} collective-permute-done((f32[32,512]{1,0:T(8,128)S(1)}, f32[32,512]{1,0:T(8,128)S(1)}, u32[]{:S(2)}, u32[]{:S(2)}) %collective-permute-start.7) | collective-permute-done | bytes 65568 | tf_op jit(solution)/shard_map/ppermute | solution.py:636
  25.0 0.4 gram.1
  25.3 0.0 collective-permute-start.8
  25.4 1.2 %collective-permute-done.8.other = f32[24,128]{1,0:T(8,128)S(1)} collective-permute-done((f32[24,128]{1,0:T(8,128)S(1)}, f32[24,128]{1,0:T(8,128)S(1)}, u32[]{:S(2)}, u32[]{:S(2)}) %collective-permute-start.8) | collective-permute-done | bytes 12320 | tf_op jit(solution)/shard_map/ppermute | solution.py:636
  26.5 0.2 collective-permute-start.9
  26.7 10.1 %all_to_all.5.grams = f32[8,24,128]{2,1,0:T(8,128)S(1)} all-to-all(f32[8,24,128]{2,1,0:T(8,128)S(1)} %copies.1), channel_id=1, replica_groups=mesh['lon'=8,'probe'=4] {'lon'}, dimensions={0} | all-to-all | bytes 196608 | tf_op jit(solution)/shard_map/all_to_all | solution.py:729
  36.8 0.0 collective-permute-done.9.panel_other
  36.8 3.3 %factor.1 = (f32[6,16,512]{2,1,0:T(8,128)}, f32[64,64]{1,0:T(8,128)}) custom-call(s32[1]{0:T(128)} %bitcast.where, f32[8,24,128]{2,1,0:T(8,128)S(1)} %all_to_all.5.grams, f32[64,1536]{1,0:T(8,128)S(1)} %get-tuple-element.35.panel, f32[64,1536]{1,0:T(8,128)S(1)} %collective-permute-done.9.panel_other), custom_call_target="tpu_custom_call" | custom-call | flops 1000000 | bytes 100000 | tf_op jit(solution)/shard_map/factor/pallas_call | solution.py:730
  (4 shorter events, 0.0 us)
Async XLA Ops:
  1.9 6.2 %collective-permute-start = (f32[16,4,8,256]{3,2,1,0:T(8,128)S(1)}, f32[16,4,8,256]{3,2,1,0:T(8,128)S(1)}, u32[]{:S(2)}, u32[]{:S(2)}) collective-permute-start(f32[16,4,8,256]{3,2,1,0:T(8,128)S(1)} %get-tuple-element.22), channel_id=1, source_target_pairs={{0,1},{1,0},{2,3},{3,2},{4,5},{5,4},{6,7},{7,6},{8,9},{9,8},{10,11... | collective-permute-start | bytes 1572872 | tf_op jit(solution)/shard_map/ppermute | solution.py:636
  2.5 10.3 %collective-permute-start.3 = (f32[10,8,256]{2,1,0:T(8,128)S(1)}, f32[10,8,256]{2,1,0:T(8,128)S(1)}, u32[]{:S(2)}, u32[]{:S(2)}) collective-permute-start(f32[10,8,256]{2,1,0:T(8,128)S(1)} %get-tuple-element.25), channel_id=1, source_target_pairs={{0,4},{4,8},{8,12},{12,16},{16,20},{20,24},{24,28},{28,0},{1,5},{5... | collective-permute-start | bytes 245768 | tf_op jit(solution)/shard_map/ppermute | solution.py:665
  5.0 7.8 %collective-permute-start.4 = (f32[9,8,256]{2,1,0:T(8,128)S(1)}, f32[9,8,256]{2,1,0:T(8,128)S(1)}, u32[]{:S(2)}, u32[]{:S(2)}) collective-permute-start(f32[9,8,256]{2,1,0:T(8,128)S(1)} %get-tuple-element.26), channel_id=1, source_target_pairs={{0,28},{4,0},{8,4},{12,8},{16,12},{20,16},{24,20},{28,24},{1,29},{... | collective-permute-start | bytes 221192 | tf_op jit(solution)/shard_map/ppermute | solution.py:666
  12.6 1.3 %collective-permute-start.1 = (f32[16,1024]{1,0:T(8,128)S(1)}, f32[16,1024]{1,0:T(8,128)S(1)}, u32[]{:S(2)}, u32[]{:S(2)}) collective-permute-start(f32[16,1024]{1,0:T(8,128)S(1)} %get-tuple-element.24), channel_id=1, source_target_pairs={{0,1},{1,0},{2,3},{3,2},{4,5},{5,4},{6,7},{7,6},{8,9},{9,8},{10,11... | collective-permute-start | bytes 196616 | tf_op jit(solution)/shard_map/ppermute | solution.py:636
  13.6 7.0 %collective-permute-start.6 = (f32[32,512]{1,0:T(8,128)S(1)}, f32[32,512]{1,0:T(8,128)S(1)}, u32[]{:S(2)}, u32[]{:S(2)}) collective-permute-start(f32[32,512]{1,0:T(8,128)S(1)} %share.1.after), channel_id=1, source_target_pairs={{0,4},{1,29},{2,6},{3,31},{4,8},{5,1},{6,10},{7,3},{8,12},{9,5},{1... | collective-permute-start | bytes 196616 | tf_op jit(solution)/shard_map/ppermute | solution.py:695
  15.0 5.6 %collective-permute-start.5 = (f32[16,512]{1,0:T(8,128)S(1)}, f32[16,512]{1,0:T(8,128)S(1)}, u32[]{:S(2)}, u32[]{:S(2)}) collective-permute-start(f32[16,512]{1,0:T(8,128)S(1)} %get-tuple-element.31), channel_id=1, source_target_pairs={{0,1},{1,0},{2,3},{3,2},{4,5},{5,4},{6,7},{7,6},{8,9},{9,8},{10,11... | collective-permute-start | bytes 98312 | tf_op jit(solution)/shard_map/ppermute | solution.py:636
  16.9 6.2 %collective-permute-start.2 = (f32[32,1024]{1,0:T(8,128)S(1)}, f32[32,1024]{1,0:T(8,128)S(1)}, u32[]{:S(2)}, u32[]{:S(2)}) collective-permute-start(f32[32,1024]{1,0:T(8,128)S(1)} %constant_dynamic-update-slice_fusion.chip.after_inner.inner_chip), channel_id=1, source_target_pairs={{0,2},{1,3},{2,0},{3,1},{4,6},{5,7},{6,4},{7,5},{8,10},{9,11},{10,... | collective-permute-start | bytes 393224 | tf_op jit(solution)/shard_map/ppermute | solution.py:636
  20.6 4.3 %collective-permute-start.7 = (f32[32,512]{1,0:T(8,128)S(1)}, f32[32,512]{1,0:T(8,128)S(1)}, u32[]{:S(2)}, u32[]{:S(2)}) collective-permute-start(f32[32,512]{1,0:T(8,128)S(1)} %maximum_add_fusion.edge_chip), channel_id=1, source_target_pairs={{0,2},{1,3},{2,0},{3,1},{4,6},{5,7},{6,4},{7,5},{8,10},{9,11},{10,... | collective-permute-start | bytes 196616 | tf_op jit(solution)/shard_map/ppermute | solution.py:636
  25.3 1.2 %collective-permute-start.8 = (f32[24,128]{1,0:T(8,128)S(1)}, f32[24,128]{1,0:T(8,128)S(1)}, u32[]{:S(2)}, u32[]{:S(2)}) collective-permute-start(f32[24,128]{1,0:T(8,128)S(1)} %get-tuple-element.32.mine), channel_id=1, source_target_pairs={{0,1},{1,0},{2,3},{3,2},{4,5},{5,4},{6,7},{7,6},{8,9},{9,8},{10,11... | collective-permute-start | bytes 36872 | tf_op jit(solution)/shard_map/ppermute | solution.py:636
  26.5 10.3 %collective-permute-start.9 = (f32[64,1536]{1,0:T(8,128)S(1)}, f32[64,1536]{1,0:T(8,128)S(1)}, u32[]{:S(2)}, u32[]{:S(2)}) collective-permute-start(f32[64,1536]{1,0:T(8,128)S(1)} %get-tuple-element.35.panel), channel_id=1, source_target_pairs={{0,1},{1,0},{2,3},{3,2},{4,5},{5,4},{6,7},{7,6},{8,9},{9,8},{10,11... | collective-permute-start | bytes 1179656 | tf_op jit(solution)/shard_map/ppermute | solution.py:636
